TPU v7x, 128 devices: a whole 4x4x4 slice. The times are simulated.
128 devices in a mesh: comp: 2 (over y_hi), gx: 16 (over z, x), gy: 4 (over y_lo, core).
Axes of the slice: x: 4, y: 4 (y_hi: 2, y_lo: 2; y = y_hi * 2 + y_lo), z: 4, core: 2. Of those that a mesh axis runs over, the one named last changes fastest.
Arguments:
- state: float32 [2, 16, 512, 2048], P('comp', None, 'gx', 'gy'), may hold values from -5 to 8
- guess: bfloat16 [2, 6, 512, 2048], P('comp', None, 'gx', 'gy'), may hold values from -5 to 5
- diffusion: float32 [2, 16], P('comp'), may hold values from 0.05 to 0.22
- mixing: float32 [2, 15], P('comp'), may hold values from 0.15 to 0.24
- coupling: float32 [2, 512, 2048], P('comp', 'gx', 'gy'), may hold values from 0.3 to 0.6
- land_temp: float32 [512, 2048], P('gx', 'gy'), may hold values from -6 to 6
- land_mask: int32 [512, 2048], P('gx', 'gy'), may hold values from 0 to 1
- weights: bfloat16 [2, 2048, 128, 128], P('comp', ('gx', 'gy')), may hold values from -0.375 to 0.375
- source_block: int32 [2, 512, 16, 2], P('comp', 'gx', 'gy'), may hold values from 0 to 127
- pattern: int32 [2, 512, 16, 2], P('comp', 'gx', 'gy'), may hold values from 0 to 31
Outputs:
- final_state: float32 [2, 16, 512, 2048], P('comp', None, 'gx', 'gy')
- forcing: float32 [2, 6, 512, 2048], P('comp', None, 'gx', 'gy')
Inputs may be any that keep to these rules, and one draw needn't show every extreme that they name: `source_block`: a block number of the same tile. `pattern`: a weight block of the same tile.
All inputs are finite; a program needn't handle non-finite values.
Results may differ from a plain program's by a relative error of at most 0.0023.
The roundings to bfloat16 on the way count: a program that leaves them out, or rounds other values in their place, can miss the bound.
Values may be sent and summed in bfloat16 or wider, within the bound.
No kernel may reach another device: no remote copies, remote signals or barrier semaphores. Data moves between devices by JAX's collectives and lax.ppermute only.
A program may use at most 128 MiB of HBM per device.

v0:
```python
import math

import jax
import jax.numpy as jnp
from jax import lax
from jax.sharding import PartitionSpec as P

ITERS = 2


def with_halo(cells, sides, width, closed):
    for axis, dim in sides:
        count = lax.axis_size(axis)
        ends = count if closed else count - 1
        head = lax.slice_in_dim(cells, 0, width, axis=dim)
        tail = lax.slice_in_dim(cells, cells.shape[dim] - width, cells.shape[dim], axis=dim)
        cells = jnp.concatenate(
            [
                lax.ppermute(tail, axis, [(i, (i + 1) % count) for i in range(ends)]),
                cells,
                lax.ppermute(head, axis, [((i + 1) % count, i) for i in range(ends)]),
            ],
            axis=dim,
        )
    return cells


def swapped(value, axis, stride):
    mask = 2**stride
    pairs = [(source, source ^ mask) for source in range(lax.axis_size(axis))]
    return lax.ppermute(value, axis, pairs)


def vertical_mix(spread, mixing_row):
    upward = mixing_row[:, None, None] * (spread[1:] - spread[:-1])
    zero_layer = jnp.zeros_like(spread[:1])
    return (
        spread + jnp.concatenate([upward, zero_layer], 0) - jnp.concatenate([zero_layer, upward], 0)
    )


def advance(
    extended, diffusion_row, mixing_row, exchange_rate, maskf, land_temp, forcing_now, is_ocean
):
    center = extended[:, 1:-1, 1:-1]
    laplace = extended[:, 2:, 1:-1] + extended[:, :-2, 1:-1]
    laplace = laplace + extended[:, 1:-1, 2:] + extended[:, 1:-1, :-2] - 4.0 * center
    spread = center + diffusion_row[:, None, None] * laplace
    mixed = vertical_mix(spread, mixing_row)
    surface = mixed[0]
    below = maskf * forcing_now + (1.0 - maskf) * land_temp
    flux_value = exchange_rate * (surface - below)
    warmed = surface + exchange_rate * maskf * forcing_now
    top_level = jnp.where(is_ocean, warmed, surface - flux_value)
    emitted = jnp.where(is_ocean, maskf * warmed, flux_value)
    return (jnp.concatenate([top_level[None], mixed[1:]], 0), emitted)


def regrid(series_block, chosen, source_idx):
    step_count, row_count, col_count = series_block.shape
    block_count = row_count * col_count // 128
    blocks = series_block.reshape(step_count, block_count, 128)
    group_size = math.gcd(block_count, 64)
    group_count = block_count // group_size
    source_groups = source_idx.reshape(group_count, group_size, -1)
    chosen_groups = chosen.reshape(group_count, group_size, chosen.shape[1], 128, 128)

    def per_group(members):
        source_row, chosen_row = members
        picked = jnp.take(blocks, source_row, axis=1)
        return jnp.einsum("sbki,bkij->sbj", picked, chosen_row, preferred_element_type=jnp.float32)

    result = lax.map(per_group, (source_groups, chosen_groups))
    return result.transpose(1, 0, 2, 3).reshape(step_count, row_count, col_count)


def per_device(
    state, guess, diffusion, mixing, coupling, land_temp, land_mask, weights, source_block, pattern
):
    is_ocean = lax.axis_index("comp") == 1
    start = state[0]
    diffusion_row = diffusion[0]
    mixing_row = mixing[0]
    exchange_rate = coupling[0]
    maskf = land_mask.astype(jnp.float32)
    table = weights[0]
    sources_dev = source_block.shape[3]
    source_idx = source_block[0].reshape(-1, sources_dev)
    pattern_idx = pattern[0].reshape(-1, sources_dev)
    chosen = jnp.take(table, pattern_idx, axis=0)
    step_count = guess.shape[1]
    wet = lax.psum(jnp.sum(maskf), ("gx", "gy"))
    forcing = guess[0].astype(jnp.float32)
    current = start
    for iteration in range(ITERS):
        received_list = []

        def emit(values):
            received_list.append(values)

        current = start
        for instant in range(step_count):
            extended = with_halo(current, (("gx", 1),), 1, True)
            extended = with_halo(extended, (("gy", 2),), 1, False)
            current, emitted = advance(
                extended,
                diffusion_row,
                mixing_row,
                exchange_rate,
                maskf,
                land_temp,
                forcing[instant],
                is_ocean,
            )
            emit(emitted.astype(jnp.bfloat16))
        received = swapped(jnp.stack(received_list), "comp", 0)
        regridded = regrid(received, chosen, source_idx)
        local_gap = jnp.sum(maskf * received.astype(jnp.float32), axis=(1, 2)) - jnp.sum(
            maskf * regridded, axis=(1, 2)
        )
        total_gap = lax.psum(local_gap, ("gx", "gy"))
        forcing = regridded + maskf * (total_gap / wet)[:, None, None]
    return (current[None], forcing[None])


def solution(mesh):
    placed = (
        P("comp", None, "gx", "gy"),
        P("comp", None, "gx", "gy"),
        P("comp", None),
        P("comp", None),
        P("comp", "gx", "gy"),
        P("gx", "gy"),
        P("gx", "gy"),
        P("comp", ("gx", "gy"), None, None),
        P("comp", "gx", "gy", None),
        P("comp", "gx", "gy", None),
    )
    return jax.shard_map(
        per_device,
        mesh=mesh,
        in_specs=placed,
        out_specs=(P("comp", None, "gx", "gy"), P("comp", None, "gx", "gy")),
        check_vma=False,
    )
```

profile of v0, /device:TPU:1, one launch (start us, length us, event | category | flops | bytes accessed | tf_op | source)
XLA Modules:
  0.0 569.8 jit_solution(2986322879747508042)
XLA Ops:
  1.9 6.8 %collective-permute-start = (f32[16,1,512]{2,1,0:T(1,128)S(1)}, f32[16,1,512]{2,1,0:T(1,128)S(1)}, u32[]{:S(2)}, u32[]{:S(2)}) collective-permute-start(f32[16,1,512]{2,1,0:T(1,128)S(1)} %get-tuple-element.161), channel_id=1, source_target_pairs={{4,0},{8,4},{12,8},{16,12},{20,16},{24,20},{28,24},{32,28},{36,32}... | collective-permute-start | bytes 98312 | tf_op jit(solution)/shard_map/ppermute | solution.py:21
  9.8 5.1 collective-permute-done.1
  16.7 4.0 collective-permute-start.2
  40.7 5.5 collective-permute-start.7
  63.9 5.4 collective-permute-start.11
  82.1 8.7 %gather_fusion.2 = bf16[256,128,128]{2,1,0:T(8,128)(2,1)} fusion(bf16[32,128,128]{2,1,0:T(8,128)(2,1)S(1)} %bitcast.465, s32[1024]{0:T(1024)S(1)} %pad_clamp_fusion.2), kind=kCustom, calls=%fused_computation.2 | custom fusion | bytes 16778240 | tf_op jit(solution)/shard_map/jit(_take)/gather | solution.py:90
  92.9 5.0 collective-permute-start.15
  110.3 4.6 collective-permute-done.17
  117.0 5.8 %collective-permute-start.19 = (f32[16,34,1]{2,1,0:T(8,128)S(1)}, f32[16,34,1]{2,1,0:T(8,128)S(1)}, u32[]{:S(2)}, u32[]{:S(2)}) collective-permute-start(f32[16,34,1]{2,1,0:T(8,128)S(1)} %get-tuple-element.133), channel_id=1, source_target_pairs={{0,1},{1,2},{2,3},{4,5},{5,6},{6,7},{8,9},{9,10},{10,11},{12,13},{... | collective-permute-start | bytes 6536 | tf_op jit(solution)/shard_map/ppermute | solution.py:19
  132.5 3.4 collective-permute-done.21
  138.1 5.5 collective-permute-start.23
  149.4 4.9 collective-permute-start.24
  154.3 7.6 %broadcast_select_fusion = bf16[2,64,2,128,128]{4,3,2,1,0:T(8,128)(2,1)} fusion(bf16[2,64,2,128,128]{4,3,2,1,0:T(8,128)(2,1)} %bitcast.466, pred[2,64,2]{2,1,0:T(8,128)(4,1)S(1)} %copy.25), kind=kLoop, calls=%fused_computation.31 | loop fusion | flops 4194304 | bytes 16777472 | tf_op jit(solution)/shard_map/jit(_take)/select_n | solution.py:90
  162.4 8.0 %while.20 = (s32[]{:T(128)}, f32[2,6,64,128]{3,1,2,0:T(8,128)S(1)}, bf16[2,64,2,128,128]{4,3,2,1,0:T(8,128)(2,1)}, s32[2,64,2]{1,2,0:T(2,128)S(1)}, bf16[6,128,128]{2,0,1:T(8,128)(2,1)S(1)}, /*index=5*/s32[]{:T(128)}) while((s32[]{:T(128)}, f32[2,6,64,128]{3,1,2,0:T(8,128)S(1)}, bf16[2,64,2,128,128]{4,3,2,1,0:T(8,128)(2,1)}, ...), condition=%wide.region_1.3_spmd, body=%wide.region_0.0_spmd.sunk | while | flops 25265920 | bytes 5129673 | solution.py:73
  170.9 134.5 %all-reduce.22 = (f32[6]{0:T(128)S(1)}, f32[]{:T(128)}) all-reduce(f32[6]{0:T(128)S(1)} %sub.221, f32[]{:T(128)} %get-tuple-element.162), channel_id=1, replica_groups=mesh['comp'=2,'gx'=16,'gy'=4] {'gx','gy'}, use_global_device_ids=true, to_apply=%region_4.6 | all-reduce | flops 7 | bytes 56 | tf_op jit(solution)/shard_map/psum | solution.py:121
  314.6 8.0 %collective-permute-start.27 = (f32[16,34,1]{2,1,0:T(8,128)S(1)}, f32[16,34,1]{2,1,0:T(8,128)S(1)}, u32[]{:S(2)}, u32[]{:S(2)}) collective-permute-start(f32[16,34,1]{2,1,0:T(8,128)S(1)} %get-tuple-element.118), channel_id=1, source_target_pairs={{1,0},{2,1},{3,2},{5,4},{6,5},{7,6},{9,8},{10,9},{11,10},{13,12},{... | collective-permute-start | bytes 6536 | tf_op jit(solution)/shard_map/ppermute | solution.py:21
  324.6 4.0 collective-permute-done.28
  339.9 5.5 collective-permute-start.32
  360.7 5.8 %collective-permute-start.36 = (f32[16,34,1]{2,1,0:T(8,128)S(1)}, f32[16,34,1]{2,1,0:T(8,128)S(1)}, u32[]{:S(2)}, u32[]{:S(2)}) collective-permute-start(f32[16,34,1]{2,1,0:T(8,128)S(1)} %get-tuple-element.127), channel_id=1, source_target_pairs={{0,1},{1,2},{2,3},{4,5},{5,6},{6,7},{8,9},{9,10},{10,11},{12,13},{... | collective-permute-start | bytes 6536 | tf_op jit(solution)/shard_map/ppermute | solution.py:19
  381.5 5.5 collective-permute-start.40
  402.4 5.5 collective-permute-start.44
  417.6 5.2 collective-permute-done.45
  423.1 8.0 %while.21 = (s32[]{:T(128)}, f32[2,6,64,128]{3,1,2,0:T(8,128)S(1)}, bf16[2,64,2,128,128]{4,3,2,1,0:T(8,128)(2,1)}, s32[2,64,2]{1,2,0:T(2,128)S(1)}, bf16[6,128,128]{2,0,1:T(8,128)(2,1)S(1)}, /*index=5*/s32[]{:T(128)}) while((s32[]{:T(128)}, f32[2,6,64,128]{3,1,2,0:T(8,128)S(1)}, bf16[2,64,2,128,128]{4,3,2,1,0:T(8,128)(2,1)}, ...), condition=%wide.region_8.10_spmd, body=%wide.region_7.9_spmd.sunk | while | flops 25265920 | bytes 5129673 | solution.py:73
  432.5 135.3 %psum.23 = f32[6]{0:T(128)S(1)} all-reduce(f32[6]{0:T(128)S(1)} %sub.249), channel_id=1, replica_groups=mesh['comp'=2,'gx'=16,'gy'=4] {'gx','gy'}, use_global_device_ids=true, to_apply=%region_11.13 | all-reduce | flops 6 | bytes 48 | tf_op jit(solution)/shard_map/psum | solution.py:121
  (262 shorter events, 186.0 us)
Async XLA Ops:
  1.9 7.9 %collective-permute-start = (f32[16,1,512]{2,1,0:T(1,128)S(1)}, f32[16,1,512]{2,1,0:T(1,128)S(1)}, u32[]{:S(2)}, u32[]{:S(2)}) collective-permute-start(f32[16,1,512]{2,1,0:T(1,128)S(1)} %get-tuple-element.161), channel_id=1, source_target_pairs={{4,0},{8,4},{12,8},{16,12},{20,16},{24,20},{28,24},{32,28},{36,32}... | collective-permute-start | bytes 98312 | tf_op jit(solution)/shard_map/ppermute | solution.py:21
  16.7 10.1 %collective-permute-start.2 = (f32[16,34,1]{2,1,0:T(8,128)}, f32[16,34,1]{2,1,0:T(8,128)S(1)}, u32[]{:S(2)}, u32[]{:S(2)}) collective-permute-start(f32[16,34,1]{2,1,0:T(8,128)} %get-tuple-element.138), channel_id=1, source_target_pairs={{1,0},{2,1},{3,2},{5,4},{6,5},{7,6},{9,8},{10,9},{11,10},{13,12},{... | collective-permute-start | bytes 6536 | tf_op jit(solution)/shard_map/ppermute | solution.py:21
  38.7 10.5 %collective-permute-start.6 = (f32[16,34,1]{2,1,0:T(8,128)}, f32[16,34,1]{2,1,0:T(8,128)S(1)}, u32[]{:S(2)}, u32[]{:S(2)}) collective-permute-start(f32[16,34,1]{2,1,0:T(8,128)} %get-tuple-element.120), channel_id=1, source_target_pairs={{1,0},{2,1},{3,2},{5,4},{6,5},{7,6},{9,8},{10,9},{11,10},{13,12},{... | collective-permute-start | bytes 6536 | tf_op jit(solution)/shard_map/ppermute | solution.py:21
  40.7 9.9 %collective-permute-start.7 = (f32[16,34,1]{2,1,0:T(8,128)}, f32[16,34,1]{2,1,0:T(8,128)S(1)}, u32[]{:S(2)}, u32[]{:S(2)}) collective-permute-start(f32[16,34,1]{2,1,0:T(8,128)} %get-tuple-element.121), channel_id=1, source_target_pairs={{0,1},{1,2},{2,3},{4,5},{5,6},{6,7},{8,9},{9,10},{10,11},{12,13},{... | collective-permute-start | bytes 6536 | tf_op jit(solution)/shard_map/ppermute | solution.py:19
  62.0 10.5 %collective-permute-start.10 = (f32[16,34,1]{2,1,0:T(8,128)}, f32[16,34,1]{2,1,0:T(8,128)}, u32[]{:S(2)}, u32[]{:S(2)}) collective-permute-start(f32[16,34,1]{2,1,0:T(8,128)} %get-tuple-element.136), channel_id=1, source_target_pairs={{1,0},{2,1},{3,2},{5,4},{6,5},{7,6},{9,8},{10,9},{11,10},{13,12},{... | collective-permute-start | bytes 6536 | tf_op jit(solution)/shard_map/ppermute | solution.py:21
  63.9 9.8 %collective-permute-start.11 = (f32[16,34,1]{2,1,0:T(8,128)}, f32[16,34,1]{2,1,0:T(8,128)}, u32[]{:S(2)}, u32[]{:S(2)}) collective-permute-start(f32[16,34,1]{2,1,0:T(8,128)} %get-tuple-element.137), channel_id=1, source_target_pairs={{0,1},{1,2},{2,3},{4,5},{5,6},{6,7},{8,9},{9,10},{10,11},{12,13},{... | collective-permute-start | bytes 6536 | tf_op jit(solution)/shard_map/ppermute | solution.py:19
  80.1 10.7 %collective-permute-start.12 = (f32[16,1,512]{2,1,0:T(1,128)}, f32[16,1,512]{2,1,0:T(1,128)S(1)}, u32[]{:S(2)}, u32[]{:S(2)}) collective-permute-start(f32[16,1,512]{2,1,0:T(1,128)} %get-tuple-element.155), channel_id=1, source_target_pairs={{4,0},{8,4},{12,8},{16,12},{20,16},{24,20},{28,24},{32,28},{36,32}... | collective-permute-start | bytes 98312 | tf_op jit(solution)/shard_map/ppermute | solution.py:21
  80.1 10.7 %collective-permute-start.13 = (f32[16,1,512]{2,1,0:T(1,128)}, f32[16,1,512]{2,1,0:T(1,128)S(1)}, u32[]{:S(2)}, u32[]{:S(2)}) collective-permute-start(f32[16,1,512]{2,1,0:T(1,128)} %get-tuple-element.154), channel_id=1, source_target_pairs={{0,4},{4,8},{8,12},{12,16},{16,20},{20,24},{24,28},{28,32},{32,36}... | collective-permute-start | bytes 98312 | tf_op jit(solution)/shard_map/ppermute | solution.py:19
  91.0 9.7 %collective-permute-start.14 = (f32[16,34,1]{2,1,0:T(8,128)S(1)}, f32[16,34,1]{2,1,0:T(8,128)S(1)}, u32[]{:S(2)}, u32[]{:S(2)}) collective-permute-start(f32[16,34,1]{2,1,0:T(8,128)S(1)} %get-tuple-element.134), channel_id=1, source_target_pairs={{1,0},{2,1},{3,2},{5,4},{6,5},{7,6},{9,8},{10,9},{11,10},{13,12},{... | collective-permute-start | bytes 6536 | tf_op jit(solution)/shard_map/ppermute | solution.py:21
  92.9 9.0 %collective-permute-start.15 = (f32[16,34,1]{2,1,0:T(8,128)S(1)}, f32[16,34,1]{2,1,0:T(8,128)S(1)}, u32[]{:S(2)}, u32[]{:S(2)}) collective-permute-start(f32[16,34,1]{2,1,0:T(8,128)S(1)} %get-tuple-element.135), channel_id=1, source_target_pairs={{0,1},{1,2},{2,3},{4,5},{5,6},{6,7},{8,9},{9,10},{10,11},{12,13},{... | collective-permute-start | bytes 6536 | tf_op jit(solution)/shard_map/ppermute | solution.py:19
  115.1 10.6 %collective-permute-start.18 = (f32[16,34,1]{2,1,0:T(8,128)S(1)}, f32[16,34,1]{2,1,0:T(8,128)S(1)}, u32[]{:S(2)}, u32[]{:S(2)}) collective-permute-start(f32[16,34,1]{2,1,0:T(8,128)S(1)} %get-tuple-element.132), channel_id=1, source_target_pairs={{1,0},{2,1},{3,2},{5,4},{6,5},{7,6},{9,8},{10,9},{11,10},{13,12},{... | collective-permute-start | bytes 6536 | tf_op jit(solution)/shard_map/ppermute | solution.py:21
  117.0 9.8 %collective-permute-start.19 = (f32[16,34,1]{2,1,0:T(8,128)S(1)}, f32[16,34,1]{2,1,0:T(8,128)S(1)}, u32[]{:S(2)}, u32[]{:S(2)}) collective-permute-start(f32[16,34,1]{2,1,0:T(8,128)S(1)} %get-tuple-element.133), channel_id=1, source_target_pairs={{0,1},{1,2},{2,3},{4,5},{5,6},{6,7},{8,9},{9,10},{10,11},{12,13},{... | collective-permute-start | bytes 6536 | tf_op jit(solution)/shard_map/ppermute | solution.py:19
  136.1 10.3 %collective-permute-start.22 = (f32[16,34,1]{2,1,0:T(8,128)S(1)}, f32[16,34,1]{2,1,0:T(8,128)S(1)}, u32[]{:S(2)}, u32[]{:S(2)}) collective-permute-start(f32[16,34,1]{2,1,0:T(8,128)S(1)} %get-tuple-element.130), channel_id=1, source_target_pairs={{1,0},{2,1},{3,2},{5,4},{6,5},{7,6},{9,8},{10,9},{11,10},{13,12},{... | collective-permute-start | bytes 6536 | tf_op jit(solution)/shard_map/ppermute | solution.py:21
  138.1 9.5 %collective-permute-start.23 = (f32[16,34,1]{2,1,0:T(8,128)S(1)}, f32[16,34,1]{2,1,0:T(8,128)S(1)}, u32[]{:S(2)}, u32[]{:S(2)}) collective-permute-start(f32[16,34,1]{2,1,0:T(8,128)S(1)} %get-tuple-element.131), channel_id=1, source_target_pairs={{0,1},{1,2},{2,3},{4,5},{5,6},{6,7},{8,9},{9,10},{10,11},{12,13},{... | collective-permute-start | bytes 6536 | tf_op jit(solution)/shard_map/ppermute | solution.py:19
  149.4 12.7 %collective-permute-start.24 = (bf16[6,32,512]{2,1,0:T(8,128)(2,1)}, bf16[6,32,512]{2,1,0:T(8,128)(2,1)S(1)}, u32[]{:S(2)}, u32[]{:S(2)}) collective-permute-start(bf16[6,32,512]{2,1,0:T(8,128)(2,1)} %bitcast_dynamic-update-slice_fusion), channel_id=1, source_target_pairs={{0,64},{64,0},{1,65},{65,1},{2,66},{66,2},{3,67},{67,3},{4,68},{68... | collective-permute-start | bytes 589832 | tf_op jit(solution)/shard_map/ppermute | solution.py:31
  314.6 10.0 %collective-permute-start.27 = (f32[16,34,1]{2,1,0:T(8,128)S(1)}, f32[16,34,1]{2,1,0:T(8,128)S(1)}, u32[]{:S(2)}, u32[]{:S(2)}) collective-permute-start(f32[16,34,1]{2,1,0:T(8,128)S(1)} %get-tuple-element.118), channel_id=1, source_target_pairs={{1,0},{2,1},{3,2},{5,4},{6,5},{7,6},{9,8},{10,9},{11,10},{13,12},{... | collective-permute-start | bytes 6536 | tf_op jit(solution)/shard_map/ppermute | solution.py:21
  337.9 10.3 %collective-permute-start.31 = (f32[16,34,1]{2,1,0:T(8,128)S(1)}, f32[16,34,1]{2,1,0:T(8,128)S(1)}, u32[]{:S(2)}, u32[]{:S(2)}) collective-permute-start(f32[16,34,1]{2,1,0:T(8,128)S(1)} %get-tuple-element.128), channel_id=1, source_target_pairs={{1,0},{2,1},{3,2},{5,4},{6,5},{7,6},{9,8},{10,9},{11,10},{13,12},{... | collective-permute-start | bytes 6536 | tf_op jit(solution)/shard_map/ppermute | solution.py:21
  339.9 9.5 %collective-permute-start.32 = (f32[16,34,1]{2,1,0:T(8,128)S(1)}, f32[16,34,1]{2,1,0:T(8,128)S(1)}, u32[]{:S(2)}, u32[]{:S(2)}) collective-permute-start(f32[16,34,1]{2,1,0:T(8,128)S(1)} %get-tuple-element.129), channel_id=1, source_target_pairs={{0,1},{1,2},{2,3},{4,5},{5,6},{6,7},{8,9},{9,10},{10,11},{12,13},{... | collective-permute-start | bytes 6536 | tf_op jit(solution)/shard_map/ppermute | solution.py:19
  358.8 10.3 %collective-permute-start.35 = (f32[16,34,1]{2,1,0:T(8,128)S(1)}, f32[16,34,1]{2,1,0:T(8,128)S(1)}, u32[]{:S(2)}, u32[]{:S(2)}) collective-permute-start(f32[16,34,1]{2,1,0:T(8,128)S(1)} %get-tuple-element.126), channel_id=1, source_target_pairs={{1,0},{2,1},{3,2},{5,4},{6,5},{7,6},{9,8},{10,9},{11,10},{13,12},{... | collective-permute-start | bytes 6536 | tf_op jit(solution)/shard_map/ppermute | solution.py:21
  360.7 9.5 %collective-permute-start.36 = (f32[16,34,1]{2,1,0:T(8,128)S(1)}, f32[16,34,1]{2,1,0:T(8,128)S(1)}, u32[]{:S(2)}, u32[]{:S(2)}) collective-permute-start(f32[16,34,1]{2,1,0:T(8,128)S(1)} %get-tuple-element.127), channel_id=1, source_target_pairs={{0,1},{1,2},{2,3},{4,5},{5,6},{6,7},{8,9},{9,10},{10,11},{12,13},{... | collective-permute-start | bytes 6536 | tf_op jit(solution)/shard_map/ppermute | solution.py:19
  379.6 10.3 %collective-permute-start.39 = (f32[16,34,1]{2,1,0:T(8,128)S(1)}, f32[16,34,1]{2,1,0:T(8,128)S(1)}, u32[]{:S(2)}, u32[]{:S(2)}) collective-permute-start(f32[16,34,1]{2,1,0:T(8,128)S(1)} %get-tuple-element.124), channel_id=1, source_target_pairs={{1,0},{2,1},{3,2},{5,4},{6,5},{7,6},{9,8},{10,9},{11,10},{13,12},{... | collective-permute-start | bytes 6536 | tf_op jit(solution)/shard_map/ppermute | solution.py:21
  381.5 9.5 %collective-permute-start.40 = (f32[16,34,1]{2,1,0:T(8,128)S(1)}, f32[16,34,1]{2,1,0:T(8,128)S(1)}, u32[]{:S(2)}, u32[]{:S(2)}) collective-permute-start(f32[16,34,1]{2,1,0:T(8,128)S(1)} %get-tuple-element.125), channel_id=1, source_target_pairs={{0,1},{1,2},{2,3},{4,5},{5,6},{6,7},{8,9},{9,10},{10,11},{12,13},{... | collective-permute-start | bytes 6536 | tf_op jit(solution)/shard_map/ppermute | solution.py:19
  400.4 10.3 %collective-permute-start.43 = (f32[16,34,1]{2,1,0:T(8,128)S(1)}, f32[16,34,1]{2,1,0:T(8,128)S(1)}, u32[]{:S(2)}, u32[]{:S(2)}) collective-permute-start(f32[16,34,1]{2,1,0:T(8,128)S(1)} %get-tuple-element.122), channel_id=1, source_target_pairs={{1,0},{2,1},{3,2},{5,4},{6,5},{7,6},{9,8},{10,9},{11,10},{13,12},{... | collective-permute-start | bytes 6536 | tf_op jit(solution)/shard_map/ppermute | solution.py:21
  402.4 11.5 %collective-permute-start.44 = (f32[16,34,1]{2,1,0:T(8,128)S(1)}, f32[16,34,1]{2,1,0:T(8,128)S(1)}, u32[]{:S(2)}, u32[]{:S(2)}) collective-permute-start(f32[16,34,1]{2,1,0:T(8,128)S(1)} %get-tuple-element.123), channel_id=1, source_target_pairs={{0,1},{1,2},{2,3},{4,5},{5,6},{6,7},{8,9},{9,10},{10,11},{12,13},{... | collective-permute-start | bytes 6536 | tf_op jit(solution)/shard_map/ppermute | solution.py:19
  (40 other events, 447.9 us)
where the time goes:
time: 581 us; the launch traced here: 570 us
  blocking collectives  270 us (46%)
  starting transfers between devices  113 us (19%)
  waiting for transfers between devices  93.4 us (16%)
  other arithmetic  59.7 us (10%)
  local copies, waits for them, and re-layouts  20.1 us (3%)
  matrix products  11.6 us (2%)
    psum x2, blocking collectives, per_device(): total_gap = lax.psum(local_gap, ('gx', 'gy'))  270 us
    ppermute x22, starting transfers between devices, with_halo(): lax.ppermute(tail, axis, [(i, (i + 1) % count) for i in range(ends)])  68.2 us
    ppermute x22, waiting for transfers between devices, with_halo(): lax.ppermute(tail, axis, [(i, (i + 1) % count) for i in range(ends)])  53.7 us
    ppermute x22, starting transfers between devices, with_halo(): lax.ppermute(head, axis, [((i + 1) % count, i) for i in range(ends)])  40 us
    ppermute x22, waiting for transfers between devices, with_halo(): lax.ppermute(head, axis, [((i + 1) % count, i) for i in range(ends)])  34.5 us
    sub x10, other arithmetic, vertical_mix(): spread + jnp.concatenate([upward, zero_layer], 0)  15.9 us
    add x11, other arithmetic, advance(): spread = center + diffusion_row[:, None, None] * laplace  11.8 us
  transfers between devices with their start and end apart: 46, of which 41 were waited for; matrix products, arithmetic and copies ran while one was open for 4% of the time, Pallas kernels for 0%

commit v1 on v0

v1 whole, which is shorter than its diff:
```python
import jax
import jax.numpy as jnp
from jax import lax
from jax.experimental import pallas as pl
from jax.experimental.pallas import tpu as pltpu
from jax.sharding import PartitionSpec as P

F32 = jnp.float32
BF16 = jnp.bfloat16
SUB = 6
LEVELS = 16
CX = 32
CY = 512
LANES = 128
OWN_TILES = CY // LANES
COLS = CY + LANES
ROWS = CX + 32
BAND = CX + 16
PATTERNS = 32
BLOCKS = CX * OWN_TILES
VMEM_LIMIT = 48 * 1024 * 1024

N_FIELDS = LEVELS + 3 + SUB - 1
AT_COUPLING, AT_LAND, AT_MASK, AT_GUESS = LEVELS, LEVELS + 1, LEVELS + 2, LEVELS + 3
PACK_LANES = 256

VM = pl.BlockSpec(memory_space=pltpu.VMEM)
SM = pl.BlockSpec(memory_space=pltpu.SMEM)


def shape(*dims, dtype=F32):
    return jax.ShapeDtypeStruct(dims, dtype)


def call(body, outs, scratch, ins, out_specs=None, **kw):
    return pl.pallas_call(
        body,
        out_shape=outs,
        in_specs=ins,
        out_specs=[VM] * len(outs) if out_specs is None else out_specs,
        scratch_shapes=scratch,
        compiler_params=pltpu.CompilerParams(vmem_limit_bytes=VMEM_LIMIT),
        **kw,
    )


def iotas():
    row = lax.broadcasted_iota(jnp.int32, (8, LANES), 0)
    lane = lax.broadcasted_iota(jnp.int32, (8, LANES), 1)
    return row, lane


def roll_lanes(x, shift):
    shift %= LANES
    return x if shift == 0 else pltpu.roll(x, shift, 1)


def pack_columns(fields, one, three, even):
    _, lane = iotas()
    groups = PACK_LANES // LANES if len(fields) > 16 else 1
    for tile in range(6):
        for g in range(groups):
            left = jnp.zeros((8, LANES), F32)
            right = jnp.zeros((8, LANES), F32)
            for f in range(g * 16, min(len(fields), g * 16 + 16)):
                at = (f % 16) * 8
                head, tail = fields[f](tile)
                left = jnp.where((lane >= at) & (lane < at + 8), roll_lanes(head, at), left)
                right = jnp.where((lane >= at) & (lane < at + 8), roll_lanes(tail, at + 8), right)
            span = (slice(tile * 8, tile * 8 + 8), slice(g * LANES, (g + 1) * LANES))
            one[span] = jnp.where(even, right, left)
            three[span] = jnp.where(even, left, right)


def side_halos(one, three, even, first, last, tile, g):
    span = (slice(tile * 8, tile * 8 + 8), slice(g * LANES, (g + 1) * LANES))
    a, b = one[span], three[span]
    right = jnp.where(last, 0.0, jnp.where(even, a, b))
    left = jnp.where(first, 0.0, jnp.where(even, b, a))
    return right, left


def side_tile(right, left, f, lane):
    at = (f % 16) * 8
    return jnp.where(
        lane < 6,
        roll_lanes(right, -at),
        jnp.where(lane >= LANES - 6, roll_lanes(left, LANES - 8 - at), 0.0),
    )


def place_sides(dst_of, fields, one, three, even, first, last):
    _, lane = iotas()
    for tile in range(6):
        packs = {}
        for f in fields:
            g = f // 16
            if g not in packs:
                packs[g] = side_halos(one, three, even, first, last, tile, g)
            dst_of(f, tile, side_tile(*packs[g], f, lane))


def place_rows(dst, own, upper, lower):
    dst[8:16, :CY] = upper
    dst[16 : 16 + CX, :CY] = own
    dst[16 + CX : 24 + CX, :CY] = lower


def zero_pads(ref, count):
    for l in range(count):
        ref[l, 0:8, :] = jnp.zeros((8, COLS), F32)
        ref[l, ROWS - 8 : ROWS, :] = jnp.zeros((8, COLS), F32)


def position():
    gy = lax.axis_index("gy")
    return gy % 2 == 0, gy == 0, gy == lax.axis_size("gy") - 1


class Strip:
    def __init__(self, r, first, last):
        self.r = r
        row, lane = iotas()
        self.row_first, self.row_last = row == 0, row == 7
        self.lane_first, self.lane_last = lane == 0, lane == LANES - 1
        self.inside = ((lane < 6) & jnp.logical_not(last)) | (
            (lane >= LANES - 6) & jnp.logical_not(first)
        )

    def load(self, ref, l, shift=0):
        rows = pl.ds(self.r * 8 + shift, 8)
        return [ref[l, rows, k * LANES : (k + 1) * LANES] for k in range(OWN_TILES + 1)]

    def spread(self, ref, l, d):
        x = self.load(ref, l)
        above = self.load(ref, l, -8)
        below = self.load(ref, l, 8)
        out = []
        n = len(x)
        for k in range(n):
            c = x[k]
            up = pltpu.roll(jnp.where(self.row_last, above[k], c), 1, 0)
            down = pltpu.roll(jnp.where(self.row_first, below[k], c), 7, 0)
            left = pltpu.roll(jnp.where(self.lane_last, x[k - 1], c), 1, 1)
            right = pltpu.roll(jnp.where(self.lane_first, x[(k + 1) % n], c), LANES - 1, 1)
            out.append(c + d * (((up + down) + (left + right)) - 4.0 * c))
        return out

    def store(self, ref, l, values):
        rows = pl.ds(self.r * 8, 8)
        for k, v in enumerate(values):
            if k == OWN_TILES:
                v = jnp.where(self.inside, v, 0.0)
            ref[l, rows, k * LANES : (k + 1) * LANES] = v

    def save(self, ref, l, values):
        rows = pl.ds(self.r * 8 - 8, 8)
        for k, v in enumerate(values):
            ref[l, rows, k * LANES : (k + 1) * LANES] = v

    def recall(self, ref, l):
        return self.load(ref, l, -8)


def flux_between(mix, lower, upper):
    return [mix * (a - b) for a, b in zip(lower, upper)]


def added(a, b):
    return [x + y for x, y in zip(a, b)]


def less(a, b):
    return [x - y for x, y in zip(a, b)]


def surface(v, f, c, m, ml, ocean):
    new, emitted = [], []
    for vk, fk, ck, mk, lk in zip(v, f, c, m, ml):
        mf = mk * fk
        flux = ck * (vk - (mf + lk))
        warmed = vk + ck * mf
        new.append(jnp.where(ocean, warmed, vk - flux))
        emitted.append(jnp.where(ocean, mk * warmed, flux))
    return new, emitted


def strips(t):
    return (1, 7) if t < SUB - 1 else (2, 6)


def write_series(series, emitted):
    for t in range(SUB):
        for half in range(CX // 16):
            rows = slice(8 + half * 16, 24 + half * 16)
            series[t, half * 16 : half * 16 + 16, :] = emitted[t, rows, :CY].astype(BF16)


def pack_first(state, guess, coupling, land, mask, upper, lower, one, three):
    even, _, _ = position()

    def field(f):
        def of(tile):
            if tile == 0:
                block = upper.at[f]
                rows = slice(0, 8)
            elif tile == 5:
                block = lower.at[f]
                rows = slice(0, 8)
            else:
                rows = slice(tile * 8 - 8, tile * 8)
                if f < LEVELS:
                    block = state.at[f]
                elif f == AT_COUPLING:
                    block = coupling
                elif f == AT_LAND:
                    block = land
                elif f == AT_MASK:
                    block = mask
                else:
                    block = guess.at[f - AT_GUESS]
            if f >= AT_GUESS and 0 < tile < 5:
                base = (tile - 1) // 2 * 16
                part = slice((tile - 1) % 2 * 8, (tile - 1) % 2 * 8 + 8)
                head = block[base : base + 16, :LANES].astype(F32)[part]
                tail = block[base : base + 16, CY - LANES :].astype(F32)[part]
                return head, tail
            head, tail = block[rows, :LANES], block[rows, CY - LANES :]
            return head.astype(F32), tail.astype(F32)

        return of

    pack_columns([field(f) for f in range(N_FIELDS)], one, three, even)


CONE = SUB + 1


def first_cone(
    diff, mix, state, guess, coupling, land, mask, upper, lower, one, three,
    series, hd, ud, hs, us, fixed,
    s0, s1, g, emitted,
):
    even, first, last = position()
    ocean = lax.axis_index("comp") == 1
    zero_pads(s0, CONE)
    zero_pads(s1, CONE - 1)
    for l in range(CONE):
        place_rows(s0.at[l], state[l], upper[l], lower[l])

    def rows_of(ref, k, f, own):
        ref[k, 0:8, :CY] = upper[f]
        ref[k, 8 : 8 + CX, :CY] = own
        ref[k, 8 + CX : 16 + CX, :CY] = lower[f]

    rows_of(fixed, 0, AT_COUPLING, coupling[...])
    rows_of(fixed, 1, AT_MASK, mask[...].astype(F32))
    rows_of(fixed, 2, AT_LAND, land[...])
    for t in range(SUB - 1):
        rows_of(g, t, AT_GUESS + t, guess[t].astype(F32))
    g[SUB - 1, 8 : 8 + CX, :CY] = guess[SUB - 1].astype(F32)

    side = slice(CY, COLS)
    slot = {AT_COUPLING: 0, AT_MASK: 1, AT_LAND: 2}

    def put(f, tile, value):
        rows = slice(tile * 8, tile * 8 + 8)
        if f < LEVELS:
            s0[f, tile * 8 + 8 : tile * 8 + 16, side] = value
        elif f < AT_GUESS:
            fixed[slot[f], rows, side] = value
        else:
            g[f - AT_GUESS, rows, side] = value

    fields = [*range(CONE), *range(LEVELS, N_FIELDS)]
    place_sides(put, fields, one, three, even, first, last)
    g[SUB - 1, :, side] = jnp.zeros((BAND, LANES), F32)
    fixed[2] = (1.0 - fixed[1]) * fixed[2]

    for t in range(SUB):
        src, dst = (s0, s1) if t % 2 == 0 else (s1, s0)

        @pl.loop(*strips(t))
        def _(r, t=t, src=src, dst=dst):
            strip = Strip(r, first, last)
            h = strip.spread(src, 0, diff[0])
            u_prev = None
            for l in range(SUB - t):
                h_next = strip.spread(src, l + 1, diff[l + 1])
                u = flux_between(mix[l], h_next, h)
                v = added(h, u)
                if l == t and t < 3:
                    strip.save(us, t, v)
                    strip.save(hs, t, h)
                if u_prev is not None:
                    v = less(v, u_prev)
                if l == 0:
                    c, m, ml = (strip.recall(fixed, i) for i in range(3))
                    v, e = surface(v, strip.recall(g, t), c, m, ml, ocean)
                    strip.save(emitted, t, e[:OWN_TILES])
                if t < SUB - 1:
                    strip.store(dst, l, v)
                h, u_prev = h_next, u
            strip.save(hd, t, h)
            strip.save(ud, t, u_prev)

    write_series(series, emitted)


def first_rest(
    diff, mix, state, upper, lower, one, three, hd, ud,
    final, hs, us,
    s0, s1,
):
    even, first, last = position()
    zero_pads(s0, LEVELS)
    zero_pads(s1, LEVELS)
    for l in range(CONE, LEVELS):
        place_rows(s0.at[l], state[l], upper[l], lower[l])

    def put(f, tile, value):
        s0[f, tile * 8 + 8 : tile * 8 + 16, CY:COLS] = value

    place_sides(put, list(range(CONE, LEVELS)), one, three, even, first, last)

    for t in range(SUB):
        src, dst = (s0, s1) if t % 2 == 0 else (s1, s0)

        @pl.loop(*strips(t))
        def _(r, t=t, src=src, dst=dst):
            strip = Strip(r, first, last)
            h = strip.recall(hd, t)
            u_prev = strip.recall(ud, t)
            for l in range(SUB - t, LEVELS):
                if l < LEVELS - 1:
                    h_next = strip.spread(src, l + 1, diff[l + 1])
                    u = flux_between(mix[l], h_next, h)
                    v = added(h, u)
                else:
                    h_next = u = None
                    v = h
                if l == t and t >= 3:
                    strip.save(us, t - 3, v)
                    strip.save(hs, t - 3, h)
                v = less(v, u_prev)
                if t < SUB - 1:
                    strip.store(dst, l, v)
                elif l >= SUB:
                    rows = pl.ds(r * 8 - 16, 8)
                    for k in range(OWN_TILES):
                        final[l, rows, k * LANES : (k + 1) * LANES] = v[k]
                h, u_prev = h_next, u


def regrid(
    src, pat, received, weights, mask,
    out, top, bottom, gap,
    x, y,
):
    partial = [jnp.zeros((8, LANES), F32) for _ in range(SUB)]
    wet = jnp.zeros((8, LANES), F32)
    for half in range(CX // 16):
        for j in range(OWN_TILES):
            cols = slice(j * LANES, (j + 1) * LANES)
            m16 = mask[half * 16 : half * 16 + 16, cols].astype(F32)
            wet += m16[:8] + m16[8:]
            for t in range(SUB):
                v16 = received[t, half * 16 : half * 16 + 16, cols].astype(F32)
                partial[t] += m16[:8] * v16[:8] + m16[8:] * v16[8:]
                for part in range(2):
                    row = half * 16 + part * 8
                    start = (row * OWN_TILES + j) * 8 + t
                    x[pl.ds(start, 8, stride=OWN_TILES * 8), :] = v16[part * 8 : part * 8 + 8]

    @pl.loop(0, BLOCKS, unroll=8)
    def _(q):
        a = [x[pl.ds(pl.multiple_of(src[q, k] * 8, 8), 8), :].astype(BF16) for k in range(2)]
        w = [weights[pat[q, k]] for k in range(2)]
        r = jnp.dot(
            jnp.concatenate(a, 1), jnp.concatenate(w, 0), preferred_element_type=F32
        )
        y[pl.ds(q, 8, stride=BLOCKS), :] = r

    for t in range(SUB):
        for part in range(CX // 8):
            for j in range(OWN_TILES):
                cols = slice(j * LANES, (j + 1) * LANES)
                rows = slice(part * 8, part * 8 + 8)
                v = y[pl.ds(t * BLOCKS + part * 8 * OWN_TILES + j, 8, stride=OWN_TILES), :]
                out[t, rows, cols] = v
                partial[t] -= mask[rows, cols].astype(F32) * v
                if t < SUB - 1:
                    if part == 0:
                        top[t, :, cols] = v
                    if part == CX // 8 - 1:
                        bottom[t, :, cols] = v
    _, lane = iotas()
    total = jnp.zeros((8, LANES), F32)
    for t, value in enumerate([*partial, wet]):
        summed = jnp.sum(value, axis=(0, 1), keepdims=True)
        total = jnp.where(lane == t, summed, total)
    for k in range(gap.shape[0]):
        gap[k] = total[:1]


def pack_second(out, upper, lower, one, three):
    even, _, _ = position()

    def field(t):
        def of(tile):
            if tile == 0:
                block, rows = upper.at[t], slice(0, 8)
            elif tile == 5:
                block, rows = lower.at[t], slice(0, 8)
            else:
                block, rows = out.at[t], slice(tile * 8 - 8, tile * 8)
            return block[rows, :LANES], block[rows, CY - LANES :]

        return of

    pack_columns([field(t) for t in range(SUB - 1)], one, three, even)


def gap_means(gap):
    total = jnp.sum(gap[...], axis=0)
    lane = lax.broadcasted_iota(jnp.int32, (1, LANES), 1)
    wet = jnp.sum(jnp.where(lane == SUB, total, 0.0), axis=1, keepdims=True)
    return [
        jnp.sum(jnp.where(lane == t, total, 0.0), axis=1, keepdims=True) / wet for t in range(SUB)
    ]


def second_cone(
    diff, mix, fixed, regridded, upper, lower, one, three, gap, hs, hd, us,
    series, final0, hx, ux,
    s0, s1, g, emitted,
):
    even, first, last = position()
    ocean = lax.axis_index("comp") == 1
    zero_pads(s0, 3)
    zero_pads(s1, 3)
    for t in range(SUB):
        if t < SUB - 1:
            g[t, 0:8, :CY] = upper[t]
            g[t, 8 + CX : 16 + CX, :CY] = lower[t]
        g[t, 8 : 8 + CX, :CY] = regridded[t]

    def put(f, tile, value):
        g[f, tile * 8 : tile * 8 + 8, CY:COLS] = value

    place_sides(put, list(range(SUB - 1)), one, three, even, first, last)
    g[SUB - 1, :, CY:COLS] = jnp.zeros((BAND, LANES), F32)
    means = [jnp.broadcast_to(v, (8, LANES)) for v in gap_means(gap)]

    for t in range(SUB):
        src, dst = (s0, s1) if t % 2 == 0 else (s1, s0)

        @pl.loop(*strips(t))
        def _(r, t=t, src=src, dst=dst):
            strip = Strip(r, first, last)
            h = strip.spread(src, 0, diff[0]) if t else None
            u_prev = None
            for l in range(min(t, SUB - 1 - t) + 1):
                if l < t:
                    if l + 1 < t:
                        h_next = strip.spread(src, l + 1, diff[l + 1])
                    else:
                        h_next = strip.recall(hd if t == 3 else hs, t)
                    u = flux_between(mix[l], h_next, h)
                    v = added(h, u)
                else:
                    v = strip.recall(us, t)
                if u_prev is not None:
                    v = less(v, u_prev)
                if l == 0:
                    c, m, ml = (strip.recall(fixed, i) for i in range(3))
                    f = [a + b * means[t] for a, b in zip(strip.recall(g, t), m)]
                    v, e = surface(v, f, c, m, ml, ocean)
                    strip.save(emitted, t, e[:OWN_TILES])
                    if t == SUB - 1:
                        rows = pl.ds(r * 8 - 16, 8)
                        for k in range(OWN_TILES):
                            final0[rows, k * LANES : (k + 1) * LANES] = v[k]
                if t < SUB - 1:
                    strip.store(dst, l, v)
                if l < t:
                    h, u_prev = h_next, u
            if t >= 3:
                strip.save(hx, t - 3, h)
                strip.save(ux, t - 3, u_prev)

    write_series(series, emitted)


def second_rest(
    diff, mix, hx, ux, hs, us, final0, whole,
    final,
    s0, s1,
):
    del whole
    gy = lax.axis_index("gy")
    first, last = gy == 0, gy == lax.axis_size("gy") - 1
    zero_pads(s0, SUB)
    zero_pads(s1, SUB)
    final[0] = final0[...]
    for t in range(3, SUB):
        src, dst = (s0, s1) if t % 2 == 0 else (s1, s0)

        @pl.loop(*strips(t))
        def _(r, t=t, src=src, dst=dst):
            strip = Strip(r, first, last)
            h = strip.recall(hx, t - 3)
            u_prev = strip.recall(ux, t - 3)
            for l in range(SUB - t, t + 1):
                if l < t:
                    if l + 1 < t:
                        h_next = strip.spread(src, l + 1, diff[l + 1])
                    else:
                        h_next = strip.recall(hs, t - 3)
                    u = flux_between(mix[l], h_next, h)
                    v = added(h, u)
                    h = h_next
                else:
                    u = None
                    v = strip.recall(us, t - 3)
                v = less(v, u_prev)
                u_prev = u
                if t < SUB - 1:
                    strip.store(dst, l, v)
                else:
                    rows = pl.ds(r * 8 - 16, 8)
                    for k in range(OWN_TILES):
                        final[l, rows, k * LANES : (k + 1) * LANES] = v[k]


def finish(regridded, mask, gap, forcing):
    for t, mean in enumerate(gap_means(gap)):
        forcing[t] = regridded[t] + mask[...].astype(F32) * mean


def shifted(value, axis, by):
    n = lax.axis_size(axis)
    return lax.ppermute(value, axis, [(i, (i + by) % n) for i in range(n)])


def paired(value, axis, mask):
    return lax.ppermute(value, axis, [(i, i ^ mask) for i in range(lax.axis_size(axis))])


def per_device(
    state, guess, diffusion, mixing, coupling, land_temp, land_mask, weights, source_block, pattern
):
    state, guess, diff, mix, coupling = state[0], guess[0], diffusion[0], mixing[0], coupling[0]
    weights = weights[0]
    src = source_block[0].reshape(BLOCKS, 2)
    pat = pattern[0].reshape(BLOCKS, 2)
    peers = lax.axis_size("gx") * lax.axis_size("gy")
    band = lambda n: shape(n, BAND, COLS)
    field_buf = lambda n: pltpu.VMEM((n, ROWS, COLS), F32)
    band_buf = lambda n: pltpu.VMEM((n, BAND, COLS), F32)

    def edge(rows):
        return jnp.concatenate(
            [
                state[:, rows],
                coupling[None, rows],
                land_temp[None, rows],
                land_mask[None, rows].astype(F32),
                guess[: SUB - 1, rows].astype(F32),
            ]
        )

    lower = shifted(edge(slice(0, 8)), "gx", -1)
    upper = shifted(edge(slice(CX - 8, CX)), "gx", 1)
    packed = shape(BAND, PACK_LANES)
    one, three = call(pack_first, [packed, packed], [], [VM] * 7)(
        state, guess, coupling, land_temp, land_mask, upper, lower
    )
    one, three = paired(one, "gy", 1), paired(three, "gy", 3)

    series, hd, ud, hs, us, fixed = call(
        first_cone,
        [shape(SUB, CX, CY, dtype=BF16), band(SUB), band(SUB), band(3), band(3), band(3)],
        [field_buf(CONE), field_buf(CONE), band_buf(SUB), band_buf(SUB)],
        [SM, SM] + [VM] * 9,
    )(diff, mix, state, guess, coupling, land_temp, land_mask, upper, lower, one, three)

    def exchange(series):
        received = paired(series, "comp", 1)
        edges = shape(SUB - 1, 8, CY)
        out, top, bottom, gap = call(
            regrid,
            [shape(SUB, CX, CY), edges, edges, shape(peers, 1, LANES)],
            [pltpu.VMEM((BLOCKS * 8, LANES), F32), pltpu.VMEM((BLOCKS * 8, LANES), F32)],
            [SM, SM, VM, VM, VM],
        )(src, pat, received, weights, land_mask)
        return out, top, bottom, gap

    whole, hs_rest, us_rest = call(
        first_rest,
        [shape(LEVELS, CX, CY), band(3), band(3)],
        [field_buf(LEVELS), field_buf(LEVELS)],
        [SM, SM] + [VM] * 7,
    )(diff, mix, state, upper, lower, one, three, hd, ud)

    out, top, bottom, gap = exchange(series)
    lower, upper = shifted(top, "gx", -1), shifted(bottom, "gx", 1)
    gap = lax.all_to_all(gap, ("gx", "gy"), 0, 0)
    packed = shape(BAND, LANES)
    one, three = call(pack_second, [packed, packed], [], [VM] * 3)(out, upper, lower)
    one, three = paired(one, "gy", 1), paired(three, "gy", 3)

    series, final0, hx, ux = call(
        second_cone,
        [shape(SUB, CX, CY, dtype=BF16), shape(CX, CY), band(3), band(3)],
        [field_buf(3), field_buf(3), band_buf(SUB), band_buf(SUB)],
        [SM, SM] + [VM] * 10,
    )(diff, mix, fixed, out, upper, lower, one, three, gap, hs, hd, us)

    (whole,) = call(
        second_rest,
        [shape(LEVELS, CX, CY)],
        [field_buf(SUB), field_buf(SUB)],
        [SM, SM] + [VM] * 5 + [pl.BlockSpec(memory_space=pl.ANY)],
        out_specs=[pl.BlockSpec((SUB, CX, CY), lambda i: (0, 0, 0))],
        grid=(1,),
        input_output_aliases={7: 0},
    )(diff, mix, hx, ux, hs_rest, us_rest, final0, whole)

    out, _, _, gap = exchange(series)
    gap = lax.all_to_all(gap, ("gx", "gy"), 0, 0)
    (forcing,) = call(finish, [shape(SUB, CX, CY)], [], [VM] * 3)(out, land_mask, gap)
    return whole[None], forcing[None]


def solution(mesh):
    placed = (
        P("comp", None, "gx", "gy"),
        P("comp", None, "gx", "gy"),
        P("comp", None),
        P("comp", None),
        P("comp", "gx", "gy"),
        P("gx", "gy"),
        P("gx", "gy"),
        P("comp", ("gx", "gy"), None, None),
        P("comp", "gx", "gy", None),
        P("comp", "gx", "gy", None),
    )
    return jax.shard_map(
        per_device,
        mesh=mesh,
        in_specs=placed,
        out_specs=(P("comp", None, "gx", "gy"), P("comp", None, "gx", "gy")),
        check_vma=False,
    )
```

time: 581 us -> 121 us (0.21); the launches traced: 570 us -> 121 us
  blocking collectives: 270 us -> 0 us
  starting transfers between devices: 113 us -> 36.5 us
  waiting for transfers between devices: 93.4 us -> 29 us
  other arithmetic: 59.7 us -> 0.87 us
  Pallas kernels: 0 us -> 36.6 us
  matrix products: 11.6 us -> 0 us
    psum x2 -> x0, blocking collectives: 270 us -> none  [per_device(): total_gap = lax.psum(local_gap, ('gx', 'gy'))]
    ppermute x46 -> x10, starting transfers between devices: 113 us -> 22.5 us  [the longest x4 11.6 us: shifted(): return lax.ppermute(value, axis, [(i, (i + by) % n) for i in range(n)])]
    ppermute x46 -> x10, waiting for transfers between devices: 93.4 us -> 24.5 us  [the longest x4 13 us: shifted(): return lax.ppermute(value, axis, [(i, (i + by) % n) for i in range(n)])]
    pallas_call x0 -> x9, Pallas kernels: none -> 36.6 us  [the longest x2 13.5 us: exchange(): call(regrid, [shape(SUB, CX, CY), edges, edges, shape(peers, 1, LANES)],...]
    sub x12 -> x0, other arithmetic: 15.9 us -> none  [the longest x10 15.9 us: vertical_mix(): spread + jnp.concatenate([upward, zero_layer], 0)]
    unnamed x36 -> x81, local copies, waits for them, and re-layouts: 2.05 us -> 16.9 us
    all_to_all x0 -> x2, starting transfers between devices: none -> 14 us  [per_device(): gap = lax.all_to_all(gap, ('gx', 'gy'), 0, 0)]
    add x13 -> x0, other arithmetic: 12.7 us -> none  [the longest x11 11.8 us: advance(): spread = center + diffusion_row[:, None, None] * laplace]
  transfers between devices with their start and end apart: 46 -> 12, of which waited for: 41 -> 6; matrix products, arithmetic and copies ran while one was open for 4% -> 0% of each run, Pallas kernels for 0% -> 10%
where the time goes in v1:
time: 121 us
  Pallas kernels  36.6 us (30%)
  starting transfers between devices  36.5 us (30%)
  waiting for transfers between devices  29 us (24%)
  local copies, waits for them, and re-layouts  16.9 us (14%)
    unnamed x81, local copies, waits for them, and re-layouts  16.9 us
    all_to_all x2, starting transfers between devices, per_device(): gap = lax.all_to_all(gap, ('gx', 'gy'), 0, 0)  14 us
    pallas_call x2, Pallas kernels, exchange(): call(regrid, [shape(SUB, CX, CY), edges, edges, shape(peers, 1, LANES)],...  13.5 us
    ppermute x4, waiting for transfers between devices, shifted(): return lax.ppermute(value, axis, [(i, (i + by) % n) for i in range(n)])  13 us
    ppermute x4, starting transfers between devices, shifted(): return lax.ppermute(value, axis, [(i, (i + by) % n) for i in range(n)])  11.6 us
    ppermute x6, waiting for transfers between devices, paired(): lax.ppermute(value, axis, [(i, i ^ mask) for i in range(lax.axis_size(axi...  11.5 us
    ppermute x6, starting transfers between devices, paired(): lax.ppermute(value, axis, [(i, i ^ mask) for i in range(lax.axis_size(axi...  10.9 us
    pallas_call x1, Pallas kernels, per_device(): call(first_rest, [shape(LEVELS, CX, CY), band(3), band(3)], [field_buf(LE...  8.45 us
  transfers between devices with their start and end apart: 12, of which 6 were waited for; matrix products, arithmetic and copies ran while one was open for 0% of the time, Pallas kernels for 10%

profile of v1, /device:TPU:1, one launch (start us, length us, event | category | flops | bytes accessed | tf_op | source)
XLA Modules:
  0.0 120.7 jit_solution(2863378898548972590)
XLA Ops:
  0.6 1.2 slice_dynamic-update-slice_fusion
  3.5 6.8 %collective-permute-start.1 = (f32[24,8,512]{2,1,0:T(8,128)S(1)}, f32[24,8,512]{2,1,0:T(8,128)S(1)}, u32[]{:S(2)}, u32[]{:S(2)}) collective-permute-start(f32[24,8,512]{2,1,0:T(8,128)S(1)} %get-tuple-element.50), channel_id=1, source_target_pairs={{0,60},{4,0},{8,4},{12,8},{16,12},{20,16},{24,20},{28,24},{32,28},... | collective-permute-start | bytes 1179656 | tf_op jit(solution)/shard_map/ppermute | solution.py:543
  10.4 7.8 %collective-permute-done.1.lower = f32[24,8,512]{2,1,0:T(8,128)S(1)} collective-permute-done((f32[24,8,512]{2,1,0:T(8,128)S(1)}, f32[24,8,512]{2,1,0:T(8,128)S(1)}, u32[]{:S(2)}, u32[]{:S(2)}) %collective-permute-start.1) | collective-permute-done | bytes 393248 | tf_op jit(solution)/shard_map/ppermute | solution.py:543
  18.2 5.2 %collective-permute-done.upper = f32[24,8,512]{2,1,0:T(8,128)S(1)} collective-permute-done((f32[24,8,512]{2,1,0:T(8,128)S(1)}, f32[24,8,512]{2,1,0:T(8,128)S(1)}, u32[]{:S(2)}, u32[]{:S(2)}) %collective-permute-start) | collective-permute-done | bytes 393248 | tf_op jit(solution)/shard_map/ppermute | solution.py:543
  23.7 1.9 %collective-permute-start.2 = (f32[48,256]{1,0:T(8,128)S(1)}, f32[48,256]{1,0:T(8,128)S(1)}, u32[]{:S(2)}, u32[]{:S(2)}) collective-permute-start(f32[48,256]{1,0:T(8,128)S(1)} %get-tuple-element.25), channel_id=1, source_target_pairs={{0,1},{1,0},{2,3},{3,2},{4,5},{5,4},{6,7},{7,6},{8,9},{9,8},{10,11... | collective-permute-start | bytes 147464 | tf_op jit(solution)/shard_map/ppermute | solution.py:547
  25.7 1.3 %collective-permute-start.3 = (f32[48,256]{1,0:T(8,128)S(1)}, f32[48,256]{1,0:T(8,128)S(1)}, u32[]{:S(2)}, u32[]{:S(2)}) collective-permute-start(f32[48,256]{1,0:T(8,128)S(1)} %get-tuple-element.26), channel_id=1, source_target_pairs={{0,3},{1,2},{2,1},{3,0},{4,7},{5,6},{6,5},{7,4},{8,11},{9,10},{10,... | collective-permute-start | bytes 147464 | tf_op jit(solution)/shard_map/ppermute | solution.py:547
  27.0 2.2 %collective-permute-done.3.three = f32[48,256]{1,0:T(8,128)S(1)} collective-permute-done((f32[48,256]{1,0:T(8,128)S(1)}, f32[48,256]{1,0:T(8,128)S(1)}, u32[]{:S(2)}, u32[]{:S(2)}) %collective-permute-start.3) | collective-permute-done | bytes 49184 | tf_op jit(solution)/shard_map/ppermute | solution.py:547
  29.9 5.2 %shard_map.114 = (bf16[6,32,512]{2,1,0:T(8,128)(2,1)S(1)}, f32[6,48,640]{2,1,0:T(8,128)S(1)}, f32[6,48,640]{2,1,0:T(8,128)S(1)}, f32[3,48,640]{2,1,0:T(8,128)S(1...) custom-call(f32[16]{0:T(128)S(1)} %bitcast.33, f32[15]{0:T(128)S(1)} %bitcast.37, f32[16,32,512]{2,1,0:T(8,128)S(1)} %bitcast.20, ...), custom_call_target="tpu_custom_call" | custom-call | tf_op jit(solution)/shard_map/pallas_call | solution.py:581
  39.1 2.9 %collective-permute-start.4 = (bf16[6,32,512]{2,1,0:T(8,128)(2,1)S(1)}, bf16[6,32,512]{2,1,0:T(8,128)(2,1)S(1)}, u32[]{:S(2)}, u32[]{:S(2)}) collective-permute-start(bf16[6,32,512]{2,1,0:T(8,128)(2,1)S(1)} %get-tuple-element.28), channel_id=1, source_target_pairs={{0,64},{64,0},{1,65},{65,1},{2,66},{66,2},{3,67},{67,3},{4,68},{68... | collective-permute-start | bytes 589832 | tf_op jit(solution)/shard_map/ppermute | solution.py:547
  42.3 4.8 %collective-permute-done.4.received = bf16[6,32,512]{2,1,0:T(8,128)(2,1)S(1)} collective-permute-done((bf16[6,32,512]{2,1,0:T(8,128)(2,1)S(1)}, bf16[6,32,512]{2,1,0:T(8,128)(2,1)S(1)}, u32[]{:S(2)}, u32[]{:S(2)}) %collective-permute-start.4) | collective-permute-done | bytes 196640 | tf_op jit(solution)/shard_map/ppermute | solution.py:547
  48.7 6.7 %shard_map.115 = (f32[6,32,512]{2,1,0:T(8,128)S(1)}, f32[5,8,512]{2,1,0:T(8,128)}, f32[5,8,512]{2,1,0:T(8,128)}, f32[64,1,128]{2,1,0:T(1,128)S(1)}) custom-call(s32[128,2]{1,0:T(8,128)S(1)} %bitcast.27, s32[128,2]{1,0:T(8,128)S(1)} %bitcast.29, bf16[6,32,512]{2,1,0:T(8,128)(2,1)S(1)} %copy-done.22, bf16[32,128,128]{2,1,0:T(8,128)(2,1)S(1)} %bitcast.22, ...), custom_call_target="tpu_custom_call" | custom-call | tf_op jit(solution)/shard_map/pallas_call | solution.py:591
  55.4 4.8 %collective-permute-start.6 = (f32[5,8,512]{2,1,0:T(8,128)}, f32[5,8,512]{2,1,0:T(8,128)}, u32[]{:S(2)}, u32[]{:S(2)}) collective-permute-start(f32[5,8,512]{2,1,0:T(8,128)} %get-tuple-element.31), channel_id=1, source_target_pairs={{0,60},{4,0},{8,4},{12,8},{16,12},{20,16},{24,20},{28,24},{32,28},... | collective-permute-start | bytes 245768 | tf_op jit(solution)/shard_map/ppermute | solution.py:543
  60.2 6.2 %all-to-all-start = ((f32[64,1,128]{2,1,0:T(1,128)}), f32[64,1,128]{2,1,0:T(1,128)}, u32[]{:S(2)}, u32[]{:S(2)}) async-start(f32[64,1,128]{2,1,0:T(1,128)} %copy-done.29), calls=%async_computation | async-start | bytes 65536 | tf_op jit(solution)/shard_map/all_to_all | solution.py:608
  66.5 1.6 %shard_map.116 = (f32[48,128]{1,0:T(8,128)}, f32[48,128]{1,0:T(8,128)}) custom-call(f32[6,32,512]{2,1,0:T(8,128)S(1)} %get-tuple-element.29.out.regridded, f32[5,8,512]{2,1,0:T(8,128)S(1)} %collective-permute-done.5.upper, f32[5,8,512]{2,1,0:T(8,128)} %collective-permute-done.6.lower), custom_call_target="tpu_custom_call" | custom-call | tf_op jit(solution)/shard_map/pallas_call | solution.py:610
  68.7 1.2 collective-permute-start.8
  69.9 4.5 %all-to-all-done.gap = f32[64,1,128]{2,1,0:T(1,128)} async-done(((f32[64,1,128]{2,1,0:T(1,128)}), f32[64,1,128]{2,1,0:T(1,128)}, u32[]{:S(2)}, u32[]{:S(2)}) %all-to-all-start) | async-done | bytes 32800 | tf_op jit(solution)/shard_map/all_to_all | solution.py:608
  75.1 1.1 copy-done.3
  79.2 4.1 %shard_map.117 = (bf16[6,32,512]{2,1,0:T(8,128)(2,1)S(1)}, f32[32,512]{1,0:T(8,128)S(1)}, f32[3,48,640]{2,1,0:T(8,128)S(1)}, f32[3,48,640]{2,1,0:T(8,128)S(1)}) custom-call(f32[16]{0:T(128)S(1)} %bitcast.34, f32[15]{0:T(128)S(1)} %bitcast.38, f32[3,48,640]{2,1,0:T(8,128)S(1)} %copy-done.16, f32[6,32,512]{2,1,0:T(8,128)S(1)} %get-tuple-element.29.out.regridded, ...), custom_call_target="tpu_custom_call" | custom-call | tf_op jit(solution)/shard_map/pallas_call | solution.py:613
  84.0 2.9 %collective-permute-start.9 = (bf16[6,32,512]{2,1,0:T(8,128)(2,1)S(1)}, bf16[6,32,512]{2,1,0:T(8,128)(2,1)S(1)}, u32[]{:S(2)}, u32[]{:S(2)}) collective-permute-start(bf16[6,32,512]{2,1,0:T(8,128)(2,1)S(1)} %get-tuple-element.45), channel_id=1, source_target_pairs={{0,64},{64,0},{1,65},{65,1},{2,66},{66,2},{3,67},{67,3},{4,68},{68... | collective-permute-start | bytes 589832 | tf_op jit(solution)/shard_map/ppermute | solution.py:547
  87.0 4.5 %collective-permute-done.9.received = bf16[6,32,512]{2,1,0:T(8,128)(2,1)S(1)} collective-permute-done((bf16[6,32,512]{2,1,0:T(8,128)(2,1)S(1)}, bf16[6,32,512]{2,1,0:T(8,128)(2,1)S(1)}, u32[]{:S(2)}, u32[]{:S(2)}) %collective-permute-start.9) | collective-permute-done | bytes 196640 | tf_op jit(solution)/shard_map/ppermute | solution.py:547
  91.4 6.8 %shard_map.120 = (f32[6,32,512]{2,1,0:T(8,128)S(1)}, f32[5,8,512]{2,1,0:T(8,128)}, f32[5,8,512]{2,1,0:T(8,128)}, f32[64,1,128]{2,1,0:T(1,128)}) custom-call(s32[128,2]{1,0:T(8,128)S(1)} %bitcast.28, s32[128,2]{1,0:T(8,128)S(1)} %bitcast.30, bf16[6,32,512]{2,1,0:T(8,128)(2,1)S(1)} %collective-permute-done.9.received, bf16[32,128,128]{2,1,0:T(8,128)(2,1)S(1)} %bitcast.23, ...), custom_call_target="tpu_custom_call" | custom-call | tf_op jit(solution)/shard_map/pallas_call | solution.py:591
  98.2 7.8 %all-to-all-start.1 = ((f32[64,1,128]{2,1,0:T(1,128)}), f32[64,1,128]{2,1,0:T(1,128)S(1)}, u32[]{:S(2)}, u32[]{:S(2)}) async-start(f32[64,1,128]{2,1,0:T(1,128)} %get-tuple-element.47), calls=%async_computation.1 | async-start | bytes 65536 | tf_op jit(solution)/shard_map/all_to_all | solution.py:631
  109.0 8.4 %shard_map.118 = (f32[16,32,512]{2,1,0:T(8,128)}, f32[3,48,640]{2,1,0:T(8,128)S(1)}, f32[3,48,640]{2,1,0:T(8,128)S(1)}) custom-call(f32[16]{0:T(128)S(1)} %bitcast.35, f32[15]{0:T(128)S(1)} %bitcast.39, f32[16,32,512]{2,1,0:T(8,128)S(1)} %bitcast.21, f32[24,8,512]{2,1,0:T(8,128)S(1)} %collective-permute-done.upper, ...), custom_call_target="tpu_custom_call" | custom-call | tf_op jit(solution)/shard_map/pallas_call | solution.py:599
  117.4 2.4 %shard_map.119 = f32[16,32,512]{2,1,0:T(8,128)} custom-call(f32[16]{0:T(128)S(1)} %bitcast.36, f32[15]{0:T(128)S(1)} %bitcast.40, f32[3,48,640]{2,1,0:T(8,128)S(1)} %copy-done.18, f32[3,48,640]{2,1,0:T(8,128)S(1)} %copy-done.20, f32[3,48,640]{2,1,0:T(8,128)S(1)} %get-tuple-element.41.hs, ...), custom_call_target="tpu_custom_call", output_to_operand_aliasing={{}: (7, {})} | custom-call | tf_op jit(solution)/shard_map/pallas_call | solution.py:620
  (92 shorter events, 17.4 us)
Async XLA Ops:
  0.6 22.8 %copy-start = (f32[1,16,32,512]{3,2,1,0:T(8,128)S(1)}, f32[1,16,32,512]{3,2,1,0:T(8,128)}, u32[]{:S(2)}) copy-start(f32[1,16,32,512]{3,2,1,0:T(8,128)} %param.10) | copy-start | bytes 3145732
  2.6 20.8 %copy-start.6 = (bf16[1,6,32,512]{3,2,1,0:T(8,128)(2,1)S(1)}, bf16[1,6,32,512]{3,2,1,0:T(8,128)(2,1)}, u32[]{:S(2)}) copy-start(bf16[1,6,32,512]{3,2,1,0:T(8,128)(2,1)} %param.11) | copy-start | bytes 589828
  2.7 20.7 %copy-start.9 = (f32[1,32,512]{2,1,0:T(8,128)S(1)}, f32[1,32,512]{2,1,0:T(8,128)}, u32[]{:S(2)}) copy-start(f32[1,32,512]{2,1,0:T(8,128)} %param.14) | copy-start | bytes 196612
  3.5 14.6 %collective-permute-start.1 = (f32[24,8,512]{2,1,0:T(8,128)S(1)}, f32[24,8,512]{2,1,0:T(8,128)S(1)}, u32[]{:S(2)}, u32[]{:S(2)}) collective-permute-start(f32[24,8,512]{2,1,0:T(8,128)S(1)} %get-tuple-element.50), channel_id=1, source_target_pairs={{0,60},{4,0},{8,4},{12,8},{16,12},{20,16},{24,20},{28,24},{32,28},... | collective-permute-start | bytes 1179656 | tf_op jit(solution)/shard_map/ppermute | solution.py:543
  10.4 13.0 %collective-permute-start = (f32[24,8,512]{2,1,0:T(8,128)S(1)}, f32[24,8,512]{2,1,0:T(8,128)S(1)}, u32[]{:S(2)}, u32[]{:S(2)}) collective-permute-start(f32[24,8,512]{2,1,0:T(8,128)S(1)} %get-tuple-element.51), channel_id=1, source_target_pairs={{0,4},{4,8},{8,12},{12,16},{16,20},{20,24},{24,28},{28,32},{32,36}... | collective-permute-start | bytes 1179656 | tf_op jit(solution)/shard_map/ppermute | solution.py:543
  23.7 3.2 %collective-permute-start.2 = (f32[48,256]{1,0:T(8,128)S(1)}, f32[48,256]{1,0:T(8,128)S(1)}, u32[]{:S(2)}, u32[]{:S(2)}) collective-permute-start(f32[48,256]{1,0:T(8,128)S(1)} %get-tuple-element.25), channel_id=1, source_target_pairs={{0,1},{1,0},{2,3},{3,2},{4,5},{5,4},{6,7},{7,6},{8,9},{9,8},{10,11... | collective-permute-start | bytes 147464 | tf_op jit(solution)/shard_map/ppermute | solution.py:547
  25.7 3.5 %collective-permute-start.3 = (f32[48,256]{1,0:T(8,128)S(1)}, f32[48,256]{1,0:T(8,128)S(1)}, u32[]{:S(2)}, u32[]{:S(2)}) collective-permute-start(f32[48,256]{1,0:T(8,128)S(1)} %get-tuple-element.26), channel_id=1, source_target_pairs={{0,3},{1,2},{2,1},{3,0},{4,7},{5,6},{6,5},{7,4},{8,11},{9,10},{10,... | collective-permute-start | bytes 147464 | tf_op jit(solution)/shard_map/ppermute | solution.py:547
  27.0 8.2 %copy-start.23 = (f32[48,256]{1,0:T(8,128)}, f32[48,256]{1,0:T(8,128)S(1)}, u32[]{:S(2)}) copy-start(f32[48,256]{1,0:T(8,128)S(1)} %collective-permute-done.2.one) | copy-start | bytes 147460
  29.9 12.1 %copy-start.36 = (s32[1,32,4,2]{1,3,2,0:T(2,128)S(1)}, s32[1,32,4,2]{1,3,2,0:T(2,128)}, u32[]{:S(2)}) copy-start(s32[1,32,4,2]{1,3,2,0:T(2,128)} %param.18) | copy-start | bytes 3076
  29.9 17.9 %copy-start.1 = (bf16[1,32,128,128]{3,2,1,0:T(8,128)(2,1)S(1)}, bf16[1,32,128,128]{3,2,1,0:T(8,128)(2,1)}, u32[]{:S(2)}) copy-start(bf16[1,32,128,128]{3,2,1,0:T(8,128)(2,1)} %param.17) | copy-start | bytes 3145732
  39.1 8.0 %collective-permute-start.4 = (bf16[6,32,512]{2,1,0:T(8,128)(2,1)S(1)}, bf16[6,32,512]{2,1,0:T(8,128)(2,1)S(1)}, u32[]{:S(2)}, u32[]{:S(2)}) collective-permute-start(bf16[6,32,512]{2,1,0:T(8,128)(2,1)S(1)} %get-tuple-element.28), channel_id=1, source_target_pairs={{0,64},{64,0},{1,65},{65,1},{2,66},{66,2},{3,67},{67,3},{4,68},{68... | collective-permute-start | bytes 589832 | tf_op jit(solution)/shard_map/ppermute | solution.py:547
  55.4 11.0 %collective-permute-start.5 = (f32[5,8,512]{2,1,0:T(8,128)}, f32[5,8,512]{2,1,0:T(8,128)S(1)}, u32[]{:S(2)}, u32[]{:S(2)}) collective-permute-start(f32[5,8,512]{2,1,0:T(8,128)} %get-tuple-element.30), channel_id=1, source_target_pairs={{0,4},{4,8},{8,12},{12,16},{16,20},{20,24},{24,28},{28,32},{32,36}... | collective-permute-start | bytes 245768 | tf_op jit(solution)/shard_map/ppermute | solution.py:543
  55.4 11.0 %collective-permute-start.6 = (f32[5,8,512]{2,1,0:T(8,128)}, f32[5,8,512]{2,1,0:T(8,128)}, u32[]{:S(2)}, u32[]{:S(2)}) collective-permute-start(f32[5,8,512]{2,1,0:T(8,128)} %get-tuple-element.31), channel_id=1, source_target_pairs={{0,60},{4,0},{8,4},{12,8},{16,12},{20,16},{24,20},{28,24},{32,28},... | collective-permute-start | bytes 245768 | tf_op jit(solution)/shard_map/ppermute | solution.py:543
  60.2 14.2 %all-to-all-start = ((f32[64,1,128]{2,1,0:T(1,128)}), f32[64,1,128]{2,1,0:T(1,128)}, u32[]{:S(2)}, u32[]{:S(2)}) async-start(f32[64,1,128]{2,1,0:T(1,128)} %copy-done.29), calls=%async_computation | async-start | bytes 65536 | tf_op jit(solution)/shard_map/all_to_all | solution.py:608
  68.1 6.3 %collective-permute-start.7 = (f32[48,128]{1,0:T(8,128)}, f32[48,128]{1,0:T(8,128)}, u32[]{:S(2)}, u32[]{:S(2)}) collective-permute-start(f32[48,128]{1,0:T(8,128)} %get-tuple-element.32), channel_id=1, source_target_pairs={{0,1},{1,0},{2,3},{3,2},{4,5},{5,4},{6,7},{7,6},{8,9},{9,8},{10,11... | collective-permute-start | bytes 73736 | tf_op jit(solution)/shard_map/ppermute | solution.py:547
  68.7 5.7 %collective-permute-start.8 = (f32[48,128]{1,0:T(8,128)}, f32[48,128]{1,0:T(8,128)}, u32[]{:S(2)}, u32[]{:S(2)}) collective-permute-start(f32[48,128]{1,0:T(8,128)} %get-tuple-element.33), channel_id=1, source_target_pairs={{0,3},{1,2},{2,1},{3,0},{4,7},{5,6},{6,5},{7,4},{8,11},{9,10},{10,... | collective-permute-start | bytes 73736 | tf_op jit(solution)/shard_map/ppermute | solution.py:547
  84.0 14.2 %copy-start.17 = (f32[3,48,640]{2,1,0:T(8,128)}, f32[3,48,640]{2,1,0:T(8,128)S(1)}, u32[]{:S(2)}) copy-start(f32[3,48,640]{2,1,0:T(8,128)S(1)} %get-tuple-element.38.hx) | copy-start | bytes 1105924
  84.0 14.2 %copy-start.27 = (f32[32,512]{1,0:T(8,128)}, f32[32,512]{1,0:T(8,128)S(1)}, u32[]{:S(2)}) copy-start(f32[32,512]{1,0:T(8,128)S(1)} %get-tuple-element.43.final0) | copy-start | bytes 196612
  84.0 7.4 %collective-permute-start.9 = (bf16[6,32,512]{2,1,0:T(8,128)(2,1)S(1)}, bf16[6,32,512]{2,1,0:T(8,128)(2,1)S(1)}, u32[]{:S(2)}, u32[]{:S(2)}) collective-permute-start(bf16[6,32,512]{2,1,0:T(8,128)(2,1)S(1)} %get-tuple-element.45), channel_id=1, source_target_pairs={{0,64},{64,0},{1,65},{65,1},{2,66},{66,2},{3,67},{67,3},{4,68},{68... | collective-permute-start | bytes 589832 | tf_op jit(solution)/shard_map/ppermute | solution.py:547
  91.4 14.7 %copy-start.26 = (f32[48,256]{1,0:T(8,128)S(1)}, f32[48,256]{1,0:T(8,128)}, u32[]{:S(2)}) copy-start(f32[48,256]{1,0:T(8,128)} %copy-done.25) | copy-start | bytes 147460
  98.2 21.5 %all-to-all-start.1 = ((f32[64,1,128]{2,1,0:T(1,128)}), f32[64,1,128]{2,1,0:T(1,128)S(1)}, u32[]{:S(2)}, u32[]{:S(2)}) async-start(f32[64,1,128]{2,1,0:T(1,128)} %get-tuple-element.47), calls=%async_computation.1 | async-start | bytes 65536 | tf_op jit(solution)/shard_map/all_to_all | solution.py:631
  109.0 8.5 %copy-start.18 = (f32[3,48,640]{2,1,0:T(8,128)S(1)}, f32[3,48,640]{2,1,0:T(8,128)}, u32[]{:S(2)}) copy-start(f32[3,48,640]{2,1,0:T(8,128)} %copy-done.17) | copy-start | bytes 1105924
  109.0 8.5 %copy-start.20 = (f32[3,48,640]{2,1,0:T(8,128)S(1)}, f32[3,48,640]{2,1,0:T(8,128)}, u32[]{:S(2)}) copy-start(f32[3,48,640]{2,1,0:T(8,128)} %copy-done.19) | copy-start | bytes 1105924
  109.0 8.5 %copy-start.28 = (f32[32,512]{1,0:T(8,128)S(1)}, f32[32,512]{1,0:T(8,128)}, u32[]{:S(2)}) copy-start(f32[32,512]{1,0:T(8,128)} %copy-done.27) | copy-start | bytes 196612
  (26 other events, 39.9 us)

commit v2 on v1

--- a/solution.py
+++ b/solution.py
@@ -18,7 +18,7 @@
 BAND = CX + 16
 PATTERNS = 32
 BLOCKS = CX * OWN_TILES
-VMEM_LIMIT = 48 * 1024 * 1024
+VMEM_LIMIT = 10 * 1024 * 1024
 
 N_FIELDS = LEVELS + 3 + SUB - 1
 AT_COUPLING, AT_LAND, AT_MASK, AT_GUESS = LEVELS, LEVELS + 1, LEVELS + 2, LEVELS + 3
@@ -309,9 +309,10 @@
 
 def first_rest(
     diff, mix, state, upper, lower, one, three, hd, ud,
-    final, hs, us,
+    final, hs, us, token,
     s0, s1,
 ):
+    token[...] = jnp.zeros_like(token)
     even, first, last = position()
     zero_pads(s0, LEVELS)
     zero_pads(s1, LEVELS)
@@ -353,10 +354,11 @@
 
 
 def regrid(
-    src, pat, received, weights, mask,
+    src, pat, received, weights, mask, before,
     out, top, bottom, gap,
     x, y,
 ):
+    del before
     partial = [jnp.zeros((8, LANES), F32) for _ in range(SUB)]
     wet = jnp.zeros((8, LANES), F32)
     for half in range(CX // 16):
@@ -494,10 +496,11 @@
 
 def second_rest(
     diff, mix, hx, ux, hs, us, final0, whole,
-    final,
+    final, token,
     s0, s1,
 ):
     del whole
+    token[...] = jnp.zeros_like(token)
     gy = lax.axis_index("gy")
     first, last = gy == 0, gy == lax.axis_size("gy") - 1
     zero_pads(s0, SUB)
@@ -585,25 +588,25 @@
         [SM, SM] + [VM] * 9,
     )(diff, mix, state, guess, coupling, land_temp, land_mask, upper, lower, one, three)
 
-    def exchange(series):
+    def exchange(series, before):
         received = paired(series, "comp", 1)
         edges = shape(SUB - 1, 8, CY)
         out, top, bottom, gap = call(
             regrid,
             [shape(SUB, CX, CY), edges, edges, shape(peers, 1, LANES)],
             [pltpu.VMEM((BLOCKS * 8, LANES), F32), pltpu.VMEM((BLOCKS * 8, LANES), F32)],
-            [SM, SM, VM, VM, VM],
-        )(src, pat, received, weights, land_mask)
+            [SM, SM, VM, VM, VM, VM],
+        )(src, pat, received, weights, land_mask, before)
         return out, top, bottom, gap
 
-    whole, hs_rest, us_rest = call(
+    whole, hs_rest, us_rest, token = call(
         first_rest,
-        [shape(LEVELS, CX, CY), band(3), band(3)],
+        [shape(LEVELS, CX, CY), band(3), band(3), shape(8, LANES)],
         [field_buf(LEVELS), field_buf(LEVELS)],
         [SM, SM] + [VM] * 7,
     )(diff, mix, state, upper, lower, one, three, hd, ud)
 
-    out, top, bottom, gap = exchange(series)
+    out, top, bottom, gap = exchange(series, token)
     lower, upper = shifted(top, "gx", -1), shifted(bottom, "gx", 1)
     gap = lax.all_to_all(gap, ("gx", "gy"), 0, 0)
     packed = shape(BAND, LANES)
@@ -617,17 +620,17 @@
         [SM, SM] + [VM] * 10,
     )(diff, mix, fixed, out, upper, lower, one, three, gap, hs, hd, us)
 
-    (whole,) = call(
+    whole, token = call(
         second_rest,
-        [shape(LEVELS, CX, CY)],
+        [shape(LEVELS, CX, CY), shape(8, LANES)],
         [field_buf(SUB), field_buf(SUB)],
         [SM, SM] + [VM] * 5 + [pl.BlockSpec(memory_space=pl.ANY)],
-        out_specs=[pl.BlockSpec((SUB, CX, CY), lambda i: (0, 0, 0))],
+        out_specs=[pl.BlockSpec((SUB, CX, CY), lambda i: (0, 0, 0)), VM],
         grid=(1,),
         input_output_aliases={7: 0},
     )(diff, mix, hx, ux, hs_rest, us_rest, final0, whole)
 
-    out, _, _, gap = exchange(series)
+    out, _, _, gap = exchange(series, token)
     gap = lax.all_to_all(gap, ("gx", "gy"), 0, 0)
     (forcing,) = call(finish, [shape(SUB, CX, CY)], [], [VM] * 3)(out, land_mask, gap)
     return whole[None], forcing[None]

time: 121 us -> 108 us (0.89)
  blocking collectives: 0 us -> 13.8 us
  starting transfers between devices: 36.5 us -> 25.3 us
  waiting for transfers between devices: 29 us -> 20.4 us
  local copies, waits for them, and re-layouts: 16.9 us -> 11.1 us
    all_to_all x0 -> x1, blocking collectives: none -> 13.8 us  [per_device(): gap = lax.all_to_all(gap, ('gx', 'gy'), 0, 0)]
    all_to_all x2 -> x1, starting transfers between devices: 14 us -> 4.73 us  [per_device(): gap = lax.all_to_all(gap, ('gx', 'gy'), 0, 0)]
    unnamed x81 -> x51, local copies, waits for them, and re-layouts: 16.9 us -> 11.1 us
    ppermute x6, waiting for transfers between devices: 11.5 us -> 5.81 us  [paired(): lax.ppermute(value, axis, [(i, i ^ mask) for i in range(lax.axis_size(axi...]
    ppermute x4, waiting for transfers between devices: 13 us -> 8.77 us  [shifted(): return lax.ppermute(value, axis, [(i, (i + by) % n) for i in range(n)])]
    ppermute x6, starting transfers between devices: 10.9 us -> 8.71 us  [paired(): lax.ppermute(value, axis, [(i, i ^ mask) for i in range(lax.axis_size(axi...]
    pallas_call x1, Pallas kernels: 1.63 us -> 0.12 us  [per_device(): call(pack_second, [packed, packed], [], [VM] * 3)(out, upper, lower)]
    all_to_all x2 -> x1, waiting for transfers between devices: 4.5 us -> 5.79 us  [per_device(): gap = lax.all_to_all(gap, ('gx', 'gy'), 0, 0)]
  transfers between devices with their start and end apart: 12 -> 11, of which waited for: 6 -> 4; matrix products, arithmetic and copies ran while one was open for 0% -> 0% of each run, Pallas kernels for 10% -> 10%
where the time goes in v2:
time: 108 us
  Pallas kernels  35.4 us (33%)
  starting transfers between devices  25.3 us (23%)
  waiting for transfers between devices  20.4 us (19%)
  blocking collectives  13.8 us (13%)
  local copies, waits for them, and re-layouts  11.1 us (10%)
    all_to_all x1, blocking collectives, per_device(): gap = lax.all_to_all(gap, ('gx', 'gy'), 0, 0)  13.8 us
    pallas_call x2, Pallas kernels, exchange(): call(regrid, [shape(SUB, CX, CY), edges, edges, shape(peers, 1, LANES)],...  13.6 us
    ppermute x4, starting transfers between devices, shifted(): return lax.ppermute(value, axis, [(i, (i + by) % n) for i in range(n)])  11.8 us
    unnamed x51, local copies, waits for them, and re-layouts  11.1 us
    ppermute x4, waiting for transfers between devices, shifted(): return lax.ppermute(value, axis, [(i, (i + by) % n) for i in range(n)])  8.77 us
    ppermute x6, starting transfers between devices, paired(): lax.ppermute(value, axis, [(i, i ^ mask) for i in range(lax.axis_size(axi...  8.71 us
    pallas_call x1, Pallas kernels, per_device(): call(first_rest, [shape(LEVELS, CX, CY), band(3), band(3), shape(8, LANES...  8.45 us
    pallas_call x1, Pallas kernels, per_device(): call(first_cone, [shape(SUB, CX, CY, dtype=BF16), band(SUB), band(SUB), b...  5.88 us
  transfers between devices with their start and end apart: 11, of which 4 were waited for; matrix products, arithmetic and copies ran while one was open for 0% of the time, Pallas kernels for 10%

profile of v2, /device:TPU:1, one launch (start us, length us, event | category | flops | bytes accessed | tf_op | source)
XLA Modules:
  0.0 107.6 jit_solution(13867762193583731615)
XLA Ops:
  0.6 1.2 %slice_dynamic-update-slice_fusion = (f32[24,8,512]{2,1,0:T(8,128)S(1)}, f32[24,8,512]{2,1,0:T(8,128)S(1)}) fusion(f32[16,32,512]{2,1,0:T(8,128)} %bitcast.18), kind=kLoop, calls=%fused_computation | loop fusion | bytes 1048576
  3.5 2.1 %collective-permute-start = (f32[24,8,512]{2,1,0:T(8,128)S(1)}, f32[24,8,512]{2,1,0:T(8,128)S(1)}, u32[]{:S(2)}, u32[]{:S(2)}) collective-permute-start(f32[24,8,512]{2,1,0:T(8,128)S(1)} %get-tuple-element.57), channel_id=1, source_target_pairs={{0,4},{4,8},{8,12},{12,16},{16,20},{20,24},{24,28},{28,32},{32,36}... | collective-permute-start | bytes 1179656 | tf_op jit(solution)/shard_map/ppermute | solution.py:546
  5.7 4.8 %collective-permute-start.1 = (f32[24,8,512]{2,1,0:T(8,128)S(1)}, f32[24,8,512]{2,1,0:T(8,128)S(1)}, u32[]{:S(2)}, u32[]{:S(2)}) collective-permute-start(f32[24,8,512]{2,1,0:T(8,128)S(1)} %get-tuple-element.56), channel_id=1, source_target_pairs={{0,60},{4,0},{8,4},{12,8},{16,12},{20,16},{24,20},{28,24},{32,28},... | collective-permute-start | bytes 1179656 | tf_op jit(solution)/shard_map/ppermute | solution.py:546
  10.5 8.8 %collective-permute-done.upper = f32[24,8,512]{2,1,0:T(8,128)S(1)} collective-permute-done((f32[24,8,512]{2,1,0:T(8,128)S(1)}, f32[24,8,512]{2,1,0:T(8,128)S(1)}, u32[]{:S(2)}, u32[]{:S(2)}) %collective-permute-start) | collective-permute-done | bytes 393248 | tf_op jit(solution)/shard_map/ppermute | solution.py:546
  19.6 1.3 %collective-permute-start.2 = (f32[48,256]{1,0:T(8,128)S(1)}, f32[48,256]{1,0:T(8,128)S(1)}, u32[]{:S(2)}, u32[]{:S(2)}) collective-permute-start(f32[48,256]{1,0:T(8,128)S(1)} %get-tuple-element.28), channel_id=1, source_target_pairs={{0,1},{1,0},{2,3},{3,2},{4,5},{5,4},{6,7},{7,6},{8,9},{9,8},{10,11... | collective-permute-start | bytes 147464 | tf_op jit(solution)/shard_map/ppermute | solution.py:550
  20.9 1.3 %collective-permute-start.3 = (f32[48,256]{1,0:T(8,128)S(1)}, f32[48,256]{1,0:T(8,128)S(1)}, u32[]{:S(2)}, u32[]{:S(2)}) collective-permute-start(f32[48,256]{1,0:T(8,128)S(1)} %get-tuple-element.29), channel_id=1, source_target_pairs={{0,3},{1,2},{2,1},{3,0},{4,7},{5,6},{6,5},{7,4},{8,11},{9,10},{10,... | collective-permute-start | bytes 147464 | tf_op jit(solution)/shard_map/ppermute | solution.py:550
  22.2 2.3 %collective-permute-done.3.three = f32[48,256]{1,0:T(8,128)S(1)} collective-permute-done((f32[48,256]{1,0:T(8,128)S(1)}, f32[48,256]{1,0:T(8,128)S(1)}, u32[]{:S(2)}, u32[]{:S(2)}) %collective-permute-start.3) | collective-permute-done | bytes 49184 | tf_op jit(solution)/shard_map/ppermute | solution.py:550
  25.1 5.9 %shard_map.114 = (bf16[6,32,512]{2,1,0:T(8,128)(2,1)}, f32[6,48,640]{2,1,0:T(8,128)S(1)}, f32[6,48,640]{2,1,0:T(8,128)S(1)}, f32[3,48,640]{2,1,0:T(8,128)S(1)}, ...) custom-call(f32[16]{0:T(128)S(1)} %bitcast.33, f32[15]{0:T(128)S(1)} %bitcast.37, f32[16,32,512]{2,1,0:T(8,128)S(1)} %bitcast.20, ...), custom_call_target="tpu_custom_call" | custom-call | tf_op jit(solution)/shard_map/pallas_call | solution.py:584
  35.0 2.9 %collective-permute-start.4 = (bf16[6,32,512]{2,1,0:T(8,128)(2,1)}, bf16[6,32,512]{2,1,0:T(8,128)(2,1)}, u32[]{:S(2)}, u32[]{:S(2)}) collective-permute-start(bf16[6,32,512]{2,1,0:T(8,128)(2,1)} %get-tuple-element.31), channel_id=1, source_target_pairs={{0,64},{64,0},{1,65},{65,1},{2,66},{66,2},{3,67},{67,3},{4,68},{68... | collective-permute-start | bytes 589832 | tf_op jit(solution)/shard_map/ppermute | solution.py:550
  38.1 1.1 %copy-done.3 = f32[6,48,640]{2,1,0:T(8,128)S(1)} copy-done((f32[6,48,640]{2,1,0:T(8,128)S(1)}, f32[6,48,640]{2,1,0:T(8,128)}, u32[]{:S(2)}) %copy-start.3) | copy-done | bytes 737304
  39.3 1.1 %copy-done.8 = f32[6,48,640]{2,1,0:T(8,128)S(1)} copy-done((f32[6,48,640]{2,1,0:T(8,128)S(1)}, f32[6,48,640]{2,1,0:T(8,128)}, u32[]{:S(2)}) %copy-start.8) | copy-done | bytes 737304
  40.4 8.4 %shard_map.115 = (f32[16,32,512]{2,1,0:T(8,128)}, f32[3,48,640]{2,1,0:T(8,128)S(1)}, f32[3,48,640]{2,1,0:T(8,128)S(1)}, f32[8,128]{1,0:T(8,128)S(1)}) custom-call(f32[16]{0:T(128)S(1)} %bitcast.34, f32[15]{0:T(128)S(1)} %bitcast.38, f32[16,32,512]{2,1,0:T(8,128)S(1)} %bitcast.21, f32[24,8,512]{2,1,0:T(8,128)S(1)} %collective-permute-done.upper, ...), custom_call_target="tpu_custom_call" | custom-call | tf_op jit(solution)/shard_map/pallas_call | solution.py:602
  48.8 6.8 %shard_map.116 = (f32[6,32,512]{2,1,0:T(8,128)S(1)}, f32[5,8,512]{2,1,0:T(8,128)S(1)}, f32[5,8,512]{2,1,0:T(8,128)S(1)}, f32[64,1,128]{2,1,0:T(1,128)}) custom-call(s32[128,2]{1,0:T(8,128)S(1)} %bitcast.29, s32[128,2]{1,0:T(8,128)S(1)} %bitcast.27, bf16[6,32,512]{2,1,0:T(8,128)(2,1)} %collective-permute-done.4.received, bf16[32,128,128]{2,1,0:T(8,128)(2,1)S(1)} %bitcast.22, ...), custom_call_target="tpu_custom_call" | custom-call | tf_op jit(solution)/shard_map/pallas_call | solution.py:594
  55.7 4.9 %collective-permute-start.6 = (f32[5,8,512]{2,1,0:T(8,128)S(1)}, f32[5,8,512]{2,1,0:T(8,128)S(1)}, u32[]{:S(2)}, u32[]{:S(2)}) collective-permute-start(f32[5,8,512]{2,1,0:T(8,128)S(1)} %get-tuple-element.37), channel_id=1, source_target_pairs={{0,60},{4,0},{8,4},{12,8},{16,12},{20,16},{24,20},{28,24},{32,28},... | collective-permute-start | bytes 245768 | tf_op jit(solution)/shard_map/ppermute | solution.py:546
  60.6 4.7 %all-to-all-start = ((f32[64,1,128]{2,1,0:T(1,128)}), f32[64,1,128]{2,1,0:T(1,128)S(1)}, u32[]{:S(2)}, u32[]{:S(2)}) async-start(f32[64,1,128]{2,1,0:T(1,128)} %get-tuple-element.40), calls=%async_computation | async-start | bytes 65536 | tf_op jit(solution)/shard_map/all_to_all | solution.py:611
  66.1 1.2 %collective-permute-start.8 = (f32[48,128]{1,0:T(8,128)S(1)}, f32[48,128]{1,0:T(8,128)S(1)}, u32[]{:S(2)}, u32[]{:S(2)}) collective-permute-start(f32[48,128]{1,0:T(8,128)S(1)} %get-tuple-element.39), channel_id=1, source_target_pairs={{0,3},{1,2},{2,1},{3,0},{4,7},{5,6},{6,5},{7,4},{8,11},{9,10},{10,... | collective-permute-start | bytes 73736 | tf_op jit(solution)/shard_map/ppermute | solution.py:550
  67.4 5.8 %all-to-all-done.gap = f32[64,1,128]{2,1,0:T(1,128)S(1)} async-done(((f32[64,1,128]{2,1,0:T(1,128)}), f32[64,1,128]{2,1,0:T(1,128)S(1)}, u32[]{:S(2)}, u32[]{:S(2)}) %all-to-all-start) | async-done | bytes 32800 | tf_op jit(solution)/shard_map/all_to_all | solution.py:611
  74.2 1.0 copy-done.18
  75.2 3.8 %shard_map.118 = (bf16[6,32,512]{2,1,0:T(8,128)(2,1)S(1)}, f32[32,512]{1,0:T(8,128)S(1)}, f32[3,48,640]{2,1,0:T(8,128)S(1)}, f32[3,48,640]{2,1,0:T(8,128)S(1)}) custom-call(f32[16]{0:T(128)S(1)} %bitcast.35, f32[15]{0:T(128)S(1)} %bitcast.39, f32[3,48,640]{2,1,0:T(8,128)S(1)} %copy-done.18, f32[6,32,512]{2,1,0:T(8,128)S(1)} %get-tuple-element.35.out.regridded, ...), custom_call_target="tpu_custom_call" | custom-call | tf_op jit(solution)/shard_map/pallas_call | solution.py:616
  78.9 1.3 %collective-permute-start.9 = (bf16[6,32,512]{2,1,0:T(8,128)(2,1)S(1)}, bf16[6,32,512]{2,1,0:T(8,128)(2,1)S(1)}, u32[]{:S(2)}, u32[]{:S(2)}) collective-permute-start(bf16[6,32,512]{2,1,0:T(8,128)(2,1)S(1)} %get-tuple-element.50), channel_id=1, source_target_pairs={{0,64},{64,0},{1,65},{65,1},{2,66},{66,2},{3,67},{67,3},{4,68},{68... | collective-permute-start | bytes 589832 | tf_op jit(solution)/shard_map/ppermute | solution.py:550
  80.3 2.4 %shard_map.119 = (f32[16,32,512]{2,1,0:T(8,128)}, f32[8,128]{1,0:T(8,128)S(1)}) custom-call(f32[16]{0:T(128)S(1)} %bitcast.36, f32[15]{0:T(128)S(1)} %bitcast.40, f32[3,48,640]{2,1,0:T(8,128)S(1)} %get-tuple-element.43.hx, f32[3,48,640]{2,1,0:T(8,128)S(1)} %get-tuple-element.44.ux, ...), custom_call_target="tpu_custom_call", output_to_operand_aliasing={{0}: (7, {})} | custom-call | tf_op jit(solution)/shard_map/pallas_call | solution.py:623
  82.6 3.5 %collective-permute-done.9.received = bf16[6,32,512]{2,1,0:T(8,128)(2,1)S(1)} collective-permute-done((bf16[6,32,512]{2,1,0:T(8,128)(2,1)S(1)}, bf16[6,32,512]{2,1,0:T(8,128)(2,1)S(1)}, u32[]{:S(2)}, u32[]{:S(2)}) %collective-permute-start.9) | collective-permute-done | bytes 196640 | tf_op jit(solution)/shard_map/ppermute | solution.py:550
  86.2 6.7 %shard_map.120 = (f32[6,32,512]{2,1,0:T(8,128)S(1)}, f32[5,8,512]{2,1,0:T(8,128)}, f32[5,8,512]{2,1,0:T(8,128)}, f32[64,1,128]{2,1,0:T(1,128)S(1)}) custom-call(s32[128,2]{1,0:T(8,128)S(1)} %bitcast.30, s32[128,2]{1,0:T(8,128)S(1)} %bitcast.28, bf16[6,32,512]{2,1,0:T(8,128)(2,1)S(1)} %collective-permute-done.9.received, bf16[32,128,128]{2,1,0:T(8,128)(2,1)S(1)} %bitcast.23, ...), custom_call_target="tpu_custom_call" | custom-call | tf_op jit(solution)/shard_map/pallas_call | solution.py:594
  92.9 13.8 %all_to_all.10.gap = f32[64,1,128]{2,1,0:T(1,128)S(1)} all-to-all(f32[64,1,128]{2,1,0:T(1,128)S(1)} %get-tuple-element.53), channel_id=1, replica_groups=mesh['comp'=2,'gx'=16,'gy'=4] {'gx','gy'}, dimensions={0} | all-to-all | bytes 65536 | tf_op jit(solution)/shard_map/all_to_all | solution.py:634
  (61 shorter events, 9.7 us)
Async XLA Ops:
  0.6 18.6 %copy-start = (f32[1,16,32,512]{3,2,1,0:T(8,128)S(1)}, f32[1,16,32,512]{3,2,1,0:T(8,128)}, u32[]{:S(2)}) copy-start(f32[1,16,32,512]{3,2,1,0:T(8,128)} %param.10) | copy-start | bytes 3145732
  2.6 16.6 %copy-start.6 = (bf16[1,6,32,512]{3,2,1,0:T(8,128)(2,1)S(1)}, bf16[1,6,32,512]{3,2,1,0:T(8,128)(2,1)}, u32[]{:S(2)}) copy-start(bf16[1,6,32,512]{3,2,1,0:T(8,128)(2,1)} %param.11) | copy-start | bytes 589828
  2.7 16.6 %copy-start.9 = (f32[1,32,512]{2,1,0:T(8,128)S(1)}, f32[1,32,512]{2,1,0:T(8,128)}, u32[]{:S(2)}) copy-start(f32[1,32,512]{2,1,0:T(8,128)} %param.14) | copy-start | bytes 196612
  3.5 15.7 %collective-permute-start = (f32[24,8,512]{2,1,0:T(8,128)S(1)}, f32[24,8,512]{2,1,0:T(8,128)S(1)}, u32[]{:S(2)}, u32[]{:S(2)}) collective-permute-start(f32[24,8,512]{2,1,0:T(8,128)S(1)} %get-tuple-element.57), channel_id=1, source_target_pairs={{0,4},{4,8},{8,12},{12,16},{16,20},{20,24},{24,28},{28,32},{32,36}... | collective-permute-start | bytes 1179656 | tf_op jit(solution)/shard_map/ppermute | solution.py:546
  5.7 13.6 %collective-permute-start.1 = (f32[24,8,512]{2,1,0:T(8,128)S(1)}, f32[24,8,512]{2,1,0:T(8,128)S(1)}, u32[]{:S(2)}, u32[]{:S(2)}) collective-permute-start(f32[24,8,512]{2,1,0:T(8,128)S(1)} %get-tuple-element.56), channel_id=1, source_target_pairs={{0,60},{4,0},{8,4},{12,8},{16,12},{20,16},{24,20},{28,24},{32,28},... | collective-permute-start | bytes 1179656 | tf_op jit(solution)/shard_map/ppermute | solution.py:546
  19.6 2.6 %collective-permute-start.2 = (f32[48,256]{1,0:T(8,128)S(1)}, f32[48,256]{1,0:T(8,128)S(1)}, u32[]{:S(2)}, u32[]{:S(2)}) collective-permute-start(f32[48,256]{1,0:T(8,128)S(1)} %get-tuple-element.28), channel_id=1, source_target_pairs={{0,1},{1,0},{2,3},{3,2},{4,5},{5,4},{6,7},{7,6},{8,9},{9,8},{10,11... | collective-permute-start | bytes 147464 | tf_op jit(solution)/shard_map/ppermute | solution.py:550
  20.9 3.5 %collective-permute-start.3 = (f32[48,256]{1,0:T(8,128)S(1)}, f32[48,256]{1,0:T(8,128)S(1)}, u32[]{:S(2)}, u32[]{:S(2)}) collective-permute-start(f32[48,256]{1,0:T(8,128)S(1)} %get-tuple-element.29), channel_id=1, source_target_pairs={{0,3},{1,2},{2,1},{3,0},{4,7},{5,6},{6,5},{7,4},{8,11},{9,10},{10,... | collective-permute-start | bytes 147464 | tf_op jit(solution)/shard_map/ppermute | solution.py:550
  25.1 12.8 %copy-start.21 = (s32[1,32,4,2]{1,3,2,0:T(2,128)S(1)}, s32[1,32,4,2]{1,3,2,0:T(2,128)}, u32[]{:S(2)}) copy-start(s32[1,32,4,2]{1,3,2,0:T(2,128)} %param.19) | copy-start | bytes 3076
  35.0 3.0 %copy-start.22 = (s32[1,32,4,2]{1,3,2,0:T(2,128)S(1)}, s32[1,32,4,2]{1,3,2,0:T(2,128)}, u32[]{:S(2)}) copy-start(s32[1,32,4,2]{1,3,2,0:T(2,128)} %param.18) | copy-start | bytes 3076
  35.0 13.9 %collective-permute-start.4 = (bf16[6,32,512]{2,1,0:T(8,128)(2,1)}, bf16[6,32,512]{2,1,0:T(8,128)(2,1)}, u32[]{:S(2)}, u32[]{:S(2)}) collective-permute-start(bf16[6,32,512]{2,1,0:T(8,128)(2,1)} %get-tuple-element.31), channel_id=1, source_target_pairs={{0,64},{64,0},{1,65},{65,1},{2,66},{66,2},{3,67},{67,3},{4,68},{68... | collective-permute-start | bytes 589832 | tf_op jit(solution)/shard_map/ppermute | solution.py:550
  38.1 1.1 %copy-start.3 = (f32[6,48,640]{2,1,0:T(8,128)S(1)}, f32[6,48,640]{2,1,0:T(8,128)}, u32[]{:S(2)}) copy-start(f32[6,48,640]{2,1,0:T(8,128)} %copy-done.2) | copy-start | bytes 2211844
  39.3 1.1 %copy-start.8 = (f32[6,48,640]{2,1,0:T(8,128)S(1)}, f32[6,48,640]{2,1,0:T(8,128)}, u32[]{:S(2)}) copy-start(f32[6,48,640]{2,1,0:T(8,128)} %copy-done.7) | copy-start | bytes 2211844
  40.4 8.5 %copy-start.1 = (bf16[1,32,128,128]{3,2,1,0:T(8,128)(2,1)S(1)}, bf16[1,32,128,128]{3,2,1,0:T(8,128)(2,1)}, u32[]{:S(2)}) copy-start(bf16[1,32,128,128]{3,2,1,0:T(8,128)(2,1)} %param.17) | copy-start | bytes 3145732
  48.8 6.9 %copy-start.11 = (f32[3,48,640]{2,1,0:T(8,128)}, f32[3,48,640]{2,1,0:T(8,128)S(1)}, u32[]{:S(2)}) copy-start(f32[3,48,640]{2,1,0:T(8,128)S(1)} %get-tuple-element.46.us) | copy-start | bytes 1105924
  48.8 24.3 %copy-start.4 = (f32[6,48,640]{2,1,0:T(8,128)S(1)}, f32[6,48,640]{2,1,0:T(8,128)}, u32[]{:S(2)}) copy-start(f32[6,48,640]{2,1,0:T(8,128)} %copy-done.2) | copy-start | bytes 2211844
  55.7 17.5 %copy-start.14 = (f32[3,48,640]{2,1,0:T(8,128)S(1)}, f32[3,48,640]{2,1,0:T(8,128)}, u32[]{:S(2)}) copy-start(f32[3,48,640]{2,1,0:T(8,128)} %copy-done.13) | copy-start | bytes 1105924
  55.7 9.7 %collective-permute-start.5 = (f32[5,8,512]{2,1,0:T(8,128)S(1)}, f32[5,8,512]{2,1,0:T(8,128)S(1)}, u32[]{:S(2)}, u32[]{:S(2)}) collective-permute-start(f32[5,8,512]{2,1,0:T(8,128)S(1)} %get-tuple-element.36), channel_id=1, source_target_pairs={{0,4},{4,8},{8,12},{12,16},{16,20},{20,24},{24,28},{28,32},{32,36}... | collective-permute-start | bytes 245768 | tf_op jit(solution)/shard_map/ppermute | solution.py:546
  55.7 9.7 %collective-permute-start.6 = (f32[5,8,512]{2,1,0:T(8,128)S(1)}, f32[5,8,512]{2,1,0:T(8,128)S(1)}, u32[]{:S(2)}, u32[]{:S(2)}) collective-permute-start(f32[5,8,512]{2,1,0:T(8,128)S(1)} %get-tuple-element.37), channel_id=1, source_target_pairs={{0,60},{4,0},{8,4},{12,8},{16,12},{20,16},{24,20},{28,24},{32,28},... | collective-permute-start | bytes 245768 | tf_op jit(solution)/shard_map/ppermute | solution.py:546
  60.6 12.6 %all-to-all-start = ((f32[64,1,128]{2,1,0:T(1,128)}), f32[64,1,128]{2,1,0:T(1,128)S(1)}, u32[]{:S(2)}, u32[]{:S(2)}) async-start(f32[64,1,128]{2,1,0:T(1,128)} %get-tuple-element.40), calls=%async_computation | async-start | bytes 65536 | tf_op jit(solution)/shard_map/all_to_all | solution.py:611
  65.5 7.7 %collective-permute-start.7 = (f32[48,128]{1,0:T(8,128)S(1)}, f32[48,128]{1,0:T(8,128)S(1)}, u32[]{:S(2)}, u32[]{:S(2)}) collective-permute-start(f32[48,128]{1,0:T(8,128)S(1)} %get-tuple-element.38), channel_id=1, source_target_pairs={{0,1},{1,0},{2,3},{3,2},{4,5},{5,4},{6,7},{7,6},{8,9},{9,8},{10,11... | collective-permute-start | bytes 73736 | tf_op jit(solution)/shard_map/ppermute | solution.py:550
  66.1 7.0 %collective-permute-start.8 = (f32[48,128]{1,0:T(8,128)S(1)}, f32[48,128]{1,0:T(8,128)S(1)}, u32[]{:S(2)}, u32[]{:S(2)}) collective-permute-start(f32[48,128]{1,0:T(8,128)S(1)} %get-tuple-element.39), channel_id=1, source_target_pairs={{0,3},{1,2},{2,1},{3,0},{4,7},{5,6},{6,5},{7,4},{8,11},{9,10},{10,... | collective-permute-start | bytes 73736 | tf_op jit(solution)/shard_map/ppermute | solution.py:550
  73.2 1.0 copy-start.16
  75.2 5.1 %copy-start.12 = (f32[3,48,640]{2,1,0:T(8,128)S(1)}, f32[3,48,640]{2,1,0:T(8,128)}, u32[]{:S(2)}) copy-start(f32[3,48,640]{2,1,0:T(8,128)} %copy-done.11) | copy-start | bytes 1105924
  78.9 7.2 %collective-permute-start.9 = (bf16[6,32,512]{2,1,0:T(8,128)(2,1)S(1)}, bf16[6,32,512]{2,1,0:T(8,128)(2,1)S(1)}, u32[]{:S(2)}, u32[]{:S(2)}) collective-permute-start(bf16[6,32,512]{2,1,0:T(8,128)(2,1)S(1)} %get-tuple-element.50), channel_id=1, source_target_pairs={{0,64},{64,0},{1,65},{65,1},{2,66},{66,2},{3,67},{67,3},{4,68},{68... | collective-permute-start | bytes 589832 | tf_op jit(solution)/shard_map/ppermute | solution.py:550
  (10 other events, 8.0 us)

commit v3 on v2

--- a/solution.py
+++ b/solution.py
@@ -18,7 +18,7 @@
 BAND = CX + 16
 PATTERNS = 32
 BLOCKS = CX * OWN_TILES
-VMEM_LIMIT = 10 * 1024 * 1024
+VMEM_LIMIT = 12 * 1024 * 1024
 
 N_FIELDS = LEVELS + 3 + SUB - 1
 AT_COUPLING, AT_LAND, AT_MASK, AT_GUESS = LEVELS, LEVELS + 1, LEVELS + 2, LEVELS + 3
@@ -26,6 +26,7 @@
 
 VM = pl.BlockSpec(memory_space=pltpu.VMEM)
 SM = pl.BlockSpec(memory_space=pltpu.SMEM)
+HBM = pl.BlockSpec(memory_space=pltpu.HBM)
 
 
 def shape(*dims, dtype=F32):
@@ -128,7 +129,7 @@
         )
 
     def load(self, ref, l, shift=0):
-        rows = pl.ds(self.r * 8 + shift, 8)
+        rows = slice(self.r * 8 + shift, self.r * 8 + shift + 8)
         return [ref[l, rows, k * LANES : (k + 1) * LANES] for k in range(OWN_TILES + 1)]
 
     def spread(self, ref, l, d):
@@ -147,14 +148,14 @@
         return out
 
     def store(self, ref, l, values):
-        rows = pl.ds(self.r * 8, 8)
+        rows = slice(self.r * 8, self.r * 8 + 8)
         for k, v in enumerate(values):
             if k == OWN_TILES:
                 v = jnp.where(self.inside, v, 0.0)
             ref[l, rows, k * LANES : (k + 1) * LANES] = v
 
     def save(self, ref, l, values):
-        rows = pl.ds(self.r * 8 - 8, 8)
+        rows = slice(self.r * 8 - 8, self.r * 8)
         for k, v in enumerate(values):
             ref[l, rows, k * LANES : (k + 1) * LANES] = v
 
@@ -196,17 +197,71 @@
             series[t, half * 16 : half * 16 + 16, :] = emitted[t, rows, :CY].astype(BF16)
 
 
-def pack_first(state, guess, coupling, land, mask, upper, lower, one, three):
+AUX = 3 + SUB - 1
+
+
+def aux_slots():
+    n = 0
+    for a in range(AUX):
+        for i in range(SUB - 1 if a < 3 else SUB - 1 - (a - 3)):
+            yield a, i, n // 2, n % 2
+            n += 1
+
+
+def first_edges(
+    state, guess, coupling, land, mask, table,
+    to_lower, to_upper,
+    head, tail, ints, short, sems,
+):
+    del table
+    n = 0
+    copies = []
+
+    def copy(src, dst):
+        nonlocal n
+        c = pltpu.make_async_copy(src, dst, sems.at[n])
+        c.start()
+        copies.append(c)
+        n += 1
+
+    for side, msg, buf in ((0, to_lower, head), (1, to_upper, tail)):
+        rows = pl.ds(side * (CX - 8), 8)
+        copy(state.at[:, rows, :], msg)
+        copy(coupling.at[rows, :], buf.at[0])
+        copy(land.at[rows, :], buf.at[1])
+        copy(mask.at[rows, :], ints.at[side])
+        copy(guess.at[pl.ds(0, SUB - 1), pl.ds(side * (CX - 16), 16), :], short.at[side])
+    for c in copies:
+        c.wait()
+    for side, buf in ((0, head), (1, tail)):
+        buf[2] = ints[side].astype(F32)
+        for t in range(SUB - 1):
+            rows16 = short[side, t].astype(F32)
+            buf[3 + t] = rows16[8:] if side else rows16[:8]
+    for a, i, tile, spare in aux_slots():
+        to_lower[tile, 6 + spare : 7 + spare, :] = head[a, i : i + 1, :]
+        to_upper[tile, spare : spare + 1, :] = tail[a, 7 - i : 8 - i, :]
+
+
+def pack_first(
+    state, guess, coupling, land, mask, upper, lower,
+    aux, one, three,
+):
     even, _, _ = position()
+    aux[...] = jnp.zeros_like(aux)
+    for a, i, tile, spare in aux_slots():
+        aux[a, 7 - i : 8 - i, :] = upper[tile, spare : spare + 1, :]
+        aux[a, 8 + i : 9 + i, :] = lower[tile, 6 + spare : 7 + spare, :]
 
     def field(f):
         def of(tile):
-            if tile == 0:
-                block = upper.at[f]
-                rows = slice(0, 8)
-            elif tile == 5:
-                block = lower.at[f]
-                rows = slice(0, 8)
+            rows = slice(0, 8)
+            if tile in (0, 5):
+                if f < LEVELS:
+                    block = upper.at[f] if tile == 0 else lower.at[f]
+                else:
+                    block = aux.at[f - LEVELS]
+                    rows = slice(0, 8) if tile == 0 else slice(8, 16)
             else:
                 rows = slice(tile * 8 - 8, tile * 8)
                 if f < LEVELS:
@@ -219,12 +274,11 @@
                     block = mask
                 else:
                     block = guess.at[f - AT_GUESS]
-            if f >= AT_GUESS and 0 < tile < 5:
-                base = (tile - 1) // 2 * 16
-                part = slice((tile - 1) % 2 * 8, (tile - 1) % 2 * 8 + 8)
-                head = block[base : base + 16, :LANES].astype(F32)[part]
-                tail = block[base : base + 16, CY - LANES :].astype(F32)[part]
-                return head, tail
+                    base = (tile - 1) // 2 * 16
+                    part = slice((tile - 1) % 2 * 8, (tile - 1) % 2 * 8 + 8)
+                    head = block[base : base + 16, :LANES].astype(F32)[part]
+                    tail = block[base : base + 16, CY - LANES :].astype(F32)[part]
+                    return head, tail
             head, tail = block[rows, :LANES], block[rows, CY - LANES :]
             return head.astype(F32), tail.astype(F32)
 
@@ -237,10 +291,17 @@
 
 
 def first_cone(
-    diff, mix, state, guess, coupling, land, mask, upper, lower, one, three,
-    series, hd, ud, hs, us, fixed,
-    s0, s1, g, emitted,
+    diff, mix, state, guess, coupling, land, mask, upper, lower, aux, one, three,
+    series, hd, ud, hs_out, us_out, fixed_out,
+    s0, s1, g, emitted, hs, us, fixed, sems,
 ):
+    writes = []
+
+    def write(src, dst):
+        c = pltpu.make_async_copy(src, dst, sems.at[len(writes)])
+        c.start()
+        writes.append(c)
+
     even, first, last = position()
     ocean = lax.axis_index("comp") == 1
     zero_pads(s0, CONE)
@@ -249,9 +310,9 @@
         place_rows(s0.at[l], state[l], upper[l], lower[l])
 
     def rows_of(ref, k, f, own):
-        ref[k, 0:8, :CY] = upper[f]
+        ref[k, 0:8, :CY] = aux[f - LEVELS, 0:8, :]
         ref[k, 8 : 8 + CX, :CY] = own
-        ref[k, 8 + CX : 16 + CX, :CY] = lower[f]
+        ref[k, 8 + CX : 16 + CX, :CY] = aux[f - LEVELS, 8:16, :]
 
     rows_of(fixed, 0, AT_COUPLING, coupling[...])
     rows_of(fixed, 1, AT_MASK, mask[...].astype(F32))
@@ -276,12 +337,12 @@
     place_sides(put, fields, one, three, even, first, last)
     g[SUB - 1, :, side] = jnp.zeros((BAND, LANES), F32)
     fixed[2] = (1.0 - fixed[1]) * fixed[2]
+    write(fixed, fixed_out)
 
     for t in range(SUB):
         src, dst = (s0, s1) if t % 2 == 0 else (s1, s0)
 
-        @pl.loop(*strips(t))
-        def _(r, t=t, src=src, dst=dst):
+        for r in range(*strips(t)):
             strip = Strip(r, first, last)
             h = strip.spread(src, 0, diff[0])
             u_prev = None
@@ -291,7 +352,8 @@
                 v = added(h, u)
                 if l == t and t < 3:
                     strip.save(us, t, v)
-                    strip.save(hs, t, h)
+                    if t:
+                        strip.save(hs, t - 1, h)
                 if u_prev is not None:
                     v = less(v, u_prev)
                 if l == 0:
@@ -303,14 +365,22 @@
                 h, u_prev = h_next, u
             strip.save(hd, t, h)
             strip.save(ud, t, u_prev)
+            if t == 3:
+                strip.save(hs, 2, h)
+        if t < 3:
+            write(us.at[t], us_out.at[t])
+        if 0 < t < 4:
+            write(hs.at[t - 1], hs_out.at[t - 1])
 
     write_series(series, emitted)
+    for c in writes:
+        c.wait()
 
 
 def first_rest(
     diff, mix, state, upper, lower, one, three, hd, ud,
-    final, hs, us, token,
-    s0, s1,
+    final, hs_out, us_out, token,
+    s0, s1, hs, us, sems,
 ):
     token[...] = jnp.zeros_like(token)
     even, first, last = position()
@@ -327,8 +397,7 @@
     for t in range(SUB):
         src, dst = (s0, s1) if t % 2 == 0 else (s1, s0)
 
-        @pl.loop(*strips(t))
-        def _(r, t=t, src=src, dst=dst):
+        for r in range(*strips(t)):
             strip = Strip(r, first, last)
             h = strip.recall(hd, t)
             u_prev = strip.recall(ud, t)
@@ -347,62 +416,79 @@
                 if t < SUB - 1:
                     strip.store(dst, l, v)
                 elif l >= SUB:
-                    rows = pl.ds(r * 8 - 16, 8)
+                    rows = slice(r * 8 - 16, r * 8 - 8)
                     for k in range(OWN_TILES):
                         final[l, rows, k * LANES : (k + 1) * LANES] = v[k]
                 h, u_prev = h_next, u
+    writes = [
+        pltpu.make_async_copy(hs, hs_out, sems.at[0]),
+        pltpu.make_async_copy(us, us_out, sems.at[1]),
+    ]
+    for c in writes:
+        c.start()
+    for c in writes:
+        c.wait()
 
 
 def regrid(
-    src, pat, received, weights, mask, before,
+    table, received, weights, mask, before,
     out, top, bottom, gap,
     x, y,
 ):
     del before
+    for half in range(CX // 16):
+        for j in range(OWN_TILES):
+            cols = slice(j * LANES, (j + 1) * LANES)
+            for t in range(SUB):
+                v16 = received[t, half * 16 : half * 16 + 16, cols].astype(F32)
+                for part in range(2):
+                    row = half * 16 + part * 8
+                    start = (row * OWN_TILES + j) * 8 + t
+                    x[pl.ds(start, 8, stride=OWN_TILES * 8), :] = v16[part * 8 : part * 8 + 8]
+
+    @pl.loop(0, BLOCKS, unroll=32)
+    def _(q):
+        a, w = [], []
+        for k in range(2):
+            entry = table[q * 2 + k]
+            start = pl.multiple_of((entry // PATTERNS) * 8, 8)
+            a.append(x[pl.ds(start, 8), :].astype(BF16))
+            w.append(weights[entry % PATTERNS])
+        r = jnp.dot(
+            jnp.concatenate(a, 1), jnp.concatenate(w, 0), preferred_element_type=F32
+        )
+        y[pl.ds(q, 8, stride=BLOCKS), :] = r
+
     partial = [jnp.zeros((8, LANES), F32) for _ in range(SUB)]
     wet = jnp.zeros((8, LANES), F32)
     for half in range(CX // 16):
         for j in range(OWN_TILES):
             cols = slice(j * LANES, (j + 1) * LANES)
-            m16 = mask[half * 16 : half * 16 + 16, cols].astype(F32)
-            wet += m16[:8] + m16[8:]
+            masks = []
+            for part in range(2):
+                row = half * 16 + part * 8
+                masks.append(mask[row : row + 8, cols].astype(F32))
+                wet += masks[-1]
             for t in range(SUB):
                 v16 = received[t, half * 16 : half * 16 + 16, cols].astype(F32)
-                partial[t] += m16[:8] * v16[:8] + m16[8:] * v16[8:]
                 for part in range(2):
                     row = half * 16 + part * 8
-                    start = (row * OWN_TILES + j) * 8 + t
-                    x[pl.ds(start, 8, stride=OWN_TILES * 8), :] = v16[part * 8 : part * 8 + 8]
-
-    @pl.loop(0, BLOCKS, unroll=8)
-    def _(q):
-        a = [x[pl.ds(pl.multiple_of(src[q, k] * 8, 8), 8), :].astype(BF16) for k in range(2)]
-        w = [weights[pat[q, k]] for k in range(2)]
-        r = jnp.dot(
-            jnp.concatenate(a, 1), jnp.concatenate(w, 0), preferred_element_type=F32
-        )
-        y[pl.ds(q, 8, stride=BLOCKS), :] = r
-
-    for t in range(SUB):
-        for part in range(CX // 8):
-            for j in range(OWN_TILES):
-                cols = slice(j * LANES, (j + 1) * LANES)
-                rows = slice(part * 8, part * 8 + 8)
-                v = y[pl.ds(t * BLOCKS + part * 8 * OWN_TILES + j, 8, stride=OWN_TILES), :]
-                out[t, rows, cols] = v
-                partial[t] -= mask[rows, cols].astype(F32) * v
-                if t < SUB - 1:
-                    if part == 0:
+                    start = t * BLOCKS + row * OWN_TILES + j
+                    v = y[pl.ds(start, 8, stride=OWN_TILES), :]
+                    out[t, row : row + 8, cols] = v
+                    partial[t] += masks[part] * (v16[part * 8 : part * 8 + 8] - v)
+                    if t < SUB - 1 and row == 0:
                         top[t, :, cols] = v
-                    if part == CX // 8 - 1:
+                    if t < SUB - 1 and row == CX - 8:
                         bottom[t, :, cols] = v
-    _, lane = iotas()
+    row, lane = iotas()
     total = jnp.zeros((8, LANES), F32)
     for t, value in enumerate([*partial, wet]):
-        summed = jnp.sum(value, axis=(0, 1), keepdims=True)
-        total = jnp.where(lane == t, summed, total)
+        total = jnp.where(row == t, jnp.sum(value, axis=0, keepdims=True), total)
+    total = jnp.sum(total, axis=1, keepdims=True)
+    total = jnp.sum(jnp.where(row == lane, total, 0.0), axis=0, keepdims=True)
     for k in range(gap.shape[0]):
-        gap[k] = total[:1]
+        gap[k] = total
 
 
 def pack_second(out, upper, lower, one, three):
@@ -433,10 +519,14 @@
 
 
 def second_cone(
-    diff, mix, fixed, regridded, upper, lower, one, three, gap, hs, hd, us,
+    diff, mix, fixed_in, regridded, upper, lower, one, three, gap, hs_in, us_in,
     series, final0, hx, ux,
-    s0, s1, g, emitted,
+    s0, s1, g, emitted, fixed, hs, us, sems,
 ):
+    reads = []
+    for i, (src, dst) in enumerate(((us_in, us), (fixed_in, fixed), (hs_in, hs))):
+        reads.append(pltpu.make_async_copy(src, dst, sems.at[i]))
+        reads[-1].start()
     even, first, last = position()
     ocean = lax.axis_index("comp") == 1
     zero_pads(s0, 3)
@@ -453,12 +543,13 @@
     place_sides(put, list(range(SUB - 1)), one, three, even, first, last)
     g[SUB - 1, :, CY:COLS] = jnp.zeros((BAND, LANES), F32)
     means = [jnp.broadcast_to(v, (8, LANES)) for v in gap_means(gap)]
+    for c in reads:
+        c.wait()
 
     for t in range(SUB):
         src, dst = (s0, s1) if t % 2 == 0 else (s1, s0)
 
-        @pl.loop(*strips(t))
-        def _(r, t=t, src=src, dst=dst):
+        for r in range(*strips(t)):
             strip = Strip(r, first, last)
             h = strip.spread(src, 0, diff[0]) if t else None
             u_prev = None
@@ -467,7 +558,7 @@
                     if l + 1 < t:
                         h_next = strip.spread(src, l + 1, diff[l + 1])
                     else:
-                        h_next = strip.recall(hd if t == 3 else hs, t)
+                        h_next = strip.recall(hs, t - 1)
                     u = flux_between(mix[l], h_next, h)
                     v = added(h, u)
                 else:
@@ -480,7 +571,7 @@
                     v, e = surface(v, f, c, m, ml, ocean)
                     strip.save(emitted, t, e[:OWN_TILES])
                     if t == SUB - 1:
-                        rows = pl.ds(r * 8 - 16, 8)
+                        rows = slice(r * 8 - 16, r * 8 - 8)
                         for k in range(OWN_TILES):
                             final0[rows, k * LANES : (k + 1) * LANES] = v[k]
                 if t < SUB - 1:
@@ -495,22 +586,29 @@
 
 
 def second_rest(
-    diff, mix, hx, ux, hs, us, final0, whole,
+    diff, mix, hx, ux, hs_in, us_in, final0, whole,
     final, token,
-    s0, s1,
+    s0, s1, hs, us, sems,
 ):
     del whole
+    reads = [
+        pltpu.make_async_copy(us_in, us, sems.at[0]),
+        pltpu.make_async_copy(hs_in, hs, sems.at[1]),
+    ]
+    for c in reads:
+        c.start()
     token[...] = jnp.zeros_like(token)
     gy = lax.axis_index("gy")
     first, last = gy == 0, gy == lax.axis_size("gy") - 1
     zero_pads(s0, SUB)
     zero_pads(s1, SUB)
     final[0] = final0[...]
+    for c in reads:
+        c.wait()
     for t in range(3, SUB):
         src, dst = (s0, s1) if t % 2 == 0 else (s1, s0)
 
-        @pl.loop(*strips(t))
-        def _(r, t=t, src=src, dst=dst):
+        for r in range(*strips(t)):
             strip = Strip(r, first, last)
             h = strip.recall(hx, t - 3)
             u_prev = strip.recall(ux, t - 3)
@@ -531,7 +629,7 @@
                 if t < SUB - 1:
                     strip.store(dst, l, v)
                 else:
-                    rows = pl.ds(r * 8 - 16, 8)
+                    rows = slice(r * 8 - 16, r * 8 - 8)
                     for k in range(OWN_TILES):
                         final[l, rows, k * LANES : (k + 1) * LANES] = v[k]
 
@@ -555,28 +653,28 @@
 ):
     state, guess, diff, mix, coupling = state[0], guess[0], diffusion[0], mixing[0], coupling[0]
     weights = weights[0]
-    src = source_block[0].reshape(BLOCKS, 2)
-    pat = pattern[0].reshape(BLOCKS, 2)
+    table = (source_block[0] * PATTERNS + pattern[0]).reshape(2 * BLOCKS)
     peers = lax.axis_size("gx") * lax.axis_size("gy")
     band = lambda n: shape(n, BAND, COLS)
     field_buf = lambda n: pltpu.VMEM((n, ROWS, COLS), F32)
     band_buf = lambda n: pltpu.VMEM((n, BAND, COLS), F32)
 
-    def edge(rows):
-        return jnp.concatenate(
-            [
-                state[:, rows],
-                coupling[None, rows],
-                land_temp[None, rows],
-                land_mask[None, rows].astype(F32),
-                guess[: SUB - 1, rows].astype(F32),
-            ]
-        )
-
-    lower = shifted(edge(slice(0, 8)), "gx", -1)
-    upper = shifted(edge(slice(CX - 8, CX)), "gx", 1)
+    message = shape(LEVELS, 8, CY)
+    to_lower, to_upper = call(
+        first_edges,
+        [message, message],
+        [
+            pltpu.VMEM((AUX, 8, CY), F32),
+            pltpu.VMEM((AUX, 8, CY), F32),
+            pltpu.VMEM((2, 8, CY), jnp.int32),
+            pltpu.VMEM((2, SUB - 1, 16, CY), BF16),
+            pltpu.SemaphoreType.DMA((10,)),
+        ],
+        [HBM] * 5 + [SM],
+    )(state, guess, coupling, land_temp, land_mask, table)
+    lower, upper = shifted(to_lower, "gx", -1), shifted(to_upper, "gx", 1)
     packed = shape(BAND, PACK_LANES)
-    one, three = call(pack_first, [packed, packed], [], [VM] * 7)(
+    aux, one, three = call(pack_first, [shape(AUX, 16, CY), packed, packed], [], [VM] * 7)(
         state, guess, coupling, land_temp, land_mask, upper, lower
     )
     one, three = paired(one, "gy", 1), paired(three, "gy", 3)
@@ -584,9 +682,13 @@
     series, hd, ud, hs, us, fixed = call(
         first_cone,
         [shape(SUB, CX, CY, dtype=BF16), band(SUB), band(SUB), band(3), band(3), band(3)],
-        [field_buf(CONE), field_buf(CONE), band_buf(SUB), band_buf(SUB)],
-        [SM, SM] + [VM] * 9,
-    )(diff, mix, state, guess, coupling, land_temp, land_mask, upper, lower, one, three)
+        [
+            field_buf(CONE), field_buf(CONE), band_buf(SUB), band_buf(SUB),
+            band_buf(3), band_buf(3), band_buf(3), pltpu.SemaphoreType.DMA((7,)),
+        ],
+        [SM, SM] + [VM] * 10,
+        out_specs=[VM] * 3 + [HBM] * 3,
+    )(diff, mix, state, guess, coupling, land_temp, land_mask, upper, lower, aux, one, three)
 
     def exchange(series, before):
         received = paired(series, "comp", 1)
@@ -595,15 +697,19 @@
             regrid,
             [shape(SUB, CX, CY), edges, edges, shape(peers, 1, LANES)],
             [pltpu.VMEM((BLOCKS * 8, LANES), F32), pltpu.VMEM((BLOCKS * 8, LANES), F32)],
-            [SM, SM, VM, VM, VM, VM],
-        )(src, pat, received, weights, land_mask, before)
+            [SM, VM, VM, VM, VM],
+        )(table, received, weights, land_mask, before)
         return out, top, bottom, gap
 
     whole, hs_rest, us_rest, token = call(
         first_rest,
         [shape(LEVELS, CX, CY), band(3), band(3), shape(8, LANES)],
-        [field_buf(LEVELS), field_buf(LEVELS)],
+        [
+            field_buf(LEVELS), field_buf(LEVELS),
+            band_buf(3), band_buf(3), pltpu.SemaphoreType.DMA((2,)),
+        ],
         [SM, SM] + [VM] * 7,
+        out_specs=[VM, HBM, HBM, VM],
     )(diff, mix, state, upper, lower, one, three, hd, ud)
 
     out, top, bottom, gap = exchange(series, token)
@@ -616,15 +722,21 @@
     series, final0, hx, ux = call(
         second_cone,
         [shape(SUB, CX, CY, dtype=BF16), shape(CX, CY), band(3), band(3)],
-        [field_buf(3), field_buf(3), band_buf(SUB), band_buf(SUB)],
-        [SM, SM] + [VM] * 10,
-    )(diff, mix, fixed, out, upper, lower, one, three, gap, hs, hd, us)
+        [
+            field_buf(3), field_buf(3), band_buf(SUB), band_buf(SUB),
+            band_buf(3), band_buf(3), band_buf(3), pltpu.SemaphoreType.DMA((3,)),
+        ],
+        [SM, SM, HBM] + [VM] * 6 + [HBM, HBM],
+    )(diff, mix, fixed, out, upper, lower, one, three, gap, hs, us)
 
     whole, token = call(
         second_rest,
         [shape(LEVELS, CX, CY), shape(8, LANES)],
-        [field_buf(SUB), field_buf(SUB)],
-        [SM, SM] + [VM] * 5 + [pl.BlockSpec(memory_space=pl.ANY)],
+        [
+            field_buf(SUB), field_buf(SUB),
+            band_buf(3), band_buf(3), pltpu.SemaphoreType.DMA((2,)),
+        ],
+        [SM, SM, VM, VM, HBM, HBM, VM, pl.BlockSpec(memory_space=pl.ANY)],
         out_specs=[pl.BlockSpec((SUB, CX, CY), lambda i: (0, 0, 0)), VM],
         grid=(1,),
         input_output_aliases={7: 0},

time: 108 us -> 90.6 us (0.84)
  Pallas kernels: 35.4 us -> 25.3 us
  local copies, waits for them, and re-layouts: 11.1 us -> 5.79 us
  waiting for transfers between devices: 20.4 us -> 16.5 us
  starting transfers between devices: 25.3 us -> 26.6 us
    pallas_call x2, Pallas kernels: 13.6 us -> 7.57 us  [exchange(): call(regrid, [shape(SUB, CX, CY), edges, edges, shape(peers, 1, LANES)],...]
    unnamed x51 -> x20, local copies, waits for them, and re-layouts: 11.1 us -> 5.52 us
    ppermute x4, waiting for transfers between devices: 8.77 us -> 5.96 us  [shifted(): return lax.ppermute(value, axis, [(i, (i + by) % n) for i in range(n)])]
    pallas_call x1, Pallas kernels: 8.45 us -> 6.23 us  [per_device(): call(first_rest, [shape(LEVELS, CX, CY), band(3), band(3), shape(8, LANES...]
    pallas_call x1, Pallas kernels: 5.88 us -> 4.22 us  [per_device(): call(first_cone, [shape(SUB, CX, CY, dtype=BF16), band(SUB), band(SUB), b...]
    pallas_call x1, Pallas kernels: 3.76 us -> 2.4 us  [per_device(): call(second_cone, [shape(SUB, CX, CY, dtype=BF16), shape(CX, CY), band(3)...]
where the time goes in v3:
time: 90.6 us; the launch traced here: 90.1 us
  starting transfers between devices  26.6 us (29%)
  Pallas kernels  25.3 us (28%)
  waiting for transfers between devices  16.5 us (18%)
  blocking collectives  14.6 us (16%)
  local copies, waits for them, and re-layouts  5.79 us (6%)
    all_to_all x1, blocking collectives, per_device(): gap = lax.all_to_all(gap, ('gx', 'gy'), 0, 0)  14.6 us
    ppermute x4, starting transfers between devices, shifted(): return lax.ppermute(value, axis, [(i, (i + by) % n) for i in range(n)])  11.8 us
    ppermute x6, starting transfers between devices, paired(): lax.ppermute(value, axis, [(i, i ^ mask) for i in range(lax.axis_size(axi...  9.75 us
    pallas_call x2, Pallas kernels, exchange(): call(regrid, [shape(SUB, CX, CY), edges, edges, shape(peers, 1, LANES)],...  7.57 us
    pallas_call x1, Pallas kernels, per_device(): call(first_rest, [shape(LEVELS, CX, CY), band(3), band(3), shape(8, LANES...  6.23 us
    ppermute x4, waiting for transfers between devices, shifted(): return lax.ppermute(value, axis, [(i, (i + by) % n) for i in range(n)])  5.96 us
    unnamed x20, local copies, waits for them, and re-layouts  5.52 us
    all_to_all x1, waiting for transfers between devices, per_device(): gap = lax.all_to_all(gap, ('gx', 'gy'), 0, 0)  5.29 us
  transfers between devices with their start and end apart: 11, of which 4 were waited for; matrix products, arithmetic and copies ran while one was open for 0% of the time, Pallas kernels for 10%

profile of v3, /device:TPU:1, one launch (start us, length us, event | category | flops | bytes accessed | tf_op | source)
XLA Modules:
  0.0 90.1 jit_solution(13042926973178329928)
XLA Ops:
  2.2 1.2 %copy-done = f32[1,16,32,512]{3,2,1,0:T(8,128)S(1)} copy-done((f32[1,16,32,512]{3,2,1,0:T(8,128)S(1)}, f32[1,16,32,512]{3,2,1,0:T(8,128)}, u32[]{:S(2)}) %copy-start) | copy-done | bytes 1048600
  3.4 0.9 %copy-done.3 = bf16[1,6,32,512]{3,2,1,0:T(8,128)(2,1)S(1)} copy-done((bf16[1,6,32,512]{3,2,1,0:T(8,128)(2,1)S(1)}, bf16[1,6,32,512]{3,2,1,0:T(8,128)(2,1)}, u32[]{:S(2)}) %copy-start.3) | copy-done | bytes 196632
  5.2 0.9 shard_map.113
  6.1 2.1 %collective-permute-start = (f32[16,8,512]{2,1,0:T(8,128)S(1)}, f32[16,8,512]{2,1,0:T(8,128)S(1)}, u32[]{:S(2)}, u32[]{:S(2)}) collective-permute-start(f32[16,8,512]{2,1,0:T(8,128)S(1)} %get-tuple-element.31), channel_id=1, source_target_pairs={{0,4},{4,8},{8,12},{12,16},{16,20},{20,24},{24,28},{28,32},{32,36}... | collective-permute-start | bytes 786440 | tf_op jit(solution)/shard_map/ppermute | solution.py:644
  8.2 4.8 %collective-permute-start.1 = (f32[16,8,512]{2,1,0:T(8,128)S(1)}, f32[16,8,512]{2,1,0:T(8,128)S(1)}, u32[]{:S(2)}, u32[]{:S(2)}) collective-permute-start(f32[16,8,512]{2,1,0:T(8,128)S(1)} %get-tuple-element.32), channel_id=1, source_target_pairs={{0,60},{4,0},{8,4},{12,8},{16,12},{20,16},{24,20},{28,24},{32,28},... | collective-permute-start | bytes 786440 | tf_op jit(solution)/shard_map/ppermute | solution.py:644
  13.0 6.0 %collective-permute-done.upper = f32[16,8,512]{2,1,0:T(8,128)S(1)} collective-permute-done((f32[16,8,512]{2,1,0:T(8,128)S(1)}, f32[16,8,512]{2,1,0:T(8,128)S(1)}, u32[]{:S(2)}, u32[]{:S(2)}) %collective-permute-start) | collective-permute-done | bytes 262176 | tf_op jit(solution)/shard_map/ppermute | solution.py:644
  19.3 1.3 %collective-permute-start.2 = (f32[48,256]{1,0:T(8,128)S(1)}, f32[48,256]{1,0:T(8,128)S(1)}, u32[]{:S(2)}, u32[]{:S(2)}) collective-permute-start(f32[48,256]{1,0:T(8,128)S(1)} %get-tuple-element.34), channel_id=1, source_target_pairs={{0,1},{1,0},{2,3},{3,2},{4,5},{5,4},{6,7},{7,6},{8,9},{9,8},{10,11... | collective-permute-start | bytes 147464 | tf_op jit(solution)/shard_map/ppermute | solution.py:648
  20.6 1.3 %collective-permute-start.3 = (f32[48,256]{1,0:T(8,128)S(1)}, f32[48,256]{1,0:T(8,128)S(1)}, u32[]{:S(2)}, u32[]{:S(2)}) collective-permute-start(f32[48,256]{1,0:T(8,128)S(1)} %get-tuple-element.35), channel_id=1, source_target_pairs={{0,3},{1,2},{2,1},{3,0},{4,7},{5,6},{6,5},{7,4},{8,11},{9,10},{10,... | collective-permute-start | bytes 147464 | tf_op jit(solution)/shard_map/ppermute | solution.py:648
  21.9 2.3 %collective-permute-done.3.three = f32[48,256]{1,0:T(8,128)S(1)} collective-permute-done((f32[48,256]{1,0:T(8,128)S(1)}, f32[48,256]{1,0:T(8,128)S(1)}, u32[]{:S(2)}, u32[]{:S(2)}) %collective-permute-start.3) | collective-permute-done | bytes 49184 | tf_op jit(solution)/shard_map/ppermute | solution.py:648
  24.9 4.2 %shard_map.115 = (bf16[6,32,512]{2,1,0:T(8,128)(2,1)S(1)}, f32[6,48,640]{2,1,0:T(8,128)S(1)}, f32[6,48,640]{2,1,0:T(8,128)S(1)}, f32[3,48,640]{2,1,0:T(8,128)S(1...) custom-call(f32[16]{0:T(128)S(1)} %bitcast.20, f32[15]{0:T(128)S(1)} %bitcast.24, f32[16,32,512]{2,1,0:T(8,128)S(1)} %bitcast.10, ...), custom_call_target="tpu_custom_call" | custom-call | tf_op jit(solution)/shard_map/pallas_call | solution.py:682
  29.1 3.0 %collective-permute-start.4 = (bf16[6,32,512]{2,1,0:T(8,128)(2,1)S(1)}, bf16[6,32,512]{2,1,0:T(8,128)(2,1)S(1)}, u32[]{:S(2)}, u32[]{:S(2)}) collective-permute-start(bf16[6,32,512]{2,1,0:T(8,128)(2,1)S(1)} %get-tuple-element.37), channel_id=1, source_target_pairs={{0,64},{64,0},{1,65},{65,1},{2,66},{66,2},{3,67},{67,3},{4,68},{68... | collective-permute-start | bytes 589832 | tf_op jit(solution)/shard_map/ppermute | solution.py:648
  32.1 6.2 %shard_map.116 = (f32[16,32,512]{2,1,0:T(8,128)}, f32[3,48,640]{2,1,0:T(8,128)S(1)}, f32[3,48,640]{2,1,0:T(8,128)S(1)}, f32[8,128]{1,0:T(8,128)S(1)}) custom-call(f32[16]{0:T(128)S(1)} %bitcast.21, f32[15]{0:T(128)S(1)} %bitcast.25, f32[16,32,512]{2,1,0:T(8,128)S(1)} %bitcast.11, f32[16,8,512]{2,1,0:T(8,128)S(1)} %collective-permute-done.upper, ...), custom_call_target="tpu_custom_call" | custom-call | tf_op jit(solution)/shard_map/pallas_call | solution.py:704
  38.4 3.8 %shard_map.117 = (f32[6,32,512]{2,1,0:T(8,128)S(1)}, f32[5,8,512]{2,1,0:T(8,128)}, f32[5,8,512]{2,1,0:T(8,128)}, f32[64,1,128]{2,1,0:T(1,128)S(1)}) custom-call(s32[256]{0:T(256)S(1)} %add.8.table, bf16[6,32,512]{2,1,0:T(8,128)(2,1)S(1)} %collective-permute-done.4.received, bf16[32,128,128]{2,1,0:T(8,128)(2,1)S(1)} %bitcast.12, s32[32,512]{1,0:T(8,128)S(1)} %copy-done.2, ...), custom_call_target="tpu_custom_call" | custom-call | tf_op jit(solution)/shard_map/pallas_call | solution.py:696
  42.7 4.9 %collective-permute-start.6 = (f32[5,8,512]{2,1,0:T(8,128)}, f32[5,8,512]{2,1,0:T(8,128)S(1)}, u32[]{:S(2)}, u32[]{:S(2)}) collective-permute-start(f32[5,8,512]{2,1,0:T(8,128)} %get-tuple-element.43), channel_id=1, source_target_pairs={{0,60},{4,0},{8,4},{12,8},{16,12},{20,16},{24,20},{28,24},{32,28},... | collective-permute-start | bytes 245768 | tf_op jit(solution)/shard_map/ppermute | solution.py:644
  47.6 5.0 %all-to-all-start = ((f32[64,1,128]{2,1,0:T(1,128)}), f32[64,1,128]{2,1,0:T(1,128)S(1)}, u32[]{:S(2)}, u32[]{:S(2)}) async-start(f32[64,1,128]{2,1,0:T(1,128)} %copy-done.6), calls=%async_computation | async-start | bytes 65536 | tf_op jit(solution)/shard_map/all_to_all | solution.py:717
  54.0 1.2 %collective-permute-start.8 = (f32[48,128]{1,0:T(8,128)}, f32[48,128]{1,0:T(8,128)}, u32[]{:S(2)}, u32[]{:S(2)}) collective-permute-start(f32[48,128]{1,0:T(8,128)} %get-tuple-element.45), channel_id=1, source_target_pairs={{0,3},{1,2},{2,1},{3,0},{4,7},{5,6},{6,5},{7,4},{8,11},{9,10},{10,... | collective-permute-start | bytes 73736 | tf_op jit(solution)/shard_map/ppermute | solution.py:648
  55.2 5.3 %all-to-all-done.gap = f32[64,1,128]{2,1,0:T(1,128)S(1)} async-done(((f32[64,1,128]{2,1,0:T(1,128)}), f32[64,1,128]{2,1,0:T(1,128)S(1)}, u32[]{:S(2)}, u32[]{:S(2)}) %all-to-all-start) | async-done | bytes 32800 | tf_op jit(solution)/shard_map/all_to_all | solution.py:717
  61.1 2.4 %shard_map.119 = (bf16[6,32,512]{2,1,0:T(8,128)(2,1)S(1)}, f32[32,512]{1,0:T(8,128)S(1)}, f32[3,48,640]{2,1,0:T(8,128)S(1)}, f32[3,48,640]{2,1,0:T(8,128)S(1)}) custom-call(f32[16]{0:T(128)S(1)} %bitcast.22, f32[15]{0:T(128)S(1)} %bitcast.26, f32[3,48,640]{2,1,0:T(8,128)S(1)} %get-tuple-element.36.fixed_in, ...), custom_call_target="tpu_custom_call" | custom-call | tf_op jit(solution)/shard_map/pallas_call | solution.py:722
  63.6 2.4 %collective-permute-start.9 = (bf16[6,32,512]{2,1,0:T(8,128)(2,1)S(1)}, bf16[6,32,512]{2,1,0:T(8,128)(2,1)S(1)}, u32[]{:S(2)}, u32[]{:S(2)}) collective-permute-start(bf16[6,32,512]{2,1,0:T(8,128)(2,1)S(1)} %get-tuple-element.56), channel_id=1, source_target_pairs={{0,64},{64,0},{1,65},{65,1},{2,66},{66,2},{3,67},{67,3},{4,68},{68... | collective-permute-start | bytes 589832 | tf_op jit(solution)/shard_map/ppermute | solution.py:648
  65.9 1.9 %shard_map.120 = (f32[16,32,512]{2,1,0:T(8,128)}, f32[8,128]{1,0:T(8,128)S(1)}) custom-call(f32[16]{0:T(128)S(1)} %bitcast.23, f32[15]{0:T(128)S(1)} %bitcast.27, f32[3,48,640]{2,1,0:T(8,128)S(1)} %get-tuple-element.49.hx, f32[3,48,640]{2,1,0:T(8,128)S(1)} %get-tuple-element.50.ux, ...), custom_call_target="tpu_custom_call", output_to_operand_aliasing={{0}: (7, {})} | custom-call | tf_op jit(solution)/shard_map/pallas_call | solution.py:732
  67.8 3.0 %collective-permute-done.9.received = bf16[6,32,512]{2,1,0:T(8,128)(2,1)S(1)} collective-permute-done((bf16[6,32,512]{2,1,0:T(8,128)(2,1)S(1)}, bf16[6,32,512]{2,1,0:T(8,128)(2,1)S(1)}, u32[]{:S(2)}, u32[]{:S(2)}) %collective-permute-start.9) | collective-permute-done | bytes 196640 | tf_op jit(solution)/shard_map/ppermute | solution.py:648
  70.8 3.8 %shard_map.121 = (f32[6,32,512]{2,1,0:T(8,128)S(1)}, f32[5,8,512]{2,1,0:T(8,128)}, f32[5,8,512]{2,1,0:T(8,128)}, f32[64,1,128]{2,1,0:T(1,128)S(1)}) custom-call(s32[256]{0:T(256)S(1)} %add.8.table, bf16[6,32,512]{2,1,0:T(8,128)(2,1)S(1)} %collective-permute-done.9.received, bf16[32,128,128]{2,1,0:T(8,128)(2,1)S(1)} %bitcast.13, s32[32,512]{1,0:T(8,128)S(1)} %copy-done.2, ...), custom_call_target="tpu_custom_call" | custom-call | tf_op jit(solution)/shard_map/pallas_call | solution.py:696
  74.6 14.6 %all_to_all.10.gap = f32[64,1,128]{2,1,0:T(1,128)S(1)} all-to-all(f32[64,1,128]{2,1,0:T(1,128)S(1)} %get-tuple-element.59), channel_id=1, replica_groups=mesh['comp'=2,'gx'=16,'gy'=4] {'gx','gy'}, dimensions={0} | all-to-all | bytes 65536 | tf_op jit(solution)/shard_map/all_to_all | solution.py:746
  89.2 0.9 %shard_map.122 = f32[6,32,512]{2,1,0:T(8,128)} custom-call(f32[6,32,512]{2,1,0:T(8,128)S(1)} %get-tuple-element.58.regridded, s32[32,512]{1,0:T(8,128)S(1)} %copy-done.2, f32[64,1,128]{2,1,0:T(1,128)S(1)} %all_to_all.10.gap), custom_call_target="tpu_custom_call" | custom-call | tf_op jit(solution)/shard_map/pallas_call | solution.py:747
  (32 shorter events, 6.0 us)
Async XLA Ops:
  1.3 0.8 copy-start.2
  1.3 0.9 copy-start.4
  2.2 1.2 %copy-start = (f32[1,16,32,512]{3,2,1,0:T(8,128)S(1)}, f32[1,16,32,512]{3,2,1,0:T(8,128)}, u32[]{:S(2)}) copy-start(f32[1,16,32,512]{3,2,1,0:T(8,128)} %param.10) | copy-start | bytes 3145732
  3.4 0.9 %copy-start.3 = (bf16[1,6,32,512]{3,2,1,0:T(8,128)(2,1)S(1)}, bf16[1,6,32,512]{3,2,1,0:T(8,128)(2,1)}, u32[]{:S(2)}) copy-start(bf16[1,6,32,512]{3,2,1,0:T(8,128)(2,1)} %param.11) | copy-start | bytes 589828
  4.4 0.8 copy-start.5
  6.1 12.9 %collective-permute-start = (f32[16,8,512]{2,1,0:T(8,128)S(1)}, f32[16,8,512]{2,1,0:T(8,128)S(1)}, u32[]{:S(2)}, u32[]{:S(2)}) collective-permute-start(f32[16,8,512]{2,1,0:T(8,128)S(1)} %get-tuple-element.31), channel_id=1, source_target_pairs={{0,4},{4,8},{8,12},{12,16},{16,20},{20,24},{24,28},{28,32},{32,36}... | collective-permute-start | bytes 786440 | tf_op jit(solution)/shard_map/ppermute | solution.py:644
  8.2 10.8 %collective-permute-start.1 = (f32[16,8,512]{2,1,0:T(8,128)S(1)}, f32[16,8,512]{2,1,0:T(8,128)S(1)}, u32[]{:S(2)}, u32[]{:S(2)}) collective-permute-start(f32[16,8,512]{2,1,0:T(8,128)S(1)} %get-tuple-element.32), channel_id=1, source_target_pairs={{0,60},{4,0},{8,4},{12,8},{16,12},{20,16},{24,20},{28,24},{32,28},... | collective-permute-start | bytes 786440 | tf_op jit(solution)/shard_map/ppermute | solution.py:644
  19.3 2.6 %collective-permute-start.2 = (f32[48,256]{1,0:T(8,128)S(1)}, f32[48,256]{1,0:T(8,128)S(1)}, u32[]{:S(2)}, u32[]{:S(2)}) collective-permute-start(f32[48,256]{1,0:T(8,128)S(1)} %get-tuple-element.34), channel_id=1, source_target_pairs={{0,1},{1,0},{2,3},{3,2},{4,5},{5,4},{6,7},{7,6},{8,9},{9,8},{10,11... | collective-permute-start | bytes 147464 | tf_op jit(solution)/shard_map/ppermute | solution.py:648
  20.6 3.5 %collective-permute-start.3 = (f32[48,256]{1,0:T(8,128)S(1)}, f32[48,256]{1,0:T(8,128)S(1)}, u32[]{:S(2)}, u32[]{:S(2)}) collective-permute-start(f32[48,256]{1,0:T(8,128)S(1)} %get-tuple-element.35), channel_id=1, source_target_pairs={{0,3},{1,2},{2,1},{3,0},{4,7},{5,6},{6,5},{7,4},{8,11},{9,10},{10,... | collective-permute-start | bytes 147464 | tf_op jit(solution)/shard_map/ppermute | solution.py:648
  24.2 0.7 copy-start.7
  24.2 0.7 copy-start.8
  29.1 9.3 %collective-permute-start.4 = (bf16[6,32,512]{2,1,0:T(8,128)(2,1)S(1)}, bf16[6,32,512]{2,1,0:T(8,128)(2,1)S(1)}, u32[]{:S(2)}, u32[]{:S(2)}) collective-permute-start(bf16[6,32,512]{2,1,0:T(8,128)(2,1)S(1)} %get-tuple-element.37), channel_id=1, source_target_pairs={{0,64},{64,0},{1,65},{65,1},{2,66},{66,2},{3,67},{67,3},{4,68},{68... | collective-permute-start | bytes 589832 | tf_op jit(solution)/shard_map/ppermute | solution.py:648
  32.1 6.3 %copy-start.1 = (bf16[1,32,128,128]{3,2,1,0:T(8,128)(2,1)S(1)}, bf16[1,32,128,128]{3,2,1,0:T(8,128)(2,1)}, u32[]{:S(2)}) copy-start(bf16[1,32,128,128]{3,2,1,0:T(8,128)(2,1)} %param.17) | copy-start | bytes 3145732
  42.1 0.6 copy-start.6
  42.7 9.9 %collective-permute-start.5 = (f32[5,8,512]{2,1,0:T(8,128)}, f32[5,8,512]{2,1,0:T(8,128)S(1)}, u32[]{:S(2)}, u32[]{:S(2)}) collective-permute-start(f32[5,8,512]{2,1,0:T(8,128)} %get-tuple-element.42), channel_id=1, source_target_pairs={{0,4},{4,8},{8,12},{12,16},{16,20},{20,24},{24,28},{28,32},{32,36}... | collective-permute-start | bytes 245768 | tf_op jit(solution)/shard_map/ppermute | solution.py:644
  42.7 9.9 %collective-permute-start.6 = (f32[5,8,512]{2,1,0:T(8,128)}, f32[5,8,512]{2,1,0:T(8,128)S(1)}, u32[]{:S(2)}, u32[]{:S(2)}) collective-permute-start(f32[5,8,512]{2,1,0:T(8,128)} %get-tuple-element.43), channel_id=1, source_target_pairs={{0,60},{4,0},{8,4},{12,8},{16,12},{20,16},{24,20},{28,24},{32,28},... | collective-permute-start | bytes 245768 | tf_op jit(solution)/shard_map/ppermute | solution.py:644
  47.6 12.9 %all-to-all-start = ((f32[64,1,128]{2,1,0:T(1,128)}), f32[64,1,128]{2,1,0:T(1,128)S(1)}, u32[]{:S(2)}, u32[]{:S(2)}) async-start(f32[64,1,128]{2,1,0:T(1,128)} %copy-done.6), calls=%async_computation | async-start | bytes 65536 | tf_op jit(solution)/shard_map/all_to_all | solution.py:717
  53.4 7.1 %collective-permute-start.7 = (f32[48,128]{1,0:T(8,128)}, f32[48,128]{1,0:T(8,128)}, u32[]{:S(2)}, u32[]{:S(2)}) collective-permute-start(f32[48,128]{1,0:T(8,128)} %get-tuple-element.44), channel_id=1, source_target_pairs={{0,1},{1,0},{2,3},{3,2},{4,5},{5,4},{6,7},{7,6},{8,9},{9,8},{10,11... | collective-permute-start | bytes 73736 | tf_op jit(solution)/shard_map/ppermute | solution.py:648
  54.0 6.5 %collective-permute-start.8 = (f32[48,128]{1,0:T(8,128)}, f32[48,128]{1,0:T(8,128)}, u32[]{:S(2)}, u32[]{:S(2)}) collective-permute-start(f32[48,128]{1,0:T(8,128)} %get-tuple-element.45), channel_id=1, source_target_pairs={{0,3},{1,2},{2,1},{3,0},{4,7},{5,6},{6,5},{7,4},{8,11},{9,10},{10,... | collective-permute-start | bytes 73736 | tf_op jit(solution)/shard_map/ppermute | solution.py:648
  60.5 0.7 copy-start.9
  63.6 7.3 %collective-permute-start.9 = (bf16[6,32,512]{2,1,0:T(8,128)(2,1)S(1)}, bf16[6,32,512]{2,1,0:T(8,128)(2,1)S(1)}, u32[]{:S(2)}, u32[]{:S(2)}) collective-permute-start(bf16[6,32,512]{2,1,0:T(8,128)(2,1)S(1)} %get-tuple-element.56), channel_id=1, source_target_pairs={{0,64},{64,0},{1,65},{65,1},{2,66},{66,2},{3,67},{67,3},{4,68},{68... | collective-permute-start | bytes 589832 | tf_op jit(solution)/shard_map/ppermute | solution.py:648

commit v4 on v3

--- a/solution.py
+++ b/solution.py
@@ -19,6 +19,7 @@
 PATTERNS = 32
 BLOCKS = CX * OWN_TILES
 VMEM_LIMIT = 12 * 1024 * 1024
+EDGE_GRANT = 60 * 1024 * 1024
 
 N_FIELDS = LEVELS + 3 + SUB - 1
 AT_COUPLING, AT_LAND, AT_MASK, AT_GUESS = LEVELS, LEVELS + 1, LEVELS + 2, LEVELS + 3
@@ -33,14 +34,14 @@
     return jax.ShapeDtypeStruct(dims, dtype)
 
 
-def call(body, outs, scratch, ins, out_specs=None, **kw):
+def call(body, outs, scratch, ins, out_specs=None, grant=VMEM_LIMIT, **kw):
     return pl.pallas_call(
         body,
         out_shape=outs,
         in_specs=ins,
         out_specs=[VM] * len(outs) if out_specs is None else out_specs,
         scratch_shapes=scratch,
-        compiler_params=pltpu.CompilerParams(vmem_limit_bytes=VMEM_LIMIT),
+        compiler_params=pltpu.CompilerParams(vmem_limit_bytes=grant),
         **kw,
     )
 
@@ -186,6 +187,18 @@
     return new, emitted
 
 
+class Rows:
+    def __init__(self, ref, start):
+        self.ref, self.start = ref, start
+
+    def __getitem__(self, l):
+        return self.ref[self.start + l]
+
+
+def coefficients(coeff):
+    return Rows(coeff, 0), Rows(coeff, LEVELS)
+
+
 def strips(t):
     return (1, 7) if t < SUB - 1 else (2, 6)
 
@@ -209,11 +222,11 @@
 
 
 def first_edges(
-    state, guess, coupling, land, mask, table,
-    to_lower, to_upper,
+    state, guess, coupling, land, mask,
+    to_lower, to_upper, token,
     head, tail, ints, short, sems,
 ):
-    del table
+    token[...] = jnp.zeros_like(token)
     n = 0
     copies = []
 
@@ -244,9 +257,10 @@
 
 
 def pack_first(
-    state, guess, coupling, land, mask, upper, lower,
+    state, guess, coupling, land, mask, upper, lower, before,
     aux, one, three,
 ):
+    del before
     even, _, _ = position()
     aux[...] = jnp.zeros_like(aux)
     for a, i, tile, spare in aux_slots():
@@ -291,10 +305,11 @@
 
 
 def first_cone(
-    diff, mix, state, guess, coupling, land, mask, upper, lower, aux, one, three,
-    series, hd, ud, hs_out, us_out, fixed_out,
+    coeff, state, guess, coupling, land, mask, upper, lower, aux, one, three,
+    series, hd, ud, hs_out, us_out, fixed_out, coeff_out,
     s0, s1, g, emitted, hs, us, fixed, sems,
 ):
+    diff, mix = coefficients(coeff)
     writes = []
 
     def write(src, dst):
@@ -338,6 +353,7 @@
     g[SUB - 1, :, side] = jnp.zeros((BAND, LANES), F32)
     fixed[2] = (1.0 - fixed[1]) * fixed[2]
     write(fixed, fixed_out)
+    write(coeff, coeff_out)
 
     for t in range(SUB):
         src, dst = (s0, s1) if t % 2 == 0 else (s1, s0)
@@ -378,10 +394,11 @@
 
 
 def first_rest(
-    diff, mix, state, upper, lower, one, three, hd, ud,
+    coeff, state, upper, lower, one, three, hd, ud,
     final, hs_out, us_out, token,
     s0, s1, hs, us, sems,
 ):
+    diff, mix = coefficients(coeff)
     token[...] = jnp.zeros_like(token)
     even, first, last = position()
     zero_pads(s0, LEVELS)
@@ -430,12 +447,101 @@
         c.wait()
 
 
-def regrid(
-    table, received, weights, mask, before,
-    out, top, bottom, gap,
-    x, y,
+def balance(
+    diff, mix, src, pat, weights, mask, after,
+    out, wet, coeff,
+    m, z, total, b, sem,
+):
+    del after
+    for l in range(LEVELS):
+        coeff[l] = jnp.full((8, LANES), diff[l], F32)
+    for l in range(LEVELS - 1):
+        coeff[LEVELS + l] = jnp.full((8, LANES), mix[l], F32)
+    coeff[2 * LEVELS - 1] = jnp.zeros((8, LANES), F32)
+    count = jnp.zeros((8, LANES), F32)
+    for part in range(CX // 8):
+        for j in range(OWN_TILES):
+            v = mask[part * 8 : part * 8 + 8, j * LANES : (j + 1) * LANES].astype(F32)
+            count += v
+            m[pl.ds(part * 8 * OWN_TILES + j, 8, stride=OWN_TILES), :] = v
+    _, lane = iotas()
+    count = jnp.sum(count, axis=(0, 1), keepdims=True)
+    wet[...] = jnp.where(lane[:1] == SUB, count, 0.0)
+    blocks = m[...].astype(BF16)
+
+    @pl.loop(0, PATTERNS)
+    def _(p):
+        z[p] = lax.dot_general(
+            blocks, weights[p], (((1,), (1,)), ((), ())), preferred_element_type=F32
+        )
+
+    total[...] = m[...]
+
+    @pl.loop(0, CX)
+    def _(r):
+        for j in range(OWN_TILES):
+            for k in range(2):
+                row = pl.ds(src[j, k, r], 1)
+                total[row, :] = total[row, :] - z[pat[j, k, r], pl.ds(r * OWN_TILES + j, 1), :]
+
+    for part in range(CX // 8):
+        for j in range(OWN_TILES):
+            v = total[pl.ds(part * 8 * OWN_TILES + j, 8, stride=OWN_TILES), :]
+            b[part * 8 : part * 8 + 8, j * LANES : (j + 1) * LANES] = v
+    c = pltpu.make_async_copy(b, out, sem)
+    c.start()
+    c.wait()
+
+
+def losses(
+    received_in, factor, wet, before,
+    gap, token,
+    received, rows, sems,
 ):
     del before
+    token[...] = jnp.zeros_like(token)
+    c = pltpu.make_async_copy(received_in, received, sems.at[0])
+    c.start()
+    c.wait()
+    partial = [jnp.zeros((8, LANES), F32) for _ in range(SUB)]
+    for half in range(CX // 16):
+        for j in range(OWN_TILES):
+            cols = slice(j * LANES, (j + 1) * LANES)
+            f = factor[half * 16 : half * 16 + 16, cols]
+            for t in range(SUB):
+                p = f * received[t, half * 16 : half * 16 + 16, cols].astype(F32)
+                partial[t] += p[:8] + p[8:]
+    row, lane = iotas()
+    total = jnp.zeros((8, LANES), F32)
+    for t, value in enumerate(partial):
+        total = jnp.where(row == t, jnp.sum(value, axis=0, keepdims=True), total)
+    total = jnp.sum(total, axis=1, keepdims=True)
+    total = jnp.sum(jnp.where(row == lane, total, 0.0), axis=0, keepdims=True) + wet[...]
+    for k in range(rows.shape[0]):
+        rows[k] = total
+    c = pltpu.make_async_copy(rows, gap, sems.at[1])
+    c.start()
+    c.wait()
+
+
+def edge_slots():
+    for t, tile, start in ((0, 0, 0), (2, 0, 5), (1, 1, 0), (3, 1, 4), (4, 1, 6)):
+        yield t, SUB - 1 - t, tile, start
+
+
+def regrid(
+    src, pat, received_in, weights_in, before,
+    out, top, bottom,
+    x, y, received, weights, sems,
+):
+    del before
+    reads = [
+        pltpu.make_async_copy(received_in, received, sems.at[0]),
+        pltpu.make_async_copy(weights_in, weights, sems.at[1]),
+    ]
+    for c in reads:
+        c.start()
+    reads[0].wait()
     for half in range(CX // 16):
         for j in range(OWN_TILES):
             cols = slice(j * LANES, (j + 1) * LANES)
@@ -445,61 +551,49 @@
                     row = half * 16 + part * 8
                     start = (row * OWN_TILES + j) * 8 + t
                     x[pl.ds(start, 8, stride=OWN_TILES * 8), :] = v16[part * 8 : part * 8 + 8]
-
-    @pl.loop(0, BLOCKS, unroll=32)
-    def _(q):
-        a, w = [], []
-        for k in range(2):
-            entry = table[q * 2 + k]
-            start = pl.multiple_of((entry // PATTERNS) * 8, 8)
-            a.append(x[pl.ds(start, 8), :].astype(BF16))
-            w.append(weights[entry % PATTERNS])
-        r = jnp.dot(
-            jnp.concatenate(a, 1), jnp.concatenate(w, 0), preferred_element_type=F32
-        )
-        y[pl.ds(q, 8, stride=BLOCKS), :] = r
-
-    partial = [jnp.zeros((8, LANES), F32) for _ in range(SUB)]
-    wet = jnp.zeros((8, LANES), F32)
-    for half in range(CX // 16):
+    reads[1].wait()
+
+    @pl.loop(0, CX, unroll=8)
+    def _(r):
+        for j in range(OWN_TILES):
+            a, w = [], []
+            for k in range(2):
+                start = pl.multiple_of(src[j, k, r] * 8, 8)
+                a.append(x[pl.ds(start, 8), :].astype(BF16))
+                w.append(weights[pat[j, k, r]])
+            product = jnp.dot(
+                jnp.concatenate(a, 1), jnp.concatenate(w, 0), preferred_element_type=F32
+            )
+            y[pl.ds(r * OWN_TILES + j, 8, stride=BLOCKS), :] = product
+
+    for part in range(CX // 8):
         for j in range(OWN_TILES):
             cols = slice(j * LANES, (j + 1) * LANES)
-            masks = []
-            for part in range(2):
-                row = half * 16 + part * 8
-                masks.append(mask[row : row + 8, cols].astype(F32))
-                wet += masks[-1]
             for t in range(SUB):
-                v16 = received[t, half * 16 : half * 16 + 16, cols].astype(F32)
-                for part in range(2):
-                    row = half * 16 + part * 8
-                    start = t * BLOCKS + row * OWN_TILES + j
-                    v = y[pl.ds(start, 8, stride=OWN_TILES), :]
-                    out[t, row : row + 8, cols] = v
-                    partial[t] += masks[part] * (v16[part * 8 : part * 8 + 8] - v)
-                    if t < SUB - 1 and row == 0:
-                        top[t, :, cols] = v
-                    if t < SUB - 1 and row == CX - 8:
-                        bottom[t, :, cols] = v
-    row, lane = iotas()
-    total = jnp.zeros((8, LANES), F32)
-    for t, value in enumerate([*partial, wet]):
-        total = jnp.where(row == t, jnp.sum(value, axis=0, keepdims=True), total)
-    total = jnp.sum(total, axis=1, keepdims=True)
-    total = jnp.sum(jnp.where(row == lane, total, 0.0), axis=0, keepdims=True)
-    for k in range(gap.shape[0]):
-        gap[k] = total
-
-
-def pack_second(out, upper, lower, one, three):
+                start = t * BLOCKS + part * 8 * OWN_TILES + j
+                out[t, part * 8 : part * 8 + 8, cols] = y[pl.ds(start, 8, stride=OWN_TILES), :]
+    top[1, 7:8, :] = jnp.zeros((1, CY), F32)
+    bottom[1, 7:8, :] = jnp.zeros((1, CY), F32)
+    for t, n, tile, start in edge_slots():
+        top[tile, start : start + n, :] = out[t, 0:n, :]
+        bottom[tile, start : start + n, :] = out[t, CX - n : CX, :]
+
+
+def halo_rows(halo, upper, lower):
+    halo[...] = jnp.zeros_like(halo)
+    for t, n, tile, start in edge_slots():
+        halo[t, 8 - n : 8, :] = upper[tile, start : start + n, :]
+        halo[t, 8 : 8 + n, :] = lower[tile, start : start + n, :]
+
+
+def pack_second(out, upper, lower, one, three, halo):
     even, _, _ = position()
+    halo_rows(halo, upper, lower)
 
     def field(t):
         def of(tile):
-            if tile == 0:
-                block, rows = upper.at[t], slice(0, 8)
-            elif tile == 5:
-                block, rows = lower.at[t], slice(0, 8)
+            if tile in (0, 5):
+                block, rows = halo.at[t], slice(0, 8) if tile == 0 else slice(8, 16)
             else:
                 block, rows = out.at[t], slice(tile * 8 - 8, tile * 8)
             return block[rows, :LANES], block[rows, CY - LANES :]
@@ -519,22 +613,25 @@
 
 
 def second_cone(
-    diff, mix, fixed_in, regridded, upper, lower, one, three, gap, hs_in, us_in,
-    series, final0, hx, ux,
-    s0, s1, g, emitted, fixed, hs, us, sems,
+    coeff_in, fixed_in, regridded, upper, lower, one, three, gap, hs_in, us_in,
+    series, final0, hx, ux, coeff_out,
+    s0, s1, g, emitted, fixed, hs, us, halo, coeff, sems,
 ):
+    diff, mix = coefficients(coeff)
     reads = []
-    for i, (src, dst) in enumerate(((us_in, us), (fixed_in, fixed), (hs_in, hs))):
+    pairs = ((us_in, us), (fixed_in, fixed), (coeff_in, coeff), (hs_in, hs))
+    for i, (src, dst) in enumerate(pairs):
         reads.append(pltpu.make_async_copy(src, dst, sems.at[i]))
         reads[-1].start()
     even, first, last = position()
     ocean = lax.axis_index("comp") == 1
     zero_pads(s0, 3)
     zero_pads(s1, 3)
+    halo_rows(halo, upper, lower)
     for t in range(SUB):
         if t < SUB - 1:
-            g[t, 0:8, :CY] = upper[t]
-            g[t, 8 + CX : 16 + CX, :CY] = lower[t]
+            g[t, 0:8, :CY] = halo[t, 0:8, :]
+            g[t, 8 + CX : 16 + CX, :CY] = halo[t, 8:16, :]
         g[t, 8 : 8 + CX, :CY] = regridded[t]
 
     def put(f, tile, value):
@@ -545,6 +642,7 @@
     means = [jnp.broadcast_to(v, (8, LANES)) for v in gap_means(gap)]
     for c in reads:
         c.wait()
+    coeff_out[...] = coeff[...]
 
     for t in range(SUB):
         src, dst = (s0, s1) if t % 2 == 0 else (s1, s0)
@@ -586,11 +684,12 @@
 
 
 def second_rest(
-    diff, mix, hx, ux, hs_in, us_in, final0, whole,
+    coeff, hx, ux, hs_in, us_in, final0, whole,
     final, token,
     s0, s1, hs, us, sems,
 ):
     del whole
+    diff, mix = coefficients(coeff)
     reads = [
         pltpu.make_async_copy(us_in, us, sems.at[0]),
         pltpu.make_async_copy(hs_in, hs, sems.at[1]),
@@ -653,16 +752,18 @@
 ):
     state, guess, diff, mix, coupling = state[0], guess[0], diffusion[0], mixing[0], coupling[0]
     weights = weights[0]
-    table = (source_block[0] * PATTERNS + pattern[0]).reshape(2 * BLOCKS)
+    src = source_block[0].transpose(1, 2, 0)
+    pat = pattern[0].transpose(1, 2, 0)
     peers = lax.axis_size("gx") * lax.axis_size("gy")
     band = lambda n: shape(n, BAND, COLS)
     field_buf = lambda n: pltpu.VMEM((n, ROWS, COLS), F32)
     band_buf = lambda n: pltpu.VMEM((n, BAND, COLS), F32)
+    numbers = shape(2 * LEVELS, 8, LANES)
 
     message = shape(LEVELS, 8, CY)
-    to_lower, to_upper = call(
+    to_lower, to_upper, token = call(
         first_edges,
-        [message, message],
+        [message, message, shape(8, LANES)],
         [
             pltpu.VMEM((AUX, 8, CY), F32),
             pltpu.VMEM((AUX, 8, CY), F32),
@@ -670,35 +771,83 @@
             pltpu.VMEM((2, SUB - 1, 16, CY), BF16),
             pltpu.SemaphoreType.DMA((10,)),
         ],
-        [HBM] * 5 + [SM],
-    )(state, guess, coupling, land_temp, land_mask, table)
+        [HBM] * 5,
+        grant=EDGE_GRANT,
+    )(state, guess, coupling, land_temp, land_mask)
+    state, guess, coupling, land_temp, mask, table, src, pat, to_lower, to_upper = (
+        lax.optimization_barrier(
+            (
+                state, guess, coupling, land_temp, land_mask, weights, src, pat,
+                to_lower, to_upper,
+            )
+        )
+    )
     lower, upper = shifted(to_lower, "gx", -1), shifted(to_upper, "gx", 1)
+    factor, wet, coeff = call(
+        balance,
+        [shape(CX, CY), shape(1, LANES), shape(2 * LEVELS, 8, LANES)],
+        [
+            pltpu.VMEM((BLOCKS, LANES), F32),
+            pltpu.VMEM((PATTERNS, BLOCKS, LANES), F32),
+            pltpu.VMEM((BLOCKS, LANES), F32),
+            pltpu.VMEM((CX, CY), F32),
+            pltpu.SemaphoreType.DMA(()),
+        ],
+        [SM, SM, SM, SM, VM, VM, VM],
+        out_specs=[HBM, VM, VM],
+    )(diff, mix, src, pat, table, mask, token)
     packed = shape(BAND, PACK_LANES)
-    aux, one, three = call(pack_first, [shape(AUX, 16, CY), packed, packed], [], [VM] * 7)(
-        state, guess, coupling, land_temp, land_mask, upper, lower
+    aux, one, three = call(pack_first, [shape(AUX, 16, CY), packed, packed], [], [VM] * 8)(
+        state, guess, coupling, land_temp, mask, upper, lower, wet
     )
     one, three = paired(one, "gy", 1), paired(three, "gy", 3)
 
-    series, hd, ud, hs, us, fixed = call(
+    series, hd, ud, hs, us, fixed, numbers_out = call(
         first_cone,
-        [shape(SUB, CX, CY, dtype=BF16), band(SUB), band(SUB), band(3), band(3), band(3)],
+        [
+            shape(SUB, CX, CY, dtype=BF16), band(SUB), band(SUB),
+            band(3), band(3), band(3), numbers,
+        ],
         [
             field_buf(CONE), field_buf(CONE), band_buf(SUB), band_buf(SUB),
-            band_buf(3), band_buf(3), band_buf(3), pltpu.SemaphoreType.DMA((7,)),
+            band_buf(3), band_buf(3), band_buf(3), pltpu.SemaphoreType.DMA((8,)),
         ],
-        [SM, SM] + [VM] * 10,
-        out_specs=[VM] * 3 + [HBM] * 3,
-    )(diff, mix, state, guess, coupling, land_temp, land_mask, upper, lower, aux, one, three)
+        [VM] * 11,
+        out_specs=[VM] * 3 + [HBM] * 4,
+    )(coeff, state, guess, coupling, land_temp, mask, upper, lower, aux, one, three)
 
     def exchange(series, before):
         received = paired(series, "comp", 1)
-        edges = shape(SUB - 1, 8, CY)
-        out, top, bottom, gap = call(
+        gap, after = call(
+            losses,
+            [shape(peers, 1, LANES), shape(8, LANES)],
+            [
+                pltpu.VMEM((SUB, CX, CY), BF16),
+                pltpu.VMEM((peers, 1, LANES), F32),
+                pltpu.SemaphoreType.DMA((2,)),
+            ],
+            [HBM, VM, VM, VM],
+            out_specs=[HBM, VM],
+        )(received, factor, wet, before)
+        gap = lax.all_to_all(gap, ("gx", "gy"), 0, 0)
+        edges = shape(2, 8, CY)
+        out, top, bottom = call(
             regrid,
-            [shape(SUB, CX, CY), edges, edges, shape(peers, 1, LANES)],
-            [pltpu.VMEM((BLOCKS * 8, LANES), F32), pltpu.VMEM((BLOCKS * 8, LANES), F32)],
-            [SM, VM, VM, VM, VM],
-        )(table, received, weights, land_mask, before)
+            [shape(SUB, CX, CY), edges, edges],
+            [
+                pltpu.VMEM((BLOCKS * 8, LANES), F32),
+                pltpu.VMEM((BLOCKS * 8, LANES), F32),
+                pltpu.VMEM((SUB, CX, CY), BF16),
+                pltpu.VMEM((PATTERNS, LANES, LANES), BF16),
+                pltpu.SemaphoreType.DMA((2,)),
+            ],
+            [SM, SM, HBM, HBM, VM],
+            cost_estimate=pl.CostEstimate(
+                flops=2 * BLOCKS * 8 * 2 * LANES * LANES,
+                bytes_accessed=BLOCKS * 2 * LANES * LANES * 2,
+                transcendentals=0,
+            ),
+        )(src, pat, received, weights, after)
         return out, top, bottom, gap
 
     whole, hs_rest, us_rest, token = call(
@@ -708,26 +857,28 @@
             field_buf(LEVELS), field_buf(LEVELS),
             band_buf(3), band_buf(3), pltpu.SemaphoreType.DMA((2,)),
         ],
-        [SM, SM] + [VM] * 7,
+        [VM] * 8,
         out_specs=[VM, HBM, HBM, VM],
-    )(diff, mix, state, upper, lower, one, three, hd, ud)
+    )(coeff, state, upper, lower, one, three, hd, ud)
 
     out, top, bottom, gap = exchange(series, token)
     lower, upper = shifted(top, "gx", -1), shifted(bottom, "gx", 1)
-    gap = lax.all_to_all(gap, ("gx", "gy"), 0, 0)
     packed = shape(BAND, LANES)
-    one, three = call(pack_second, [packed, packed], [], [VM] * 3)(out, upper, lower)
+    one, three = call(
+        pack_second, [packed, packed], [pltpu.VMEM((SUB - 1, 16, CY), F32)], [VM] * 3
+    )(out, upper, lower)
     one, three = paired(one, "gy", 1), paired(three, "gy", 3)
 
-    series, final0, hx, ux = call(
+    series, final0, hx, ux, coeff = call(
         second_cone,
-        [shape(SUB, CX, CY, dtype=BF16), shape(CX, CY), band(3), band(3)],
+        [shape(SUB, CX, CY, dtype=BF16), shape(CX, CY), band(3), band(3), numbers],
         [
             field_buf(3), field_buf(3), band_buf(SUB), band_buf(SUB),
-            band_buf(3), band_buf(3), band_buf(3), pltpu.SemaphoreType.DMA((3,)),
+            band_buf(3), band_buf(3), band_buf(3), pltpu.VMEM((SUB - 1, 16, CY), F32),
+            pltpu.VMEM(numbers.shape, F32), pltpu.SemaphoreType.DMA((4,)),
         ],
-        [SM, SM, HBM] + [VM] * 6 + [HBM, HBM],
-    )(diff, mix, fixed, out, upper, lower, one, three, gap, hs, us)
+        [HBM, HBM] + [VM] * 6 + [HBM, HBM],
+    )(numbers_out, fixed, out, upper, lower, one, three, gap, hs, us)
 
     whole, token = call(
         second_rest,
@@ -736,14 +887,13 @@
             field_buf(SUB), field_buf(SUB),
             band_buf(3), band_buf(3), pltpu.SemaphoreType.DMA((2,)),
         ],
-        [SM, SM, VM, VM, HBM, HBM, VM, pl.BlockSpec(memory_space=pl.ANY)],
+        [VM, VM, VM, HBM, HBM, VM, pl.BlockSpec(memory_space=pl.ANY)],
         out_specs=[pl.BlockSpec((SUB, CX, CY), lambda i: (0, 0, 0)), VM],
         grid=(1,),
-        input_output_aliases={7: 0},
-    )(diff, mix, hx, ux, hs_rest, us_rest, final0, whole)
+        input_output_aliases={6: 0},
+    )(coeff, hx, ux, hs_rest, us_rest, final0, whole)
 
     out, _, _, gap = exchange(series, token)
-    gap = lax.all_to_all(gap, ("gx", "gy"), 0, 0)
     (forcing,) = call(finish, [shape(SUB, CX, CY)], [], [VM] * 3)(out, land_mask, gap)
     return whole[None], forcing[None]
 

time: 90.6 us -> 87.1 us (0.961)
  blocking collectives: 14.6 us -> 0 us
  Pallas kernels: 25.3 us -> 32.5 us
  starting transfers between devices: 26.6 us -> 33.5 us
  waiting for transfers between devices: 16.5 us -> 14.7 us
    all_to_all x1 -> x0, blocking collectives: 14.6 us -> none  [per_device(): gap = lax.all_to_all(gap, ('gx', 'gy'), 0, 0)]
    pallas_call x5 -> x8, Pallas kernels: 9.56 us -> 18.7 us  [the longest x1 6.8 us: per_device(): call(balance, [shape(CX, CY), shape(1, LANES), shape(2 * LEVELS, 8, LANES...]
    all_to_all x1 -> x2, starting transfers between devices: 5.02 us -> 11.8 us  [exchange(): gap = lax.all_to_all(gap, ('gx', 'gy'), 0, 0)]
    ppermute x4, waiting for transfers between devices: 5.96 us -> 0.01 us  [shifted(): return lax.ppermute(value, axis, [(i, (i + by) % n) for i in range(n)])]
    all_to_all x1 -> x2, waiting for transfers between devices: 5.29 us -> 9.32 us  [exchange(): gap = lax.all_to_all(gap, ('gx', 'gy'), 0, 0)]
    unnamed x20 -> x32, local copies, waits for them, and re-layouts: 5.52 us -> 5.13 us
  transfers between devices with their start and end apart: 11 -> 12, of which waited for: 4 -> 4; matrix products, arithmetic and copies ran while one was open for 0% -> 0% of each run, Pallas kernels for 10% -> 21%
where the time goes in v4:
time: 87.1 us; the launch traced here: 86.7 us
  starting transfers between devices  33.5 us (38%)
  Pallas kernels  32.5 us (37%)
  waiting for transfers between devices  14.7 us (17%)
  local copies, waits for them, and re-layouts  5.13 us (6%)
  between operations  0.89 us (1%)
    all_to_all x2, starting transfers between devices, exchange(): gap = lax.all_to_all(gap, ('gx', 'gy'), 0, 0)  11.8 us
    ppermute x4, starting transfers between devices, shifted(): return lax.ppermute(value, axis, [(i, (i + by) % n) for i in range(n)])  11.8 us
    ppermute x6, starting transfers between devices, paired(): lax.ppermute(value, axis, [(i, i ^ mask) for i in range(lax.axis_size(axi...  9.92 us
    all_to_all x2, waiting for transfers between devices, exchange(): gap = lax.all_to_all(gap, ('gx', 'gy'), 0, 0)  9.32 us
    pallas_call x1, Pallas kernels, per_device(): call(balance, [shape(CX, CY), shape(1, LANES), shape(2 * LEVELS, 8, LANES...  6.8 us
    pallas_call x2, Pallas kernels, exchange(): call(regrid, [shape(SUB, CX, CY), edges, edges], [pltpu.VMEM((BLOCKS * 8,...  6.59 us
    pallas_call x1, Pallas kernels, per_device(): call(first_rest, [shape(LEVELS, CX, CY), band(3), band(3), shape(8, LANES...  5.7 us
    ppermute x6, waiting for transfers between devices, paired(): lax.ppermute(value, axis, [(i, i ^ mask) for i in range(lax.axis_size(axi...  5.36 us
  transfers between devices with their start and end apart: 12, of which 4 were waited for; matrix products, arithmetic and copies ran while one was open for 0% of the time, Pallas kernels for 21%

profile of v4, /device:TPU:1, one launch (start us, length us, event | category | flops | bytes accessed | tf_op | source)
XLA Modules:
  0.0 86.7 jit_solution(14209383163232617568)
XLA Ops:
  0.6 2.2 %shard_map.113 = (f32[16,8,512]{2,1,0:T(8,128)}, f32[16,8,512]{2,1,0:T(8,128)}, f32[8,128]{1,0:T(8,128)}) custom-call(f32[16,32,512]{2,1,0:T(8,128)} %bitcast.14, bf16[6,32,512]{2,1,0:T(8,128)(2,1)} %bitcast.21, f32[32,512]{1,0:T(8,128)} %bitcast.24, f32[32,512]{1,0:T(8,128)} %land.3, s32[32,512]{1,0:T(8,128)} %mask.6), custom_call_target="tpu_custom_call" | custom-call | tf_op jit(solution)/shard_map/pallas_call | solution.py:764
  2.9 2.1 %collective-permute-start = (f32[16,8,512]{2,1,0:T(8,128)}, f32[16,8,512]{2,1,0:T(8,128)S(1)}, u32[]{:S(2)}, u32[]{:S(2)}) collective-permute-start(f32[16,8,512]{2,1,0:T(8,128)} %get-tuple-element.61), channel_id=1, source_target_pairs={{0,4},{4,8},{8,12},{12,16},{16,20},{20,24},{24,28},{28,32},{32,36}... | collective-permute-start | bytes 786440 | tf_op jit(solution)/shard_map/ppermute | solution.py:743
  5.0 4.8 %collective-permute-start.1 = (f32[16,8,512]{2,1,0:T(8,128)}, f32[16,8,512]{2,1,0:T(8,128)S(1)}, u32[]{:S(2)}, u32[]{:S(2)}) collective-permute-start(f32[16,8,512]{2,1,0:T(8,128)} %get-tuple-element.62), channel_id=1, source_target_pairs={{0,60},{4,0},{8,4},{12,8},{16,12},{20,16},{24,20},{28,24},{32,28},... | collective-permute-start | bytes 786440 | tf_op jit(solution)/shard_map/ppermute | solution.py:743
  14.0 6.8 %shard_map.114 = (f32[32,512]{1,0:T(8,128)S(1)}, f32[1,128]{1,0:T(1,128)S(1)}, f32[32,8,128]{2,1,0:T(8,128)S(1)}) custom-call(f32[16]{0:T(128)S(1)} %bitcast.33, f32[15]{0:T(128)S(1)} %bitcast.34, s32[4,2,32]{2,1,0:T(2,128)S(1)} %bitcast.27, s32[4,2,32]{2,1,0:T(2,128)S(1)} %bitcast.30, bf16[32,128,128]{2,1,0:T(8,128)(2,1)S(1)} %bitcast.18, ...), custom_call_target="tpu_custom_call" | custom-call | tf_op jit(solution)/shard_map/pallas_call | solution.py:786
  21.2 1.0 %collective-permute-start.2 = (f32[48,256]{1,0:T(8,128)S(1)}, f32[48,256]{1,0:T(8,128)S(1)}, u32[]{:S(2)}, u32[]{:S(2)}) collective-permute-start(f32[48,256]{1,0:T(8,128)S(1)} %get-tuple-element.65), channel_id=1, source_target_pairs={{0,1},{1,0},{2,3},{3,2},{4,5},{5,4},{6,7},{7,6},{8,9},{9,8},{10,11... | collective-permute-start | bytes 147464 | tf_op jit(solution)/shard_map/ppermute | solution.py:747
  22.2 1.3 %collective-permute-start.3 = (f32[48,256]{1,0:T(8,128)S(1)}, f32[48,256]{1,0:T(8,128)S(1)}, u32[]{:S(2)}, u32[]{:S(2)}) collective-permute-start(f32[48,256]{1,0:T(8,128)S(1)} %get-tuple-element.66), channel_id=1, source_target_pairs={{0,3},{1,2},{2,1},{3,0},{4,7},{5,6},{6,5},{7,4},{8,11},{9,10},{10,... | collective-permute-start | bytes 147464 | tf_op jit(solution)/shard_map/ppermute | solution.py:747
  23.5 2.3 %collective-permute-done.3.three = f32[48,256]{1,0:T(8,128)S(1)} collective-permute-done((f32[48,256]{1,0:T(8,128)S(1)}, f32[48,256]{1,0:T(8,128)S(1)}, u32[]{:S(2)}, u32[]{:S(2)}) %collective-permute-start.3) | collective-permute-done | bytes 49184 | tf_op jit(solution)/shard_map/ppermute | solution.py:747
  25.8 3.9 %shard_map.116 = (bf16[6,32,512]{2,1,0:T(8,128)(2,1)S(1)}, f32[6,48,640]{2,1,0:T(8,128)S(1)}, f32[6,48,640]{2,1,0:T(8,128)S(1)}, f32[3,48,640]{2,1,0:T(8,128)S(1...) custom-call(f32[32,8,128]{2,1,0:T(8,128)S(1)} %get-tuple-element.56.coeff, ...), custom_call_target="tpu_custom_call" | custom-call | tf_op jit(solution)/shard_map/pallas_call | solution.py:805
  29.7 3.0 %collective-permute-start.4 = (bf16[6,32,512]{2,1,0:T(8,128)(2,1)S(1)}, bf16[6,32,512]{2,1,0:T(8,128)(2,1)S(1)}, u32[]{:S(2)}, u32[]{:S(2)}) collective-permute-start(bf16[6,32,512]{2,1,0:T(8,128)(2,1)S(1)} %get-tuple-element.69), channel_id=1, source_target_pairs={{0,64},{64,0},{1,65},{65,1},{2,66},{66,2},{3,67},{67,3},{4,68},{68... | collective-permute-start | bytes 589832 | tf_op jit(solution)/shard_map/ppermute | solution.py:747
  32.7 5.7 %shard_map.117 = (f32[16,32,512]{2,1,0:T(8,128)}, f32[3,48,640]{2,1,0:T(8,128)S(1)}, f32[3,48,640]{2,1,0:T(8,128)S(1)}, f32[8,128]{1,0:T(8,128)S(1)}) custom-call(f32[32,8,128]{2,1,0:T(8,128)S(1)} %get-tuple-element.56.coeff, f32[16,32,512]{2,1,0:T(8,128)S(1)} %bitcast.17, f32[16,8,512]{2,1,0:T(8,128)S(1)} %collective-permute-done.upper, ...), custom_call_target="tpu_custom_call" | custom-call | tf_op jit(solution)/shard_map/pallas_call | solution.py:853
  38.5 1.0 %shard_map.118 = (f32[64,1,128]{2,1,0:T(1,128)}, f32[8,128]{1,0:T(8,128)S(1)}) custom-call(bf16[6,32,512]{2,1,0:T(8,128)(2,1)S(1)} %collective-permute-done.4.received_in, f32[32,512]{1,0:T(8,128)S(1)} %get-tuple-element.70.factor, f32[1,128]{1,0:T(1,128)S(1)} %get-tuple-element.63.before.wet, f32[8,128]{1,0:T(8,128)S(1)} %get-tuple-element.73.before), custom_call_target="tpu_custom_call" | custom-call | tf_op jit(solution)/shard_map/pallas_call | solution.py:821
  39.5 3.0 %shard_map.119 = (f32[6,32,512]{2,1,0:T(8,128)S(1)}, f32[2,8,512]{2,1,0:T(8,128)S(1)}, f32[2,8,512]{2,1,0:T(8,128)S(1)}) custom-call(s32[4,2,32]{2,1,0:T(2,128)S(1)} %bitcast.28, s32[4,2,32]{2,1,0:T(2,128)S(1)} %bitcast.31, bf16[6,32,512]{2,1,0:T(8,128)(2,1)S(1)} %collective-permute-done.4.received_in, bf16[32,128,128]{2,1,0:T(8,128)(2,1)S(1)} %bitcast.19, ...), custom_call_target="tpu_custom_call" | custom-call | flops 67108864 | bytes 8388608 | tf_op jit(solution)/shard_map/pallas_call | solution.py:834
  42.6 4.8 %collective-permute-start.6 = (f32[2,8,512]{2,1,0:T(8,128)S(1)}, f32[2,8,512]{2,1,0:T(8,128)S(1)}, u32[]{:S(2)}, u32[]{:S(2)}) collective-permute-start(f32[2,8,512]{2,1,0:T(8,128)S(1)} %get-tuple-element.77), channel_id=1, source_target_pairs={{0,60},{4,0},{8,4},{12,8},{16,12},{20,16},{24,20},{28,24},{32,28},... | collective-permute-start | bytes 98312 | tf_op jit(solution)/shard_map/ppermute | solution.py:743
  47.4 5.1 %all-to-all-start = ((f32[64,1,128]{2,1,0:T(1,128)}), f32[64,1,128]{2,1,0:T(1,128)S(1)}, u32[]{:S(2)}, u32[]{:S(2)}) async-start(f32[64,1,128]{2,1,0:T(1,128)} %get-tuple-element.80), calls=%async_computation | async-start | bytes 65536 | tf_op jit(solution)/shard_map/all_to_all | solution.py:832
  53.8 1.2 %collective-permute-start.8 = (f32[48,128]{1,0:T(8,128)S(1)}, f32[48,128]{1,0:T(8,128)S(1)}, u32[]{:S(2)}, u32[]{:S(2)}) collective-permute-start(f32[48,128]{1,0:T(8,128)S(1)} %get-tuple-element.79), channel_id=1, source_target_pairs={{0,3},{1,2},{2,1},{3,0},{4,7},{5,6},{6,5},{7,4},{8,11},{9,10},{10,... | collective-permute-start | bytes 73736 | tf_op jit(solution)/shard_map/ppermute | solution.py:747
  55.0 5.3 %all-to-all-done.gap = f32[64,1,128]{2,1,0:T(1,128)S(1)} async-done(((f32[64,1,128]{2,1,0:T(1,128)}), f32[64,1,128]{2,1,0:T(1,128)S(1)}, u32[]{:S(2)}, u32[]{:S(2)}) %all-to-all-start) | async-done | bytes 32800 | tf_op jit(solution)/shard_map/all_to_all | solution.py:832
  61.2 1.8 %shard_map.121 = (bf16[6,32,512]{2,1,0:T(8,128)(2,1)S(1)}, f32[32,512]{1,0:T(8,128)S(1)}, f32[3,48,640]{2,1,0:T(8,128)S(1)}, f32[3,48,640]{2,1,0:T(8,128)S(1)}, f32[32,8,128]{2,1,0:T(8,128)S(1)}) custom-call(f32[32,8,128]{2,1,0:T(8,128)S(1)} %copy-done.8, f32[3,48,640]{2,1,0:T(8,128)S(1)} %get-tuple-element.68.fixed_in, ...), custom_call_target="tpu_custom_call" | custom-call | tf_op jit(solution)/shard_map/pallas_call | solution.py:872
  63.1 2.8 %collective-permute-start.9 = (bf16[6,32,512]{2,1,0:T(8,128)(2,1)S(1)}, bf16[6,32,512]{2,1,0:T(8,128)(2,1)S(1)}, u32[]{:S(2)}, u32[]{:S(2)}) collective-permute-start(bf16[6,32,512]{2,1,0:T(8,128)(2,1)S(1)} %get-tuple-element.91), channel_id=1, source_target_pairs={{0,64},{64,0},{1,65},{65,1},{2,66},{66,2},{3,67},{67,3},{4,68},{68... | collective-permute-start | bytes 589832 | tf_op jit(solution)/shard_map/ppermute | solution.py:747
  65.9 1.4 %shard_map.122 = (f32[16,32,512]{2,1,0:T(8,128)}, f32[8,128]{1,0:T(8,128)S(1)}) custom-call(f32[32,8,128]{2,1,0:T(8,128)S(1)} %get-tuple-element.83.coeff, f32[3,48,640]{2,1,0:T(8,128)S(1)} %get-tuple-element.84.hx, f32[3,48,640]{2,1,0:T(8,128)S(1)} %get-tuple-element.85.ux, ...), custom_call_target="tpu_custom_call", output_to_operand_aliasing={{0}: (6, {})} | custom-call | tf_op jit(solution)/shard_map/pallas_call | solution.py:883
  67.2 3.1 %collective-permute-done.9.received_in = bf16[6,32,512]{2,1,0:T(8,128)(2,1)S(1)} collective-permute-done((bf16[6,32,512]{2,1,0:T(8,128)(2,1)S(1)}, bf16[6,32,512]{2,1,0:T(8,128)(2,1)S(1)}, u32[]{:S(2)}, u32[]{:S(2)}) %collective-permute-start.9) | collective-permute-done | bytes 196640 | tf_op jit(solution)/shard_map/ppermute | solution.py:747
  70.3 1.0 %shard_map.123 = (f32[64,1,128]{2,1,0:T(1,128)}, f32[8,128]{1,0:T(8,128)S(1)}) custom-call(bf16[6,32,512]{2,1,0:T(8,128)(2,1)S(1)} %collective-permute-done.9.received_in, f32[32,512]{1,0:T(8,128)S(1)} %get-tuple-element.70.factor, f32[1,128]{1,0:T(1,128)S(1)} %get-tuple-element.63.before.wet, f32[8,128]{1,0:T(8,128)S(1)} %get-tuple-element.92.before), custom_call_target="tpu_custom_call" | custom-call | tf_op jit(solution)/shard_map/pallas_call | solution.py:821
  71.4 6.7 %all-to-all-start.1 = ((f32[64,1,128]{2,1,0:T(1,128)}), f32[64,1,128]{2,1,0:T(1,128)S(1)}, u32[]{:S(2)}, u32[]{:S(2)}) async-start(f32[64,1,128]{2,1,0:T(1,128)} %get-tuple-element.95), calls=%async_computation.1 | async-start | bytes 65536 | tf_op jit(solution)/shard_map/all_to_all | solution.py:832
  78.2 3.6 %shard_map.124 = (f32[6,32,512]{2,1,0:T(8,128)S(1)}, f32[2,8,512]{2,1,0:T(8,128)}, f32[2,8,512]{2,1,0:T(8,128)}) custom-call(s32[4,2,32]{2,1,0:T(2,128)S(1)} %bitcast.29, s32[4,2,32]{2,1,0:T(2,128)S(1)} %bitcast.32, bf16[6,32,512]{2,1,0:T(8,128)(2,1)S(1)} %collective-permute-done.9.received_in, bf16[32,128,128]{2,1,0:T(8,128)(2,1)S(1)} %bitcast.20, ...), custom_call_target="tpu_custom_call" | custom-call | flops 67108864 | bytes 8388608 | tf_op jit(solution)/shard_map/pallas_call | solution.py:834
  81.8 4.0 %all-to-all-done.1.gap = f32[64,1,128]{2,1,0:T(1,128)S(1)} async-done(((f32[64,1,128]{2,1,0:T(1,128)}), f32[64,1,128]{2,1,0:T(1,128)S(1)}, u32[]{:S(2)}, u32[]{:S(2)}) %all-to-all-start.1) | async-done | bytes 32800 | tf_op jit(solution)/shard_map/all_to_all | solution.py:832
  (45 shorter events, 7.8 us)
Async XLA Ops:
  0.6 9.2 %copy-start.1 = (bf16[1,32,128,128]{3,2,1,0:T(8,128)(2,1)S(1)}, bf16[1,32,128,128]{3,2,1,0:T(8,128)(2,1)}, u32[]{:S(2)}) copy-start(bf16[1,32,128,128]{3,2,1,0:T(8,128)(2,1)} %param.17) | copy-start | bytes 3145732
  0.6 20.2 %copy-start = (f32[1,16,32,512]{3,2,1,0:T(8,128)S(1)}, f32[1,16,32,512]{3,2,1,0:T(8,128)}, u32[]{:S(2)}) copy-start(f32[1,16,32,512]{3,2,1,0:T(8,128)} %param.10) | copy-start | bytes 3145732
  2.9 17.9 %collective-permute-start = (f32[16,8,512]{2,1,0:T(8,128)}, f32[16,8,512]{2,1,0:T(8,128)S(1)}, u32[]{:S(2)}, u32[]{:S(2)}) collective-permute-start(f32[16,8,512]{2,1,0:T(8,128)} %get-tuple-element.61), channel_id=1, source_target_pairs={{0,4},{4,8},{8,12},{12,16},{16,20},{20,24},{24,28},{28,32},{32,36}... | collective-permute-start | bytes 786440 | tf_op jit(solution)/shard_map/ppermute | solution.py:743
  5.0 15.8 %collective-permute-start.1 = (f32[16,8,512]{2,1,0:T(8,128)}, f32[16,8,512]{2,1,0:T(8,128)S(1)}, u32[]{:S(2)}, u32[]{:S(2)}) collective-permute-start(f32[16,8,512]{2,1,0:T(8,128)} %get-tuple-element.62), channel_id=1, source_target_pairs={{0,60},{4,0},{8,4},{12,8},{16,12},{20,16},{24,20},{28,24},{32,28},... | collective-permute-start | bytes 786440 | tf_op jit(solution)/shard_map/ppermute | solution.py:743
  9.8 0.8 copy-start.3
  10.6 0.7 copy-start.9
  14.0 6.8 %copy-start.2 = (bf16[1,6,32,512]{3,2,1,0:T(8,128)(2,1)S(1)}, bf16[1,6,32,512]{3,2,1,0:T(8,128)(2,1)}, u32[]{:S(2)}) copy-start(bf16[1,6,32,512]{3,2,1,0:T(8,128)(2,1)} %param.11) | copy-start | bytes 589828
  14.0 6.9 %copy-start.5 = (f32[1,32,512]{2,1,0:T(8,128)S(1)}, f32[1,32,512]{2,1,0:T(8,128)}, u32[]{:S(2)}) copy-start(f32[1,32,512]{2,1,0:T(8,128)} %param.14) | copy-start | bytes 196612
  14.0 6.9 %copy-start.6 = (f32[32,512]{1,0:T(8,128)S(1)}, f32[32,512]{1,0:T(8,128)}, u32[]{:S(2)}) copy-start(f32[32,512]{1,0:T(8,128)} %land.3) | copy-start | bytes 196612
  21.2 2.3 %collective-permute-start.2 = (f32[48,256]{1,0:T(8,128)S(1)}, f32[48,256]{1,0:T(8,128)S(1)}, u32[]{:S(2)}, u32[]{:S(2)}) collective-permute-start(f32[48,256]{1,0:T(8,128)S(1)} %get-tuple-element.65), channel_id=1, source_target_pairs={{0,1},{1,0},{2,3},{3,2},{4,5},{5,4},{6,7},{7,6},{8,9},{9,8},{10,11... | collective-permute-start | bytes 147464 | tf_op jit(solution)/shard_map/ppermute | solution.py:747
  22.2 3.5 %collective-permute-start.3 = (f32[48,256]{1,0:T(8,128)S(1)}, f32[48,256]{1,0:T(8,128)S(1)}, u32[]{:S(2)}, u32[]{:S(2)}) collective-permute-start(f32[48,256]{1,0:T(8,128)S(1)} %get-tuple-element.66), channel_id=1, source_target_pairs={{0,3},{1,2},{2,1},{3,0},{4,7},{5,6},{6,5},{7,4},{8,11},{9,10},{10,... | collective-permute-start | bytes 147464 | tf_op jit(solution)/shard_map/ppermute | solution.py:747
  29.7 8.7 %copy-start.7 = (f32[32,8,128]{2,1,0:T(8,128)}, f32[32,8,128]{2,1,0:T(8,128)S(1)}, u32[]{:S(2)}) copy-start(f32[32,8,128]{2,1,0:T(8,128)S(1)} %get-tuple-element.67.coeff_in) | copy-start | bytes 393220
  29.7 8.7 %collective-permute-start.4 = (bf16[6,32,512]{2,1,0:T(8,128)(2,1)S(1)}, bf16[6,32,512]{2,1,0:T(8,128)(2,1)S(1)}, u32[]{:S(2)}, u32[]{:S(2)}) collective-permute-start(bf16[6,32,512]{2,1,0:T(8,128)(2,1)S(1)} %get-tuple-element.69), channel_id=1, source_target_pairs={{0,64},{64,0},{1,65},{65,1},{2,66},{66,2},{3,67},{67,3},{4,68},{68... | collective-permute-start | bytes 589832 | tf_op jit(solution)/shard_map/ppermute | solution.py:747
  42.5 9.9 %collective-permute-start.5 = (f32[2,8,512]{2,1,0:T(8,128)S(1)}, f32[2,8,512]{2,1,0:T(8,128)S(1)}, u32[]{:S(2)}, u32[]{:S(2)}) collective-permute-start(f32[2,8,512]{2,1,0:T(8,128)S(1)} %get-tuple-element.76), channel_id=1, source_target_pairs={{0,4},{4,8},{8,12},{12,16},{16,20},{20,24},{24,28},{28,32},{32,36}... | collective-permute-start | bytes 98312 | tf_op jit(solution)/shard_map/ppermute | solution.py:743
  42.6 9.9 %collective-permute-start.6 = (f32[2,8,512]{2,1,0:T(8,128)S(1)}, f32[2,8,512]{2,1,0:T(8,128)S(1)}, u32[]{:S(2)}, u32[]{:S(2)}) collective-permute-start(f32[2,8,512]{2,1,0:T(8,128)S(1)} %get-tuple-element.77), channel_id=1, source_target_pairs={{0,60},{4,0},{8,4},{12,8},{16,12},{20,16},{24,20},{28,24},{32,28},... | collective-permute-start | bytes 98312 | tf_op jit(solution)/shard_map/ppermute | solution.py:743
  47.4 12.9 %all-to-all-start = ((f32[64,1,128]{2,1,0:T(1,128)}), f32[64,1,128]{2,1,0:T(1,128)S(1)}, u32[]{:S(2)}, u32[]{:S(2)}) async-start(f32[64,1,128]{2,1,0:T(1,128)} %get-tuple-element.80), calls=%async_computation | async-start | bytes 65536 | tf_op jit(solution)/shard_map/all_to_all | solution.py:832
  53.2 7.1 %collective-permute-start.7 = (f32[48,128]{1,0:T(8,128)}, f32[48,128]{1,0:T(8,128)S(1)}, u32[]{:S(2)}, u32[]{:S(2)}) collective-permute-start(f32[48,128]{1,0:T(8,128)} %get-tuple-element.78), channel_id=1, source_target_pairs={{0,1},{1,0},{2,3},{3,2},{4,5},{5,4},{6,7},{7,6},{8,9},{9,8},{10,11... | collective-permute-start | bytes 73736 | tf_op jit(solution)/shard_map/ppermute | solution.py:747
  53.8 6.5 %collective-permute-start.8 = (f32[48,128]{1,0:T(8,128)S(1)}, f32[48,128]{1,0:T(8,128)S(1)}, u32[]{:S(2)}, u32[]{:S(2)}) collective-permute-start(f32[48,128]{1,0:T(8,128)S(1)} %get-tuple-element.79), channel_id=1, source_target_pairs={{0,3},{1,2},{2,1},{3,0},{4,7},{5,6},{6,5},{7,4},{8,11},{9,10},{10,... | collective-permute-start | bytes 73736 | tf_op jit(solution)/shard_map/ppermute | solution.py:747
  60.3 0.9 %copy-start.8 = (f32[32,8,128]{2,1,0:T(8,128)S(1)}, f32[32,8,128]{2,1,0:T(8,128)}, u32[]{:S(2)}) copy-start(f32[32,8,128]{2,1,0:T(8,128)} %copy-done.7) | copy-start | bytes 393220
  63.1 7.3 %collective-permute-start.9 = (bf16[6,32,512]{2,1,0:T(8,128)(2,1)S(1)}, bf16[6,32,512]{2,1,0:T(8,128)(2,1)S(1)}, u32[]{:S(2)}, u32[]{:S(2)}) collective-permute-start(bf16[6,32,512]{2,1,0:T(8,128)(2,1)S(1)} %get-tuple-element.91), channel_id=1, source_target_pairs={{0,64},{64,0},{1,65},{65,1},{2,66},{66,2},{3,67},{67,3},{4,68},{68... | collective-permute-start | bytes 589832 | tf_op jit(solution)/shard_map/ppermute | solution.py:747
  70.3 7.8 %copy-start.10 = (s32[1,32,4,2]{1,3,2,0:T(2,128)S(1)}, s32[1,32,4,2]{1,3,2,0:T(2,128)}, u32[]{:S(2)}) copy-start(s32[1,32,4,2]{1,3,2,0:T(2,128)} %param.18) | copy-start | bytes 3076
  70.3 7.8 %copy-start.12 = (s32[1,32,4,2]{1,3,2,0:T(2,128)S(1)}, s32[1,32,4,2]{1,3,2,0:T(2,128)}, u32[]{:S(2)}) copy-start(s32[1,32,4,2]{1,3,2,0:T(2,128)} %param.19) | copy-start | bytes 3076
  71.4 14.4 %all-to-all-start.1 = ((f32[64,1,128]{2,1,0:T(1,128)}), f32[64,1,128]{2,1,0:T(1,128)S(1)}, u32[]{:S(2)}, u32[]{:S(2)}) async-start(f32[64,1,128]{2,1,0:T(1,128)} %get-tuple-element.95), calls=%async_computation.1 | async-start | bytes 65536 | tf_op jit(solution)/shard_map/all_to_all | solution.py:832
  78.1 7.7 %copy-start.4 = (s32[32,512]{1,0:T(8,128)S(1)}, s32[32,512]{1,0:T(8,128)}, u32[]{:S(2)}) copy-start(s32[32,512]{1,0:T(8,128)} %mask.6) | copy-start | bytes 196612
  (4 other events, 2.7 us)

commit v5 on v4

--- a/solution.py
+++ b/solution.py
@@ -187,6 +187,11 @@
     return new, emitted
 
 
+def coefficient_place(i):
+    rows, cols = i // 5 * 8, i % 5 * LANES
+    return slice(rows, rows + 8), slice(cols, cols + LANES)
+
+
 class Rows:
     def __init__(self, ref, start):
         self.ref, self.start = ref, start
@@ -223,10 +228,9 @@
 
 def first_edges(
     state, guess, coupling, land, mask,
-    to_lower, to_upper, token,
+    to_lower, to_upper,
     head, tail, ints, short, sems,
 ):
-    token[...] = jnp.zeros_like(token)
     n = 0
     copies = []
 
@@ -306,7 +310,7 @@
 
 def first_cone(
     coeff, state, guess, coupling, land, mask, upper, lower, aux, one, three,
-    series, hd, ud, hs_out, us_out, fixed_out, coeff_out,
+    series, hd, ud, hs_out, us_out, fixed_out,
     s0, s1, g, emitted, hs, us, fixed, sems,
 ):
     diff, mix = coefficients(coeff)
@@ -352,8 +356,11 @@
     place_sides(put, fields, one, three, even, first, last)
     g[SUB - 1, :, side] = jnp.zeros((BAND, LANES), F32)
     fixed[2] = (1.0 - fixed[1]) * fixed[2]
+    for l in range(SUB):
+        for i, start in ((l, 0), (SUB + l, LEVELS)):
+            rows, cols = coefficient_place(i)
+            fixed[3, rows, cols] = coeff[start + l]
     write(fixed, fixed_out)
-    write(coeff, coeff_out)
 
     for t in range(SUB):
         src, dst = (s0, s1) if t % 2 == 0 else (s1, s0)
@@ -450,7 +457,7 @@
 def balance(
     diff, mix, src, pat, weights, mask, after,
     out, wet, coeff,
-    m, z, total, b, sem,
+    m, z, b, sem, *totals,
 ):
     del after
     for l in range(LEVELS):
@@ -469,24 +476,27 @@
     wet[...] = jnp.where(lane[:1] == SUB, count, 0.0)
     blocks = m[...].astype(BF16)
 
-    @pl.loop(0, PATTERNS)
+    @pl.loop(0, PATTERNS, unroll=8)
     def _(p):
         z[p] = lax.dot_general(
             blocks, weights[p], (((1,), (1,)), ((), ())), preferred_element_type=F32
         )
 
-    total[...] = m[...]
-
-    @pl.loop(0, CX)
+    for j in range(OWN_TILES):
+        totals[j][...] = jnp.zeros_like(totals[j])
+
+    @pl.loop(0, CX, unroll=4)
     def _(r):
-        for j in range(OWN_TILES):
-            for k in range(2):
+        for k in range(2):
+            for j in range(OWN_TILES):
                 row = pl.ds(src[j, k, r], 1)
-                total[row, :] = total[row, :] - z[pat[j, k, r], pl.ds(r * OWN_TILES + j, 1), :]
-
+                line = z[pat[j, k, r], pl.ds(r * OWN_TILES + j, 1), :]
+                totals[j][row, :] = totals[j][row, :] + line
+
+    m[...] = m[...] - ((totals[0][...] + totals[1][...]) + (totals[2][...] + totals[3][...]))
     for part in range(CX // 8):
         for j in range(OWN_TILES):
-            v = total[pl.ds(part * 8 * OWN_TILES + j, 8, stride=OWN_TILES), :]
+            v = m[pl.ds(part * 8 * OWN_TILES + j, 8, stride=OWN_TILES), :]
             b[part * 8 : part * 8 + 8, j * LANES : (j + 1) * LANES] = v
     c = pltpu.make_async_copy(b, out, sem)
     c.start()
@@ -613,13 +623,12 @@
 
 
 def second_cone(
-    coeff_in, fixed_in, regridded, upper, lower, one, three, gap, hs_in, us_in,
-    series, final0, hx, ux, coeff_out,
-    s0, s1, g, emitted, fixed, hs, us, halo, coeff, sems,
+    fixed_in, regridded, upper, lower, one, three, gap, hs_in, us_in,
+    series, final0, hx, ux, coeff,
+    s0, s1, g, emitted, fixed, hs, us, halo, sems,
 ):
-    diff, mix = coefficients(coeff)
     reads = []
-    pairs = ((us_in, us), (fixed_in, fixed), (coeff_in, coeff), (hs_in, hs))
+    pairs = ((us_in, us), (fixed_in, fixed), (hs_in, hs))
     for i, (src, dst) in enumerate(pairs):
         reads.append(pltpu.make_async_copy(src, dst, sems.at[i]))
         reads[-1].start()
@@ -642,7 +651,10 @@
     means = [jnp.broadcast_to(v, (8, LANES)) for v in gap_means(gap)]
     for c in reads:
         c.wait()
-    coeff_out[...] = coeff[...]
+    for l in range(SUB):
+        for i, start in ((l, 0), (SUB + l, LEVELS)):
+            coeff[start + l] = fixed[(3, *coefficient_place(i))]
+    diff, mix = coefficients(coeff)
 
     for t in range(SUB):
         src, dst = (s0, s1) if t % 2 == 0 else (s1, s0)
@@ -761,9 +773,9 @@
     numbers = shape(2 * LEVELS, 8, LANES)
 
     message = shape(LEVELS, 8, CY)
-    to_lower, to_upper, token = call(
+    to_lower, to_upper = call(
         first_edges,
-        [message, message, shape(8, LANES)],
+        [message, message],
         [
             pltpu.VMEM((AUX, 8, CY), F32),
             pltpu.VMEM((AUX, 8, CY), F32),
@@ -789,31 +801,31 @@
         [
             pltpu.VMEM((BLOCKS, LANES), F32),
             pltpu.VMEM((PATTERNS, BLOCKS, LANES), F32),
-            pltpu.VMEM((BLOCKS, LANES), F32),
             pltpu.VMEM((CX, CY), F32),
             pltpu.SemaphoreType.DMA(()),
+            *[pltpu.VMEM((BLOCKS, LANES), F32)] * OWN_TILES,
         ],
         [SM, SM, SM, SM, VM, VM, VM],
         out_specs=[HBM, VM, VM],
-    )(diff, mix, src, pat, table, mask, token)
+    )(diff, mix, src, pat, table, mask, to_lower)
     packed = shape(BAND, PACK_LANES)
     aux, one, three = call(pack_first, [shape(AUX, 16, CY), packed, packed], [], [VM] * 8)(
         state, guess, coupling, land_temp, mask, upper, lower, wet
     )
     one, three = paired(one, "gy", 1), paired(three, "gy", 3)
 
-    series, hd, ud, hs, us, fixed, numbers_out = call(
+    series, hd, ud, hs, us, fixed = call(
         first_cone,
         [
             shape(SUB, CX, CY, dtype=BF16), band(SUB), band(SUB),
-            band(3), band(3), band(3), numbers,
+            band(3), band(3), band(4),
         ],
         [
             field_buf(CONE), field_buf(CONE), band_buf(SUB), band_buf(SUB),
-            band_buf(3), band_buf(3), band_buf(3), pltpu.SemaphoreType.DMA((8,)),
+            band_buf(3), band_buf(3), band_buf(4), pltpu.SemaphoreType.DMA((7,)),
         ],
         [VM] * 11,
-        out_specs=[VM] * 3 + [HBM] * 4,
+        out_specs=[VM] * 3 + [HBM] * 3,
     )(coeff, state, guess, coupling, land_temp, mask, upper, lower, aux, one, three)
 
     def exchange(series, before):
@@ -874,11 +886,11 @@
         [shape(SUB, CX, CY, dtype=BF16), shape(CX, CY), band(3), band(3), numbers],
         [
             field_buf(3), field_buf(3), band_buf(SUB), band_buf(SUB),
-            band_buf(3), band_buf(3), band_buf(3), pltpu.VMEM((SUB - 1, 16, CY), F32),
-            pltpu.VMEM(numbers.shape, F32), pltpu.SemaphoreType.DMA((4,)),
+            band_buf(4), band_buf(3), band_buf(3), pltpu.VMEM((SUB - 1, 16, CY), F32),
+            pltpu.SemaphoreType.DMA((3,)),
         ],
-        [HBM, HBM] + [VM] * 6 + [HBM, HBM],
-    )(numbers_out, fixed, out, upper, lower, one, three, gap, hs, us)
+        [HBM] + [VM] * 6 + [HBM, HBM],
+    )(fixed, out, upper, lower, one, three, gap, hs, us)
 
     whole, token = call(
         second_rest,

time: 87.1 us -> 85.1 us (0.977)
  local copies, waits for them, and re-layouts: 5.13 us -> 1.58 us
  Pallas kernels: 32.5 us -> 30.2 us
  waiting for transfers between devices: 14.7 us -> 16.6 us
  starting transfers between devices: 33.5 us -> 35.4 us
    pallas_call x1, Pallas kernels: 6.8 us -> 2.72 us  [per_device(): call(balance, [shape(CX, CY), shape(1, LANES), shape(2 * LEVELS, 8, LANES...]
    unnamed x32 -> x24, local copies, waits for them, and re-layouts: 5.13 us -> 1.58 us
    ppermute x4, waiting for transfers between devices: 0.01 us -> 2.44 us  [shifted(): return lax.ppermute(value, axis, [(i, (i + by) % n) for i in range(n)])]
    all_to_all x2, starting transfers between devices: 11.8 us -> 13.4 us  [exchange(): gap = lax.all_to_all(gap, ('gx', 'gy'), 0, 0)]
  transfers between devices with their start and end apart: 12 -> 12, of which waited for: 4 -> 5; matrix products, arithmetic and copies ran while one was open for 0% -> 0% of each run, Pallas kernels for 21% -> 18%
where the time goes in v5:
time: 85.1 us; the launch traced here: 84.7 us
  starting transfers between devices  35.4 us (42%)
  Pallas kernels  30.2 us (35%)
  waiting for transfers between devices  16.6 us (20%)
  local copies, waits for them, and re-layouts  1.58 us (2%)
  between operations  0.89 us (1%)
    all_to_all x2, starting transfers between devices, exchange(): gap = lax.all_to_all(gap, ('gx', 'gy'), 0, 0)  13.4 us
    ppermute x4, starting transfers between devices, shifted(): return lax.ppermute(value, axis, [(i, (i + by) % n) for i in range(n)])  11.9 us
    ppermute x6, starting transfers between devices, paired(): lax.ppermute(value, axis, [(i, i ^ mask) for i in range(lax.axis_size(axi...  10.1 us
    all_to_all x2, waiting for transfers between devices, exchange(): gap = lax.all_to_all(gap, ('gx', 'gy'), 0, 0)  8.66 us
    pallas_call x2, Pallas kernels, exchange(): call(regrid, [shape(SUB, CX, CY), edges, edges], [pltpu.VMEM((BLOCKS * 8,...  7.19 us
    pallas_call x1, Pallas kernels, per_device(): call(first_rest, [shape(LEVELS, CX, CY), band(3), band(3), shape(8, LANES...  5.82 us
    ppermute x6, waiting for transfers between devices, paired(): lax.ppermute(value, axis, [(i, i ^ mask) for i in range(lax.axis_size(axi...  5.49 us
    pallas_call x1, Pallas kernels, per_device(): call(first_cone, [shape(SUB, CX, CY, dtype=BF16), band(SUB), band(SUB), b...  3.99 us
  transfers between devices with their start and end apart: 12, of which 5 were waited for; matrix products, arithmetic and copies ran while one was open for 0% of the time, Pallas kernels for 18%

profile of v5, /device:TPU:1, one launch (start us, length us, event | category | flops | bytes accessed | tf_op | source)
XLA Modules:
  0.0 84.7 jit_solution(354307853069459225)
XLA Ops:
  0.7 2.1 %shard_map.113 = (f32[16,8,512]{2,1,0:T(8,128)}, f32[16,8,512]{2,1,0:T(8,128)}) custom-call(f32[16,32,512]{2,1,0:T(8,128)} %bitcast.14, bf16[6,32,512]{2,1,0:T(8,128)(2,1)} %bitcast.21, f32[32,512]{1,0:T(8,128)} %bitcast.24, f32[32,512]{1,0:T(8,128)} %land.3, s32[32,512]{1,0:T(8,128)} %mask.6), custom_call_target="tpu_custom_call" | custom-call | tf_op jit(solution)/shard_map/pallas_call | solution.py:776
  2.8 2.1 %collective-permute-start = (f32[16,8,512]{2,1,0:T(8,128)}, f32[16,8,512]{2,1,0:T(8,128)S(1)}, u32[]{:S(2)}, u32[]{:S(2)}) collective-permute-start(f32[16,8,512]{2,1,0:T(8,128)} %get-tuple-element.59), channel_id=1, source_target_pairs={{0,4},{4,8},{8,12},{12,16},{16,20},{20,24},{24,28},{28,32},{32,36}... | collective-permute-start | bytes 786440 | tf_op jit(solution)/shard_map/ppermute | solution.py:755
  4.9 4.8 %collective-permute-start.1 = (f32[16,8,512]{2,1,0:T(8,128)}, f32[16,8,512]{2,1,0:T(8,128)S(1)}, u32[]{:S(2)}, u32[]{:S(2)}) collective-permute-start(f32[16,8,512]{2,1,0:T(8,128)} %get-tuple-element.53.after), channel_id=1, source_target_pairs={{0,60},{4,0},{8,4},{12,8},{16,12},{20,16},{24,20},{28,24},{32,28},... | collective-permute-start | bytes 786440 | tf_op jit(solution)/shard_map/ppermute | solution.py:755
  10.8 2.7 %shard_map.114 = (f32[32,512]{1,0:T(8,128)S(1)}, f32[1,128]{1,0:T(1,128)S(1)}, f32[32,8,128]{2,1,0:T(8,128)S(1)}) custom-call(f32[16]{0:T(128)S(1)} %bitcast.33, f32[15]{0:T(128)S(1)} %bitcast.34, s32[4,2,32]{2,1,0:T(2,128)S(1)} %bitcast.27, s32[4,2,32]{2,1,0:T(2,128)S(1)} %bitcast.30, bf16[32,128,128]{2,1,0:T(8,128)(2,1)S(1)} %bitcast.18, ...), custom_call_target="tpu_custom_call" | custom-call | tf_op jit(solution)/shard_map/pallas_call | solution.py:798
  13.5 2.4 %collective-permute-done.upper = f32[16,8,512]{2,1,0:T(8,128)S(1)} collective-permute-done((f32[16,8,512]{2,1,0:T(8,128)}, f32[16,8,512]{2,1,0:T(8,128)S(1)}, u32[]{:S(2)}, u32[]{:S(2)}) %collective-permute-start) | collective-permute-done | bytes 262176 | tf_op jit(solution)/shard_map/ppermute | solution.py:755
  16.3 1.3 %collective-permute-start.2 = (f32[48,256]{1,0:T(8,128)S(1)}, f32[48,256]{1,0:T(8,128)S(1)}, u32[]{:S(2)}, u32[]{:S(2)}) collective-permute-start(f32[48,256]{1,0:T(8,128)S(1)} %get-tuple-element.62), channel_id=1, source_target_pairs={{0,1},{1,0},{2,3},{3,2},{4,5},{5,4},{6,7},{7,6},{8,9},{9,8},{10,11... | collective-permute-start | bytes 147464 | tf_op jit(solution)/shard_map/ppermute | solution.py:759
  17.6 1.3 %collective-permute-start.3 = (f32[48,256]{1,0:T(8,128)S(1)}, f32[48,256]{1,0:T(8,128)S(1)}, u32[]{:S(2)}, u32[]{:S(2)}) collective-permute-start(f32[48,256]{1,0:T(8,128)S(1)} %get-tuple-element.63), channel_id=1, source_target_pairs={{0,3},{1,2},{2,1},{3,0},{4,7},{5,6},{6,5},{7,4},{8,11},{9,10},{10,... | collective-permute-start | bytes 147464 | tf_op jit(solution)/shard_map/ppermute | solution.py:759
  18.9 2.3 %collective-permute-done.3.three = f32[48,256]{1,0:T(8,128)S(1)} collective-permute-done((f32[48,256]{1,0:T(8,128)S(1)}, f32[48,256]{1,0:T(8,128)S(1)}, u32[]{:S(2)}, u32[]{:S(2)}) %collective-permute-start.3) | collective-permute-done | bytes 49184 | tf_op jit(solution)/shard_map/ppermute | solution.py:759
  21.1 4.0 %shard_map.116 = (bf16[6,32,512]{2,1,0:T(8,128)(2,1)S(1)}, f32[6,48,640]{2,1,0:T(8,128)S(1)}, f32[6,48,640]{2,1,0:T(8,128)S(1)}, f32[3,48,640]{2,1,0:T(8,128)S(1...) custom-call(f32[32,8,128]{2,1,0:T(8,128)S(1)} %get-tuple-element.54.coeff, f32[16,32,512]{2,1,0:T(8,128)S(1)} %bitcast.16, ...), custom_call_target="tpu_custom_call" | custom-call | tf_op jit(solution)/shard_map/pallas_call | solution.py:817
  25.1 3.0 %collective-permute-start.4 = (bf16[6,32,512]{2,1,0:T(8,128)(2,1)S(1)}, bf16[6,32,512]{2,1,0:T(8,128)(2,1)S(1)}, u32[]{:S(2)}, u32[]{:S(2)}) collective-permute-start(bf16[6,32,512]{2,1,0:T(8,128)(2,1)S(1)} %get-tuple-element.65), channel_id=1, source_target_pairs={{0,64},{64,0},{1,65},{65,1},{2,66},{66,2},{3,67},{67,3},{4,68},{68... | collective-permute-start | bytes 589832 | tf_op jit(solution)/shard_map/ppermute | solution.py:759
  28.2 5.8 %shard_map.117 = (f32[16,32,512]{2,1,0:T(8,128)}, f32[3,48,640]{2,1,0:T(8,128)S(1)}, f32[3,48,640]{2,1,0:T(8,128)S(1)}, f32[8,128]{1,0:T(8,128)S(1)}) custom-call(f32[32,8,128]{2,1,0:T(8,128)S(1)} %get-tuple-element.54.coeff, f32[16,32,512]{2,1,0:T(8,128)S(1)} %bitcast.17, f32[16,8,512]{2,1,0:T(8,128)S(1)} %collective-permute-done.upper, ...), custom_call_target="tpu_custom_call" | custom-call | tf_op jit(solution)/shard_map/pallas_call | solution.py:865
  35.1 3.6 %shard_map.119 = (f32[6,32,512]{2,1,0:T(8,128)S(1)}, f32[2,8,512]{2,1,0:T(8,128)}, f32[2,8,512]{2,1,0:T(8,128)}) custom-call(s32[4,2,32]{2,1,0:T(2,128)S(1)} %bitcast.28, s32[4,2,32]{2,1,0:T(2,128)S(1)} %bitcast.31, bf16[6,32,512]{2,1,0:T(8,128)(2,1)S(1)} %collective-permute-done.4.received_in, bf16[32,128,128]{2,1,0:T(8,128)(2,1)S(1)} %bitcast.19, ...), custom_call_target="tpu_custom_call" | custom-call | flops 67108864 | bytes 8388608 | tf_op jit(solution)/shard_map/pallas_call | solution.py:846
  38.8 4.9 %collective-permute-start.6 = (f32[2,8,512]{2,1,0:T(8,128)}, f32[2,8,512]{2,1,0:T(8,128)}, u32[]{:S(2)}, u32[]{:S(2)}) collective-permute-start(f32[2,8,512]{2,1,0:T(8,128)} %get-tuple-element.73), channel_id=1, source_target_pairs={{0,60},{4,0},{8,4},{12,8},{16,12},{20,16},{24,20},{28,24},{32,28},... | collective-permute-start | bytes 98312 | tf_op jit(solution)/shard_map/ppermute | solution.py:755
  43.7 5.7 %all-to-all-start = ((f32[64,1,128]{2,1,0:T(1,128)}), f32[64,1,128]{2,1,0:T(1,128)}, u32[]{:S(2)}, u32[]{:S(2)}) async-start(f32[64,1,128]{2,1,0:T(1,128)} %copy-done.9), calls=%async_computation | async-start | bytes 65536 | tf_op jit(solution)/shard_map/all_to_all | solution.py:844
  49.4 1.5 %shard_map.120 = (f32[48,128]{1,0:T(8,128)}, f32[48,128]{1,0:T(8,128)}) custom-call(f32[6,32,512]{2,1,0:T(8,128)S(1)} %get-tuple-element.71.out.regridded, f32[2,8,512]{2,1,0:T(8,128)} %collective-permute-done.5.upper, f32[2,8,512]{2,1,0:T(8,128)} %collective-permute-done.6.lower), custom_call_target="tpu_custom_call" | custom-call | tf_op jit(solution)/shard_map/pallas_call | solution.py:879
  51.6 1.2 %collective-permute-start.8 = (f32[48,128]{1,0:T(8,128)}, f32[48,128]{1,0:T(8,128)}, u32[]{:S(2)}, u32[]{:S(2)}) collective-permute-start(f32[48,128]{1,0:T(8,128)} %get-tuple-element.75), channel_id=1, source_target_pairs={{0,3},{1,2},{2,1},{3,0},{4,7},{5,6},{6,5},{7,4},{8,11},{9,10},{10,... | collective-permute-start | bytes 73736 | tf_op jit(solution)/shard_map/ppermute | solution.py:759
  52.7 4.6 %all-to-all-done.gap = f32[64,1,128]{2,1,0:T(1,128)} async-done(((f32[64,1,128]{2,1,0:T(1,128)}), f32[64,1,128]{2,1,0:T(1,128)}, u32[]{:S(2)}, u32[]{:S(2)}) %all-to-all-start) | async-done | bytes 32800 | tf_op jit(solution)/shard_map/all_to_all | solution.py:844
  57.4 2.7 %shard_map.121 = (bf16[6,32,512]{2,1,0:T(8,128)(2,1)S(1)}, f32[32,512]{1,0:T(8,128)S(1)}, f32[3,48,640]{2,1,0:T(8,128)S(1)}, f32[3,48,640]{2,1,0:T(8,128)S(1)}, f32[32,8,128]{2,1,0:T(8,128)S(1)}) custom-call(f32[4,48,640]{2,1,0:T(8,128)S(1)} %get-tuple-element.64.fixed_in, f32[6,32,512]{2,1,0:T(8,128)S(1)} %get-tuple-element.71.out.regridded, ...), custom_call_target="tpu_custom_call" | custom-call | tf_op jit(solution)/shard_map/pallas_call | solution.py:884
  60.0 2.7 %collective-permute-start.9 = (bf16[6,32,512]{2,1,0:T(8,128)(2,1)S(1)}, bf16[6,32,512]{2,1,0:T(8,128)(2,1)S(1)}, u32[]{:S(2)}, u32[]{:S(2)}) collective-permute-start(bf16[6,32,512]{2,1,0:T(8,128)(2,1)S(1)} %get-tuple-element.87), channel_id=1, source_target_pairs={{0,64},{64,0},{1,65},{65,1},{2,66},{66,2},{3,67},{67,3},{4,68},{68... | collective-permute-start | bytes 589832 | tf_op jit(solution)/shard_map/ppermute | solution.py:759
  62.7 1.4 %shard_map.122 = (f32[16,32,512]{2,1,0:T(8,128)}, f32[8,128]{1,0:T(8,128)S(1)}) custom-call(f32[32,8,128]{2,1,0:T(8,128)S(1)} %get-tuple-element.79.coeff, f32[3,48,640]{2,1,0:T(8,128)S(1)} %get-tuple-element.80.hx, f32[3,48,640]{2,1,0:T(8,128)S(1)} %get-tuple-element.81.ux, ...), custom_call_target="tpu_custom_call", output_to_operand_aliasing={{0}: (6, {})} | custom-call | tf_op jit(solution)/shard_map/pallas_call | solution.py:895
  64.1 3.2 %collective-permute-done.9.received_in = bf16[6,32,512]{2,1,0:T(8,128)(2,1)S(1)} collective-permute-done((bf16[6,32,512]{2,1,0:T(8,128)(2,1)S(1)}, bf16[6,32,512]{2,1,0:T(8,128)(2,1)S(1)}, u32[]{:S(2)}, u32[]{:S(2)}) %collective-permute-start.9) | collective-permute-done | bytes 196640 | tf_op jit(solution)/shard_map/ppermute | solution.py:759
  68.3 7.7 %all-to-all-start.1 = ((f32[64,1,128]{2,1,0:T(1,128)}), f32[64,1,128]{2,1,0:T(1,128)S(1)}, u32[]{:S(2)}, u32[]{:S(2)}) async-start(f32[64,1,128]{2,1,0:T(1,128)} %get-tuple-element.91), calls=%async_computation.1 | async-start | bytes 65536 | tf_op jit(solution)/shard_map/all_to_all | solution.py:844
  76.1 3.6 %shard_map.124 = (f32[6,32,512]{2,1,0:T(8,128)S(1)}, f32[2,8,512]{2,1,0:T(8,128)}, f32[2,8,512]{2,1,0:T(8,128)}) custom-call(s32[4,2,32]{2,1,0:T(2,128)S(1)} %bitcast.29, s32[4,2,32]{2,1,0:T(2,128)S(1)} %bitcast.32, bf16[6,32,512]{2,1,0:T(8,128)(2,1)S(1)} %collective-permute-done.9.received_in, bf16[32,128,128]{2,1,0:T(8,128)(2,1)S(1)} %bitcast.20, ...), custom_call_target="tpu_custom_call" | custom-call | flops 67108864 | bytes 8388608 | tf_op jit(solution)/shard_map/pallas_call | solution.py:846
  79.7 4.1 %all-to-all-done.1.gap = f32[64,1,128]{2,1,0:T(1,128)S(1)} async-done(((f32[64,1,128]{2,1,0:T(1,128)}), f32[64,1,128]{2,1,0:T(1,128)S(1)}, u32[]{:S(2)}, u32[]{:S(2)}) %all-to-all-start.1) | async-done | bytes 32800 | tf_op jit(solution)/shard_map/all_to_all | solution.py:844
  (37 shorter events, 5.1 us)
Async XLA Ops:
  0.6 9.1 %copy-start.1 = (bf16[1,32,128,128]{3,2,1,0:T(8,128)(2,1)S(1)}, bf16[1,32,128,128]{3,2,1,0:T(8,128)(2,1)}, u32[]{:S(2)}) copy-start(bf16[1,32,128,128]{3,2,1,0:T(8,128)(2,1)} %param.17) | copy-start | bytes 3145732
  0.6 9.1 %copy-start.3 = (s32[32,512]{1,0:T(8,128)S(1)}, s32[32,512]{1,0:T(8,128)}, u32[]{:S(2)}) copy-start(s32[32,512]{1,0:T(8,128)} %mask.6) | copy-start | bytes 196612
  0.7 9.1 %copy-start.7 = (s32[1,32,4,2]{1,3,2,0:T(2,128)S(1)}, s32[1,32,4,2]{1,3,2,0:T(2,128)}, u32[]{:S(2)}) copy-start(s32[1,32,4,2]{1,3,2,0:T(2,128)} %param.18) | copy-start | bytes 3076
  0.7 9.1 %copy-start.8 = (s32[1,32,4,2]{1,3,2,0:T(2,128)S(1)}, s32[1,32,4,2]{1,3,2,0:T(2,128)}, u32[]{:S(2)}) copy-start(s32[1,32,4,2]{1,3,2,0:T(2,128)} %param.19) | copy-start | bytes 3076
  0.7 9.1 %copy-start.10 = (f32[1,16]{1,0:T(1,128)S(1)}, f32[1,16]{1,0:T(1,128)}, u32[]{:S(2)}) copy-start(f32[1,16]{1,0:T(1,128)} %param.12) | copy-start | bytes 196
  0.7 9.1 %copy-start.11 = (f32[1,15]{1,0:T(1,128)S(1)}, f32[1,15]{1,0:T(1,128)}, u32[]{:S(2)}) copy-start(f32[1,15]{1,0:T(1,128)} %param.13) | copy-start | bytes 184
  2.8 13.1 %copy-start = (f32[1,16,32,512]{3,2,1,0:T(8,128)S(1)}, f32[1,16,32,512]{3,2,1,0:T(8,128)}, u32[]{:S(2)}) copy-start(f32[1,16,32,512]{3,2,1,0:T(8,128)} %param.10) | copy-start | bytes 3145732
  2.8 13.1 %collective-permute-start = (f32[16,8,512]{2,1,0:T(8,128)}, f32[16,8,512]{2,1,0:T(8,128)S(1)}, u32[]{:S(2)}, u32[]{:S(2)}) collective-permute-start(f32[16,8,512]{2,1,0:T(8,128)} %get-tuple-element.59), channel_id=1, source_target_pairs={{0,4},{4,8},{8,12},{12,16},{16,20},{20,24},{24,28},{28,32},{32,36}... | collective-permute-start | bytes 786440 | tf_op jit(solution)/shard_map/ppermute | solution.py:755
  4.9 11.0 %collective-permute-start.1 = (f32[16,8,512]{2,1,0:T(8,128)}, f32[16,8,512]{2,1,0:T(8,128)S(1)}, u32[]{:S(2)}, u32[]{:S(2)}) collective-permute-start(f32[16,8,512]{2,1,0:T(8,128)} %get-tuple-element.53.after), channel_id=1, source_target_pairs={{0,60},{4,0},{8,4},{12,8},{16,12},{20,16},{24,20},{28,24},{32,28},... | collective-permute-start | bytes 786440 | tf_op jit(solution)/shard_map/ppermute | solution.py:755
  9.8 1.0 %copy-start.6 = (f32[16,8,512]{2,1,0:T(8,128)S(1)}, f32[16,8,512]{2,1,0:T(8,128)}, u32[]{:S(2)}) copy-start(f32[16,8,512]{2,1,0:T(8,128)} %get-tuple-element.53.after) | copy-start | bytes 786436
  10.8 5.2 %copy-start.2 = (bf16[1,6,32,512]{3,2,1,0:T(8,128)(2,1)S(1)}, bf16[1,6,32,512]{3,2,1,0:T(8,128)(2,1)}, u32[]{:S(2)}) copy-start(bf16[1,6,32,512]{3,2,1,0:T(8,128)(2,1)} %param.11) | copy-start | bytes 589828
  10.8 5.2 %copy-start.4 = (f32[1,32,512]{2,1,0:T(8,128)S(1)}, f32[1,32,512]{2,1,0:T(8,128)}, u32[]{:S(2)}) copy-start(f32[1,32,512]{2,1,0:T(8,128)} %param.14) | copy-start | bytes 196612
  10.8 5.2 %copy-start.5 = (f32[32,512]{1,0:T(8,128)S(1)}, f32[32,512]{1,0:T(8,128)}, u32[]{:S(2)}) copy-start(f32[32,512]{1,0:T(8,128)} %land.3) | copy-start | bytes 196612
  16.3 2.6 %collective-permute-start.2 = (f32[48,256]{1,0:T(8,128)S(1)}, f32[48,256]{1,0:T(8,128)S(1)}, u32[]{:S(2)}, u32[]{:S(2)}) collective-permute-start(f32[48,256]{1,0:T(8,128)S(1)} %get-tuple-element.62), channel_id=1, source_target_pairs={{0,1},{1,0},{2,3},{3,2},{4,5},{5,4},{6,7},{7,6},{8,9},{9,8},{10,11... | collective-permute-start | bytes 147464 | tf_op jit(solution)/shard_map/ppermute | solution.py:759
  17.6 3.5 %collective-permute-start.3 = (f32[48,256]{1,0:T(8,128)S(1)}, f32[48,256]{1,0:T(8,128)S(1)}, u32[]{:S(2)}, u32[]{:S(2)}) collective-permute-start(f32[48,256]{1,0:T(8,128)S(1)} %get-tuple-element.63), channel_id=1, source_target_pairs={{0,3},{1,2},{2,1},{3,0},{4,7},{5,6},{6,5},{7,4},{8,11},{9,10},{10,... | collective-permute-start | bytes 147464 | tf_op jit(solution)/shard_map/ppermute | solution.py:759
  25.1 8.8 %collective-permute-start.4 = (bf16[6,32,512]{2,1,0:T(8,128)(2,1)S(1)}, bf16[6,32,512]{2,1,0:T(8,128)(2,1)S(1)}, u32[]{:S(2)}, u32[]{:S(2)}) collective-permute-start(bf16[6,32,512]{2,1,0:T(8,128)(2,1)S(1)} %get-tuple-element.65), channel_id=1, source_target_pairs={{0,64},{64,0},{1,65},{65,1},{2,66},{66,2},{3,67},{67,3},{4,68},{68... | collective-permute-start | bytes 589832 | tf_op jit(solution)/shard_map/ppermute | solution.py:759
  34.5 0.6 copy-start.9
  38.7 10.7 %collective-permute-start.5 = (f32[2,8,512]{2,1,0:T(8,128)}, f32[2,8,512]{2,1,0:T(8,128)}, u32[]{:S(2)}, u32[]{:S(2)}) collective-permute-start(f32[2,8,512]{2,1,0:T(8,128)} %get-tuple-element.72), channel_id=1, source_target_pairs={{0,4},{4,8},{8,12},{12,16},{16,20},{20,24},{24,28},{28,32},{32,36}... | collective-permute-start | bytes 98312 | tf_op jit(solution)/shard_map/ppermute | solution.py:755
  38.8 10.7 %collective-permute-start.6 = (f32[2,8,512]{2,1,0:T(8,128)}, f32[2,8,512]{2,1,0:T(8,128)}, u32[]{:S(2)}, u32[]{:S(2)}) collective-permute-start(f32[2,8,512]{2,1,0:T(8,128)} %get-tuple-element.73), channel_id=1, source_target_pairs={{0,60},{4,0},{8,4},{12,8},{16,12},{20,16},{24,20},{28,24},{32,28},... | collective-permute-start | bytes 98312 | tf_op jit(solution)/shard_map/ppermute | solution.py:755
  43.7 13.7 %all-to-all-start = ((f32[64,1,128]{2,1,0:T(1,128)}), f32[64,1,128]{2,1,0:T(1,128)}, u32[]{:S(2)}, u32[]{:S(2)}) async-start(f32[64,1,128]{2,1,0:T(1,128)} %copy-done.9), calls=%async_computation | async-start | bytes 65536 | tf_op jit(solution)/shard_map/all_to_all | solution.py:844
  50.9 6.4 %collective-permute-start.7 = (f32[48,128]{1,0:T(8,128)}, f32[48,128]{1,0:T(8,128)}, u32[]{:S(2)}, u32[]{:S(2)}) collective-permute-start(f32[48,128]{1,0:T(8,128)} %get-tuple-element.74), channel_id=1, source_target_pairs={{0,1},{1,0},{2,3},{3,2},{4,5},{5,4},{6,7},{7,6},{8,9},{9,8},{10,11... | collective-permute-start | bytes 73736 | tf_op jit(solution)/shard_map/ppermute | solution.py:759
  51.6 5.8 %collective-permute-start.8 = (f32[48,128]{1,0:T(8,128)}, f32[48,128]{1,0:T(8,128)}, u32[]{:S(2)}, u32[]{:S(2)}) collective-permute-start(f32[48,128]{1,0:T(8,128)} %get-tuple-element.75), channel_id=1, source_target_pairs={{0,3},{1,2},{2,1},{3,0},{4,7},{5,6},{6,5},{7,4},{8,11},{9,10},{10,... | collective-permute-start | bytes 73736 | tf_op jit(solution)/shard_map/ppermute | solution.py:759
  60.0 7.3 %collective-permute-start.9 = (bf16[6,32,512]{2,1,0:T(8,128)(2,1)S(1)}, bf16[6,32,512]{2,1,0:T(8,128)(2,1)S(1)}, u32[]{:S(2)}, u32[]{:S(2)}) collective-permute-start(bf16[6,32,512]{2,1,0:T(8,128)(2,1)S(1)} %get-tuple-element.87), channel_id=1, source_target_pairs={{0,64},{64,0},{1,65},{65,1},{2,66},{66,2},{3,67},{67,3},{4,68},{68... | collective-permute-start | bytes 589832 | tf_op jit(solution)/shard_map/ppermute | solution.py:759
  68.3 15.4 %all-to-all-start.1 = ((f32[64,1,128]{2,1,0:T(1,128)}), f32[64,1,128]{2,1,0:T(1,128)S(1)}, u32[]{:S(2)}, u32[]{:S(2)}) async-start(f32[64,1,128]{2,1,0:T(1,128)} %get-tuple-element.91), calls=%async_computation.1 | async-start | bytes 65536 | tf_op jit(solution)/shard_map/all_to_all | solution.py:844

commit v6 on v5

--- a/solution.py
+++ b/solution.py
@@ -309,10 +309,11 @@
 
 
 def first_cone(
-    coeff, state, guess, coupling, land, mask, upper, lower, aux, one, three,
+    coeff, state, guess, coupling, land, mask, upper, lower, aux, one, three, beside,
     series, hd, ud, hs_out, us_out, fixed_out,
     s0, s1, g, emitted, hs, us, fixed, sems,
 ):
+    del beside
     diff, mix = coefficients(coeff)
     writes = []
 
@@ -503,23 +504,14 @@
     c.wait()
 
 
-def losses(
-    received_in, factor, wet, before,
-    gap, token,
-    received, rows, sems,
-):
-    del before
-    token[...] = jnp.zeros_like(token)
-    c = pltpu.make_async_copy(received_in, received, sems.at[0])
-    c.start()
-    c.wait()
+def share_rows(series, factor, wet, rows):
     partial = [jnp.zeros((8, LANES), F32) for _ in range(SUB)]
     for half in range(CX // 16):
         for j in range(OWN_TILES):
             cols = slice(j * LANES, (j + 1) * LANES)
             f = factor[half * 16 : half * 16 + 16, cols]
             for t in range(SUB):
-                p = f * received[t, half * 16 : half * 16 + 16, cols].astype(F32)
+                p = f * series[t, half * 16 : half * 16 + 16, cols].astype(F32)
                 partial[t] += p[:8] + p[8:]
     row, lane = iotas()
     total = jnp.zeros((8, LANES), F32)
@@ -529,7 +521,17 @@
     total = jnp.sum(jnp.where(row == lane, total, 0.0), axis=0, keepdims=True) + wet[...]
     for k in range(rows.shape[0]):
         rows[k] = total
-    c = pltpu.make_async_copy(rows, gap, sems.at[1])
+
+
+def losses(
+    received, factor, wet, before,
+    gap, token,
+    rows, sem,
+):
+    del before
+    token[...] = jnp.zeros_like(token)
+    share_rows(received, factor, wet, rows)
+    c = pltpu.make_async_copy(rows, gap, sem)
     c.start()
     c.wait()
 
@@ -540,18 +542,13 @@
 
 
 def regrid(
-    src, pat, received_in, weights_in, before,
+    src, pat, received, weights_in, before,
     out, top, bottom,
-    x, y, received, weights, sems,
+    x, y, weights, sem,
 ):
     del before
-    reads = [
-        pltpu.make_async_copy(received_in, received, sems.at[0]),
-        pltpu.make_async_copy(weights_in, weights, sems.at[1]),
-    ]
-    for c in reads:
-        c.start()
-    reads[0].wait()
+    read = pltpu.make_async_copy(weights_in, weights, sem)
+    read.start()
     for half in range(CX // 16):
         for j in range(OWN_TILES):
             cols = slice(j * LANES, (j + 1) * LANES)
@@ -561,10 +558,8 @@
                     row = half * 16 + part * 8
                     start = (row * OWN_TILES + j) * 8 + t
                     x[pl.ds(start, 8, stride=OWN_TILES * 8), :] = v16[part * 8 : part * 8 + 8]
-    reads[1].wait()
-
-    @pl.loop(0, CX, unroll=8)
-    def _(r):
+    read.wait()
+    for r in range(CX):
         for j in range(OWN_TILES):
             a, w = [], []
             for k in range(2):
@@ -613,8 +608,8 @@
     pack_columns([field(t) for t in range(SUB - 1)], one, three, even)
 
 
-def gap_means(gap):
-    total = jnp.sum(gap[...], axis=0)
+def gap_means(gap, start, count):
+    total = jnp.sum(gap[pl.ds(start, count)], axis=0)
     lane = lax.broadcasted_iota(jnp.int32, (1, LANES), 1)
     wet = jnp.sum(jnp.where(lane == SUB, total, 0.0), axis=1, keepdims=True)
     return [
@@ -648,7 +643,7 @@
 
     place_sides(put, list(range(SUB - 1)), one, three, even, first, last)
     g[SUB - 1, :, CY:COLS] = jnp.zeros((BAND, LANES), F32)
-    means = [jnp.broadcast_to(v, (8, LANES)) for v in gap_means(gap)]
+    means = [jnp.broadcast_to(v, (8, LANES)) for v in gap_means(gap, 0, gap.shape[0])]
     for c in reads:
         c.wait()
     for l in range(SUB):
@@ -696,11 +691,14 @@
 
 
 def second_rest(
-    coeff, hx, ux, hs_in, us_in, final0, whole,
-    final, token,
-    s0, s1, hs, us, sems,
+    coeff, hx, ux, hs_in, us_in, final0, series, factor, wet, whole,
+    final, token, gap,
+    s0, s1, hs, us, shares, sems,
 ):
     del whole
+    share_rows(series, factor, wet, shares)
+    send = pltpu.make_async_copy(shares, gap, sems.at[2])
+    send.start()
     diff, mix = coefficients(coeff)
     reads = [
         pltpu.make_async_copy(us_in, us, sems.at[0]),
@@ -743,10 +741,13 @@
                     rows = slice(r * 8 - 16, r * 8 - 8)
                     for k in range(OWN_TILES):
                         final[l, rows, k * LANES : (k + 1) * LANES] = v[k]
+    send.wait()
 
 
 def finish(regridded, mask, gap, forcing):
-    for t, mean in enumerate(gap_means(gap)):
+    peers = gap.shape[0] // 2
+    start = (1 - lax.axis_index("comp")) * peers
+    for t, mean in enumerate(gap_means(gap, start, peers)):
         forcing[t] = regridded[t] + mask[...].astype(F32) * mean
 
 
@@ -766,7 +767,6 @@
     weights = weights[0]
     src = source_block[0].transpose(1, 2, 0)
     pat = pattern[0].transpose(1, 2, 0)
-    peers = lax.axis_size("gx") * lax.axis_size("gy")
     band = lambda n: shape(n, BAND, COLS)
     field_buf = lambda n: pltpu.VMEM((n, ROWS, COLS), F32)
     band_buf = lambda n: pltpu.VMEM((n, BAND, COLS), F32)
@@ -808,6 +808,7 @@
         [SM, SM, SM, SM, VM, VM, VM],
         out_specs=[HBM, VM, VM],
     )(diff, mix, src, pat, table, mask, to_lower)
+    other = paired(factor, "comp", 1)
     packed = shape(BAND, PACK_LANES)
     aux, one, three = call(pack_first, [shape(AUX, 16, CY), packed, packed], [], [VM] * 8)(
         state, guess, coupling, land_temp, mask, upper, lower, wet
@@ -824,43 +825,28 @@
             field_buf(CONE), field_buf(CONE), band_buf(SUB), band_buf(SUB),
             band_buf(3), band_buf(3), band_buf(4), pltpu.SemaphoreType.DMA((7,)),
         ],
-        [VM] * 11,
+        [VM] * 11 + [pl.BlockSpec(memory_space=pl.ANY)],
         out_specs=[VM] * 3 + [HBM] * 3,
-    )(coeff, state, guess, coupling, land_temp, mask, upper, lower, aux, one, three)
-
-    def exchange(series, before):
-        received = paired(series, "comp", 1)
-        gap, after = call(
-            losses,
-            [shape(peers, 1, LANES), shape(8, LANES)],
-            [
-                pltpu.VMEM((SUB, CX, CY), BF16),
-                pltpu.VMEM((peers, 1, LANES), F32),
-                pltpu.SemaphoreType.DMA((2,)),
-            ],
-            [HBM, VM, VM, VM],
-            out_specs=[HBM, VM],
-        )(received, factor, wet, before)
-        gap = lax.all_to_all(gap, ("gx", "gy"), 0, 0)
+    )(coeff, state, guess, coupling, land_temp, mask, upper, lower, aux, one, three, other)
+
+    def regridded(received, before):
         edges = shape(2, 8, CY)
-        out, top, bottom = call(
+        return call(
             regrid,
             [shape(SUB, CX, CY), edges, edges],
             [
                 pltpu.VMEM((BLOCKS * 8, LANES), F32),
                 pltpu.VMEM((BLOCKS * 8, LANES), F32),
-                pltpu.VMEM((SUB, CX, CY), BF16),
                 pltpu.VMEM((PATTERNS, LANES, LANES), BF16),
-                pltpu.SemaphoreType.DMA((2,)),
+                pltpu.SemaphoreType.DMA(()),
             ],
-            [SM, SM, HBM, HBM, VM],
+            [SM, SM, VM, HBM, VM],
             cost_estimate=pl.CostEstimate(
                 flops=2 * BLOCKS * 8 * 2 * LANES * LANES,
                 bytes_accessed=BLOCKS * 2 * LANES * LANES * 2,
                 transcendentals=0,
             ),
-        )(src, pat, received, weights, after)
-        return out, top, bottom, gap
+        )(src, pat, received, weights, before)
 
     whole, hs_rest, us_rest, token = call(
         first_rest,
@@ -873,7 +859,17 @@
         out_specs=[VM, HBM, HBM, VM],
     )(coeff, state, upper, lower, one, three, hd, ud)
 
-    out, top, bottom, gap = exchange(series, token)
+    received = paired(series, "comp", 1)
+    peers = lax.axis_size(("gx", "gy"))
+    gap, after = call(
+        losses,
+        [shape(peers, 1, LANES), shape(8, LANES)],
+        [pltpu.VMEM((peers, 1, LANES), F32), pltpu.SemaphoreType.DMA(())],
+        [VM, VM, VM, VM],
+        out_specs=[HBM, VM],
+    )(received, factor, wet, token)
+    gap = lax.all_to_all(gap, ("gx", "gy"), 0, 0)
+    out, top, bottom = regridded(received, after)
     lower, upper = shifted(top, "gx", -1), shifted(bottom, "gx", 1)
     packed = shape(BAND, LANES)
     one, three = call(
@@ -892,20 +888,23 @@
         [HBM] + [VM] * 6 + [HBM, HBM],
     )(fixed, out, upper, lower, one, three, gap, hs, us)
 
-    whole, token = call(
+    everyone = shape(2 * peers, 1, LANES)
+    whole, token, gap = call(
         second_rest,
-        [shape(LEVELS, CX, CY), shape(8, LANES)],
+        [shape(LEVELS, CX, CY), shape(8, LANES), everyone],
         [
-            field_buf(SUB), field_buf(SUB),
-            band_buf(3), band_buf(3), pltpu.SemaphoreType.DMA((2,)),
+            field_buf(SUB), field_buf(SUB), band_buf(3), band_buf(3),
+            pltpu.VMEM(everyone.shape, F32), pltpu.SemaphoreType.DMA((3,)),
         ],
-        [VM, VM, VM, HBM, HBM, VM, pl.BlockSpec(memory_space=pl.ANY)],
-        out_specs=[pl.BlockSpec((SUB, CX, CY), lambda i: (0, 0, 0)), VM],
+        [VM, VM, VM, HBM, HBM, VM, VM, VM, VM, pl.BlockSpec(memory_space=pl.ANY)],
+        out_specs=[pl.BlockSpec((SUB, CX, CY), lambda i: (0, 0, 0)), VM, HBM],
         grid=(1,),
-        input_output_aliases={6: 0},
-    )(coeff, hx, ux, hs_rest, us_rest, final0, whole)
-
-    out, _, _, gap = exchange(series, token)
+        input_output_aliases={9: 0},
+    )(coeff, hx, ux, hs_rest, us_rest, final0, series, other, wet, whole)
+
+    received = paired(series, "comp", 1)
+    gap = lax.all_to_all(gap, ("comp", "gx", "gy"), 0, 0)
+    out, _, _ = regridded(received, token)
     (forcing,) = call(finish, [shape(SUB, CX, CY)], [], [VM] * 3)(out, land_mask, gap)
     return whole[None], forcing[None]
 

time: 85.1 us -> 80.8 us (0.949)
  waiting for transfers between devices: 16.6 us -> 14 us
    ppermute x6 -> x7, waiting for transfers between devices: 5.49 us -> 2.84 us  [paired(): lax.ppermute(value, axis, [(i, i ^ mask) for i in range(lax.axis_size(axi...]
    all_to_all x2, waiting for transfers between devices: 8.66 us -> 11.2 us  [the longest x1 6.57 us: per_device(): gap = lax.all_to_all(gap, ('comp', 'gx', 'gy'), 0, 0)]
    ppermute x4, waiting for transfers between devices: 2.44 us -> 0.01 us  [shifted(): return lax.ppermute(value, axis, [(i, (i + by) % n) for i in range(n)])]
    all_to_all x2, starting transfers between devices: 13.4 us -> 11.2 us  [the longest x1 5.64 us: per_device(): gap = lax.all_to_all(gap, ('gx', 'gy'), 0, 0)]
    ppermute x6 -> x7, starting transfers between devices: 10.1 us -> 11.7 us  [paired(): lax.ppermute(value, axis, [(i, i ^ mask) for i in range(lax.axis_size(axi...]
    pallas_call x5 -> x4, Pallas kernels: 10 us -> 8.68 us  [the longest x2 5.97 us: regridded(): call(regrid, [shape(SUB, CX, CY), edges, edges], [pltpu.VMEM((BLOCKS * 8,...]
  transfers between devices with their start and end apart: 12 -> 13, of which waited for: 5 -> 4; matrix products, arithmetic and copies ran while one was open for 0% -> 0% of each run, Pallas kernels for 18% -> 20%
where the time goes in v6:
time: 80.8 us; the launch traced here: 80.4 us
  starting transfers between devices  35 us (43%)
  Pallas kernels  29.5 us (37%)
  waiting for transfers between devices  14 us (17%)
  local copies, waits for them, and re-layouts  0.99 us (1%)
  between operations  0.9 us (1%)
    ppermute x4, starting transfers between devices, shifted(): return lax.ppermute(value, axis, [(i, (i + by) % n) for i in range(n)])  12.1 us
    ppermute x7, starting transfers between devices, paired(): lax.ppermute(value, axis, [(i, i ^ mask) for i in range(lax.axis_size(axi...  11.7 us
    all_to_all x1, waiting for transfers between devices, per_device(): gap = lax.all_to_all(gap, ('comp', 'gx', 'gy'), 0, 0)  6.57 us
    pallas_call x2, Pallas kernels, regridded(): call(regrid, [shape(SUB, CX, CY), edges, edges], [pltpu.VMEM((BLOCKS * 8,...  5.97 us
    pallas_call x1, Pallas kernels, per_device(): call(first_rest, [shape(LEVELS, CX, CY), band(3), band(3), shape(8, LANES...  5.82 us
    all_to_all x1, starting transfers between devices, per_device(): gap = lax.all_to_all(gap, ('gx', 'gy'), 0, 0)  5.64 us
    all_to_all x1, starting transfers between devices, per_device(): gap = lax.all_to_all(gap, ('comp', 'gx', 'gy'), 0, 0)  5.59 us
    all_to_all x1, waiting for transfers between devices, per_device(): gap = lax.all_to_all(gap, ('gx', 'gy'), 0, 0)  4.6 us
  transfers between devices with their start and end apart: 13, of which 4 were waited for; matrix products, arithmetic and copies ran while one was open for 0% of the time, Pallas kernels for 20%

profile of v6, /device:TPU:1, one launch (start us, length us, event | category | flops | bytes accessed | tf_op | source)
XLA Modules:
  0.0 80.4 jit_solution(1918529884545149831)
XLA Ops:
  0.7 2.1 %shard_map.113 = (f32[16,8,512]{2,1,0:T(8,128)}, f32[16,8,512]{2,1,0:T(8,128)}) custom-call(f32[16,32,512]{2,1,0:T(8,128)} %bitcast.14, bf16[6,32,512]{2,1,0:T(8,128)(2,1)} %bitcast.21, f32[32,512]{1,0:T(8,128)} %bitcast.24, f32[32,512]{1,0:T(8,128)} %land.3, s32[32,512]{1,0:T(8,128)} %mask.6), custom_call_target="tpu_custom_call" | custom-call | tf_op jit(solution)/shard_map/pallas_call | solution.py:776
  2.8 2.1 %collective-permute-start = (f32[16,8,512]{2,1,0:T(8,128)}, f32[16,8,512]{2,1,0:T(8,128)S(1)}, u32[]{:S(2)}, u32[]{:S(2)}) collective-permute-start(f32[16,8,512]{2,1,0:T(8,128)} %get-tuple-element.58), channel_id=1, source_target_pairs={{0,4},{4,8},{8,12},{12,16},{16,20},{20,24},{24,28},{28,32},{32,36}... | collective-permute-start | bytes 786440 | tf_op jit(solution)/shard_map/ppermute | solution.py:756
  4.9 4.8 %collective-permute-start.1 = (f32[16,8,512]{2,1,0:T(8,128)}, f32[16,8,512]{2,1,0:T(8,128)S(1)}, u32[]{:S(2)}, u32[]{:S(2)}) collective-permute-start(f32[16,8,512]{2,1,0:T(8,128)} %get-tuple-element.52.after), channel_id=1, source_target_pairs={{0,60},{4,0},{8,4},{12,8},{16,12},{20,16},{24,20},{28,24},{32,28},... | collective-permute-start | bytes 786440 | tf_op jit(solution)/shard_map/ppermute | solution.py:756
  9.8 0.9 %copy-done.6 = f32[16,8,512]{2,1,0:T(8,128)S(1)} copy-done((f32[16,8,512]{2,1,0:T(8,128)S(1)}, f32[16,8,512]{2,1,0:T(8,128)}, u32[]{:S(2)}) %copy-start.6) | copy-done | bytes 262168
  10.8 2.7 %shard_map.114 = (f32[32,512]{1,0:T(8,128)S(1)}, f32[1,128]{1,0:T(1,128)S(1)}, f32[32,8,128]{2,1,0:T(8,128)S(1)}) custom-call(f32[16]{0:T(128)S(1)} %bitcast.33, f32[15]{0:T(128)S(1)} %bitcast.34, s32[4,2,32]{2,1,0:T(2,128)S(1)} %bitcast.27, s32[4,2,32]{2,1,0:T(2,128)S(1)} %bitcast.30, bf16[32,128,128]{2,1,0:T(8,128)(2,1)S(1)} %bitcast.18, ...), custom_call_target="tpu_custom_call" | custom-call | tf_op jit(solution)/shard_map/pallas_call | solution.py:798
  13.5 3.0 %collective-permute-start.4 = (f32[32,512]{1,0:T(8,128)S(1)}, f32[32,512]{1,0:T(8,128)S(1)}, u32[]{:S(2)}, u32[]{:S(2)}) collective-permute-start(f32[32,512]{1,0:T(8,128)S(1)} %get-tuple-element.63.factor), channel_id=1, source_target_pairs={{0,64},{64,0},{1,65},{65,1},{2,66},{66,2},{3,67},{67,3},{4,68},{68... | collective-permute-start | bytes 196616 | tf_op jit(solution)/shard_map/ppermute | solution.py:760
  16.9 1.3 %collective-permute-start.2 = (f32[48,256]{1,0:T(8,128)S(1)}, f32[48,256]{1,0:T(8,128)S(1)}, u32[]{:S(2)}, u32[]{:S(2)}) collective-permute-start(f32[48,256]{1,0:T(8,128)S(1)} %get-tuple-element.61), channel_id=1, source_target_pairs={{0,1},{1,0},{2,3},{3,2},{4,5},{5,4},{6,7},{7,6},{8,9},{9,8},{10,11... | collective-permute-start | bytes 147464 | tf_op jit(solution)/shard_map/ppermute | solution.py:760
  19.1 2.6 %collective-permute-done.3.three = f32[48,256]{1,0:T(8,128)S(1)} collective-permute-done((f32[48,256]{1,0:T(8,128)S(1)}, f32[48,256]{1,0:T(8,128)S(1)}, u32[]{:S(2)}, u32[]{:S(2)}) %collective-permute-start.3) | collective-permute-done | bytes 49184 | tf_op jit(solution)/shard_map/ppermute | solution.py:760
  21.7 4.0 %shard_map.116 = (bf16[6,32,512]{2,1,0:T(8,128)(2,1)S(1)}, f32[6,48,640]{2,1,0:T(8,128)S(1)}, f32[6,48,640]{2,1,0:T(8,128)S(1)}, f32[3,48,640]{2,1,0:T(8,128)S(1...) custom-call(f32[32,8,128]{2,1,0:T(8,128)S(1)} %get-tuple-element.53.coeff, f32[16,32,512]{2,1,0:T(8,128)S(1)} %bitcast.16, ...), custom_call_target="tpu_custom_call" | custom-call | tf_op jit(solution)/shard_map/pallas_call | solution.py:818
  25.7 2.4 %collective-permute-start.5 = (bf16[6,32,512]{2,1,0:T(8,128)(2,1)S(1)}, bf16[6,32,512]{2,1,0:T(8,128)(2,1)S(1)}, u32[]{:S(2)}, u32[]{:S(2)}) collective-permute-start(bf16[6,32,512]{2,1,0:T(8,128)(2,1)S(1)} %get-tuple-element.65), channel_id=1, source_target_pairs={{0,64},{64,0},{1,65},{65,1},{2,66},{66,2},{3,67},{67,3},{4,68},{68... | collective-permute-start | bytes 589832 | tf_op jit(solution)/shard_map/ppermute | solution.py:760
  28.2 5.8 %shard_map.117 = (f32[16,32,512]{2,1,0:T(8,128)}, f32[3,48,640]{2,1,0:T(8,128)S(1)}, f32[3,48,640]{2,1,0:T(8,128)S(1)}, f32[8,128]{1,0:T(8,128)S(1)}) custom-call(f32[32,8,128]{2,1,0:T(8,128)S(1)} %get-tuple-element.53.coeff, f32[16,32,512]{2,1,0:T(8,128)S(1)} %bitcast.17, f32[16,8,512]{2,1,0:T(8,128)S(1)} %collective-permute-done.upper, ...), custom_call_target="tpu_custom_call" | custom-call | tf_op jit(solution)/shard_map/pallas_call | solution.py:851
  34.2 3.0 %shard_map.119 = (f32[6,32,512]{2,1,0:T(8,128)S(1)}, f32[2,8,512]{2,1,0:T(8,128)}, f32[2,8,512]{2,1,0:T(8,128)}) custom-call(s32[4,2,32]{2,1,0:T(2,128)S(1)} %bitcast.28, s32[4,2,32]{2,1,0:T(2,128)S(1)} %bitcast.31, bf16[6,32,512]{2,1,0:T(8,128)(2,1)S(1)} %collective-permute-done.5.received, bf16[32,128,128]{2,1,0:T(8,128)(2,1)S(1)} %bitcast.19, ...), custom_call_target="tpu_custom_call" | custom-call | flops 67108864 | bytes 8388608 | tf_op jit(solution)/shard_map/pallas_call | solution.py:834
  37.3 5.1 %collective-permute-start.7 = (f32[2,8,512]{2,1,0:T(8,128)}, f32[2,8,512]{2,1,0:T(8,128)}, u32[]{:S(2)}, u32[]{:S(2)}) collective-permute-start(f32[2,8,512]{2,1,0:T(8,128)} %get-tuple-element.72), channel_id=1, source_target_pairs={{0,60},{4,0},{8,4},{12,8},{16,12},{20,16},{24,20},{28,24},{32,28},... | collective-permute-start | bytes 98312 | tf_op jit(solution)/shard_map/ppermute | solution.py:756
  42.4 5.6 %all-to-all-start = ((f32[64,1,128]{2,1,0:T(1,128)}), f32[64,1,128]{2,1,0:T(1,128)}, u32[]{:S(2)}, u32[]{:S(2)}) async-start(f32[64,1,128]{2,1,0:T(1,128)} %copy-done.9), calls=%async_computation | async-start | bytes 65536 | tf_op jit(solution)/shard_map/all_to_all | solution.py:871
  48.1 1.5 %shard_map.120 = (f32[48,128]{1,0:T(8,128)}, f32[48,128]{1,0:T(8,128)}) custom-call(f32[6,32,512]{2,1,0:T(8,128)S(1)} %get-tuple-element.70.out.regridded, f32[2,8,512]{2,1,0:T(8,128)} %collective-permute-done.6.upper, f32[2,8,512]{2,1,0:T(8,128)} %collective-permute-done.7.lower), custom_call_target="tpu_custom_call" | custom-call | tf_op jit(solution)/shard_map/pallas_call | solution.py:875
  50.2 1.2 %collective-permute-start.9 = (f32[48,128]{1,0:T(8,128)}, f32[48,128]{1,0:T(8,128)}, u32[]{:S(2)}, u32[]{:S(2)}) collective-permute-start(f32[48,128]{1,0:T(8,128)} %get-tuple-element.74), channel_id=1, source_target_pairs={{0,3},{1,2},{2,1},{3,0},{4,7},{5,6},{6,5},{7,4},{8,11},{9,10},{10,... | collective-permute-start | bytes 73736 | tf_op jit(solution)/shard_map/ppermute | solution.py:760
  51.4 4.6 %all-to-all-done.gap = f32[64,1,128]{2,1,0:T(1,128)} async-done(((f32[64,1,128]{2,1,0:T(1,128)}), f32[64,1,128]{2,1,0:T(1,128)}, u32[]{:S(2)}, u32[]{:S(2)}) %all-to-all-start) | async-done | bytes 32800 | tf_op jit(solution)/shard_map/all_to_all | solution.py:871
  56.0 3.3 %shard_map.121 = (bf16[6,32,512]{2,1,0:T(8,128)(2,1)}, f32[32,512]{1,0:T(8,128)S(1)}, f32[3,48,640]{2,1,0:T(8,128)S(1)}, f32[3,48,640]{2,1,0:T(8,128)S(1)}, f32[32,8,128]{2,1,0:T(8,128)S(1)}) custom-call(f32[4,48,640]{2,1,0:T(8,128)S(1)} %get-tuple-element.64.fixed_in, f32[6,32,512]{2,1,0:T(8,128)S(1)} %get-tuple-element.70.out.regridded, ...), custom_call_target="tpu_custom_call" | custom-call | tf_op jit(solution)/shard_map/pallas_call | solution.py:880
  59.3 2.5 %collective-permute-start.10 = (bf16[6,32,512]{2,1,0:T(8,128)(2,1)}, bf16[6,32,512]{2,1,0:T(8,128)(2,1)S(1)}, u32[]{:S(2)}, u32[]{:S(2)}) collective-permute-start(bf16[6,32,512]{2,1,0:T(8,128)(2,1)} %get-tuple-element.84.series), channel_id=1, source_target_pairs={{0,64},{64,0},{1,65},{65,1},{2,66},{66,2},{3,67},{67,3},{4,68},{68... | collective-permute-start | bytes 589832 | tf_op jit(solution)/shard_map/ppermute | solution.py:760
  61.8 2.5 %shard_map.122 = (f32[16,32,512]{2,1,0:T(8,128)}, f32[8,128]{1,0:T(8,128)S(1)}, f32[128,1,128]{2,1,0:T(1,128)}) custom-call(f32[32,8,128]{2,1,0:T(8,128)S(1)} %get-tuple-element.78.coeff, f32[3,48,640]{2,1,0:T(8,128)S(1)} %get-tuple-element.79.hx, f32[3,48,640]{2,1,0:T(8,128)S(1)} %get-tuple-element.80.ux, ...), custom_call_target="tpu_custom_call", output_to_operand_aliasing={{0}: (9, {})} | custom-call | tf_op jit(solution)/shard_map/pallas_call | solution.py:892
  64.3 5.6 %all-to-all-start.1 = ((f32[128,1,128]{2,1,0:T(1,128)}), f32[128,1,128]{2,1,0:T(1,128)S(1)}, u32[]{:S(2)}, u32[]{:S(2)}) async-start(f32[128,1,128]{2,1,0:T(1,128)} %get-tuple-element.89), calls=%async_computation.1 | async-start | bytes 131072 | tf_op jit(solution)/shard_map/all_to_all | solution.py:906
  69.9 3.0 %shard_map.123 = (f32[6,32,512]{2,1,0:T(8,128)S(1)}, f32[2,8,512]{2,1,0:T(8,128)}, f32[2,8,512]{2,1,0:T(8,128)}) custom-call(s32[4,2,32]{2,1,0:T(2,128)S(1)} %bitcast.29, s32[4,2,32]{2,1,0:T(2,128)S(1)} %bitcast.32, bf16[6,32,512]{2,1,0:T(8,128)(2,1)S(1)} %collective-permute-done.10.received, bf16[32,128,128]{2,1,0:T(8,128)(2,1)S(1)} %bitcast.20, ...), custom_call_target="tpu_custom_call" | custom-call | flops 67108864 | bytes 8388608 | tf_op jit(solution)/shard_map/pallas_call | solution.py:834
  72.9 6.6 %all-to-all-done.1.gap = f32[128,1,128]{2,1,0:T(1,128)S(1)} async-done(((f32[128,1,128]{2,1,0:T(1,128)}), f32[128,1,128]{2,1,0:T(1,128)S(1)}, u32[]{:S(2)}, u32[]{:S(2)}) %all-to-all-start.1) | async-done | bytes 65568 | tf_op jit(solution)/shard_map/all_to_all | solution.py:906
  79.5 0.9 %shard_map.124 = f32[6,32,512]{2,1,0:T(8,128)} custom-call(f32[6,32,512]{2,1,0:T(8,128)S(1)} %get-tuple-element.88.regridded, s32[32,512]{1,0:T(8,128)S(1)} %copy-done.3, f32[128,1,128]{2,1,0:T(1,128)S(1)} %all-to-all-done.1.gap), custom_call_target="tpu_custom_call" | custom-call | tf_op jit(solution)/shard_map/pallas_call | solution.py:908
  (38 shorter events, 2.2 us)
Async XLA Ops:
  0.6 9.1 %copy-start.1 = (bf16[1,32,128,128]{3,2,1,0:T(8,128)(2,1)S(1)}, bf16[1,32,128,128]{3,2,1,0:T(8,128)(2,1)}, u32[]{:S(2)}) copy-start(bf16[1,32,128,128]{3,2,1,0:T(8,128)(2,1)} %param.17) | copy-start | bytes 3145732
  0.6 9.1 %copy-start.3 = (s32[32,512]{1,0:T(8,128)S(1)}, s32[32,512]{1,0:T(8,128)}, u32[]{:S(2)}) copy-start(s32[32,512]{1,0:T(8,128)} %mask.6) | copy-start | bytes 196612
  0.7 9.1 %copy-start.7 = (s32[1,32,4,2]{1,3,2,0:T(2,128)S(1)}, s32[1,32,4,2]{1,3,2,0:T(2,128)}, u32[]{:S(2)}) copy-start(s32[1,32,4,2]{1,3,2,0:T(2,128)} %param.18) | copy-start | bytes 3076
  0.7 9.1 %copy-start.8 = (s32[1,32,4,2]{1,3,2,0:T(2,128)S(1)}, s32[1,32,4,2]{1,3,2,0:T(2,128)}, u32[]{:S(2)}) copy-start(s32[1,32,4,2]{1,3,2,0:T(2,128)} %param.19) | copy-start | bytes 3076
  0.7 9.1 %copy-start.10 = (f32[1,16]{1,0:T(1,128)S(1)}, f32[1,16]{1,0:T(1,128)}, u32[]{:S(2)}) copy-start(f32[1,16]{1,0:T(1,128)} %param.12) | copy-start | bytes 196
  0.7 9.1 %copy-start.11 = (f32[1,15]{1,0:T(1,128)S(1)}, f32[1,15]{1,0:T(1,128)}, u32[]{:S(2)}) copy-start(f32[1,15]{1,0:T(1,128)} %param.13) | copy-start | bytes 184
  2.8 13.7 %copy-start = (f32[1,16,32,512]{3,2,1,0:T(8,128)S(1)}, f32[1,16,32,512]{3,2,1,0:T(8,128)}, u32[]{:S(2)}) copy-start(f32[1,16,32,512]{3,2,1,0:T(8,128)} %param.10) | copy-start | bytes 3145732
  2.8 13.6 %collective-permute-start = (f32[16,8,512]{2,1,0:T(8,128)}, f32[16,8,512]{2,1,0:T(8,128)S(1)}, u32[]{:S(2)}, u32[]{:S(2)}) collective-permute-start(f32[16,8,512]{2,1,0:T(8,128)} %get-tuple-element.58), channel_id=1, source_target_pairs={{0,4},{4,8},{8,12},{12,16},{16,20},{20,24},{24,28},{28,32},{32,36}... | collective-permute-start | bytes 786440 | tf_op jit(solution)/shard_map/ppermute | solution.py:756
  4.9 11.5 %collective-permute-start.1 = (f32[16,8,512]{2,1,0:T(8,128)}, f32[16,8,512]{2,1,0:T(8,128)S(1)}, u32[]{:S(2)}, u32[]{:S(2)}) collective-permute-start(f32[16,8,512]{2,1,0:T(8,128)} %get-tuple-element.52.after), channel_id=1, source_target_pairs={{0,60},{4,0},{8,4},{12,8},{16,12},{20,16},{24,20},{28,24},{32,28},... | collective-permute-start | bytes 786440 | tf_op jit(solution)/shard_map/ppermute | solution.py:756
  10.8 5.7 %copy-start.2 = (bf16[1,6,32,512]{3,2,1,0:T(8,128)(2,1)S(1)}, bf16[1,6,32,512]{3,2,1,0:T(8,128)(2,1)}, u32[]{:S(2)}) copy-start(bf16[1,6,32,512]{3,2,1,0:T(8,128)(2,1)} %param.11) | copy-start | bytes 589828
  10.8 5.7 %copy-start.4 = (f32[1,32,512]{2,1,0:T(8,128)S(1)}, f32[1,32,512]{2,1,0:T(8,128)}, u32[]{:S(2)}) copy-start(f32[1,32,512]{2,1,0:T(8,128)} %param.14) | copy-start | bytes 196612
  10.8 5.7 %copy-start.5 = (f32[32,512]{1,0:T(8,128)S(1)}, f32[32,512]{1,0:T(8,128)}, u32[]{:S(2)}) copy-start(f32[32,512]{1,0:T(8,128)} %land.3) | copy-start | bytes 196612
  13.5 5.4 %collective-permute-start.4 = (f32[32,512]{1,0:T(8,128)S(1)}, f32[32,512]{1,0:T(8,128)S(1)}, u32[]{:S(2)}, u32[]{:S(2)}) collective-permute-start(f32[32,512]{1,0:T(8,128)S(1)} %get-tuple-element.63.factor), channel_id=1, source_target_pairs={{0,64},{64,0},{1,65},{65,1},{2,66},{66,2},{3,67},{67,3},{4,68},{68... | collective-permute-start | bytes 196616 | tf_op jit(solution)/shard_map/ppermute | solution.py:760
  16.9 2.2 %collective-permute-start.2 = (f32[48,256]{1,0:T(8,128)S(1)}, f32[48,256]{1,0:T(8,128)S(1)}, u32[]{:S(2)}, u32[]{:S(2)}) collective-permute-start(f32[48,256]{1,0:T(8,128)S(1)} %get-tuple-element.61), channel_id=1, source_target_pairs={{0,1},{1,0},{2,3},{3,2},{4,5},{5,4},{6,7},{7,6},{8,9},{9,8},{10,11... | collective-permute-start | bytes 147464 | tf_op jit(solution)/shard_map/ppermute | solution.py:760
  18.2 3.5 %collective-permute-start.3 = (f32[48,256]{1,0:T(8,128)S(1)}, f32[48,256]{1,0:T(8,128)S(1)}, u32[]{:S(2)}, u32[]{:S(2)}) collective-permute-start(f32[48,256]{1,0:T(8,128)S(1)} %get-tuple-element.62), channel_id=1, source_target_pairs={{0,3},{1,2},{2,1},{3,0},{4,7},{5,6},{6,5},{7,4},{8,11},{9,10},{10,... | collective-permute-start | bytes 147464 | tf_op jit(solution)/shard_map/ppermute | solution.py:760
  25.7 8.3 %collective-permute-start.5 = (bf16[6,32,512]{2,1,0:T(8,128)(2,1)S(1)}, bf16[6,32,512]{2,1,0:T(8,128)(2,1)S(1)}, u32[]{:S(2)}, u32[]{:S(2)}) collective-permute-start(bf16[6,32,512]{2,1,0:T(8,128)(2,1)S(1)} %get-tuple-element.65), channel_id=1, source_target_pairs={{0,64},{64,0},{1,65},{65,1},{2,66},{66,2},{3,67},{67,3},{4,68},{68... | collective-permute-start | bytes 589832 | tf_op jit(solution)/shard_map/ppermute | solution.py:760
  34.2 3.0 %copy-start.9 = (f32[64,1,128]{2,1,0:T(1,128)}, f32[64,1,128]{2,1,0:T(1,128)S(1)}, u32[]{:S(2)}) copy-start(f32[64,1,128]{2,1,0:T(1,128)S(1)} %get-tuple-element.75) | copy-start | bytes 98308
  37.2 10.8 %collective-permute-start.6 = (f32[2,8,512]{2,1,0:T(8,128)}, f32[2,8,512]{2,1,0:T(8,128)}, u32[]{:S(2)}, u32[]{:S(2)}) collective-permute-start(f32[2,8,512]{2,1,0:T(8,128)} %get-tuple-element.71), channel_id=1, source_target_pairs={{0,4},{4,8},{8,12},{12,16},{16,20},{20,24},{24,28},{28,32},{32,36}... | collective-permute-start | bytes 98312 | tf_op jit(solution)/shard_map/ppermute | solution.py:756
  37.3 10.8 %collective-permute-start.7 = (f32[2,8,512]{2,1,0:T(8,128)}, f32[2,8,512]{2,1,0:T(8,128)}, u32[]{:S(2)}, u32[]{:S(2)}) collective-permute-start(f32[2,8,512]{2,1,0:T(8,128)} %get-tuple-element.72), channel_id=1, source_target_pairs={{0,60},{4,0},{8,4},{12,8},{16,12},{20,16},{24,20},{28,24},{32,28},... | collective-permute-start | bytes 98312 | tf_op jit(solution)/shard_map/ppermute | solution.py:756
  42.4 13.6 %all-to-all-start = ((f32[64,1,128]{2,1,0:T(1,128)}), f32[64,1,128]{2,1,0:T(1,128)}, u32[]{:S(2)}, u32[]{:S(2)}) async-start(f32[64,1,128]{2,1,0:T(1,128)} %copy-done.9), calls=%async_computation | async-start | bytes 65536 | tf_op jit(solution)/shard_map/all_to_all | solution.py:871
  49.6 6.4 %collective-permute-start.8 = (f32[48,128]{1,0:T(8,128)}, f32[48,128]{1,0:T(8,128)}, u32[]{:S(2)}, u32[]{:S(2)}) collective-permute-start(f32[48,128]{1,0:T(8,128)} %get-tuple-element.73), channel_id=1, source_target_pairs={{0,1},{1,0},{2,3},{3,2},{4,5},{5,4},{6,7},{7,6},{8,9},{9,8},{10,11... | collective-permute-start | bytes 73736 | tf_op jit(solution)/shard_map/ppermute | solution.py:760
  50.2 5.8 %collective-permute-start.9 = (f32[48,128]{1,0:T(8,128)}, f32[48,128]{1,0:T(8,128)}, u32[]{:S(2)}, u32[]{:S(2)}) collective-permute-start(f32[48,128]{1,0:T(8,128)} %get-tuple-element.74), channel_id=1, source_target_pairs={{0,3},{1,2},{2,1},{3,0},{4,7},{5,6},{6,5},{7,4},{8,11},{9,10},{10,... | collective-permute-start | bytes 73736 | tf_op jit(solution)/shard_map/ppermute | solution.py:760
  59.3 10.6 %collective-permute-start.10 = (bf16[6,32,512]{2,1,0:T(8,128)(2,1)}, bf16[6,32,512]{2,1,0:T(8,128)(2,1)S(1)}, u32[]{:S(2)}, u32[]{:S(2)}) collective-permute-start(bf16[6,32,512]{2,1,0:T(8,128)(2,1)} %get-tuple-element.84.series), channel_id=1, source_target_pairs={{0,64},{64,0},{1,65},{65,1},{2,66},{66,2},{3,67},{67,3},{4,68},{68... | collective-permute-start | bytes 589832 | tf_op jit(solution)/shard_map/ppermute | solution.py:760
  64.3 15.2 %all-to-all-start.1 = ((f32[128,1,128]{2,1,0:T(1,128)}), f32[128,1,128]{2,1,0:T(1,128)S(1)}, u32[]{:S(2)}, u32[]{:S(2)}) async-start(f32[128,1,128]{2,1,0:T(1,128)} %get-tuple-element.89), calls=%async_computation.1 | async-start | bytes 131072 | tf_op jit(solution)/shard_map/all_to_all | solution.py:906
  (1 other events, 1.0 us)

commit v7 on v6

--- a/solution.py
+++ b/solution.py
@@ -436,7 +436,8 @@
                     v = h
                 if l == t and t >= 3:
                     strip.save(us, t - 3, v)
-                    strip.save(hs, t - 3, h)
+                    if t > 3:
+                        strip.save(hs, t - 4, h)
                 v = less(v, u_prev)
                 if t < SUB - 1:
                     strip.store(dst, l, v)
@@ -520,7 +521,7 @@
     total = jnp.sum(total, axis=1, keepdims=True)
     total = jnp.sum(jnp.where(row == lane, total, 0.0), axis=0, keepdims=True) + wet[...]
     for k in range(rows.shape[0]):
-        rows[k] = total
+        rows[k] = jnp.broadcast_to(total, rows.shape[1:])
 
 
 def losses(
@@ -591,7 +592,15 @@
         halo[t, 8 : 8 + n, :] = lower[tile, start : start + n, :]
 
 
-def pack_second(out, upper, lower, one, three, halo):
+def pack_second(out, upper_in, lower_in, one, three, halo, upper, lower, sems):
+    reads = [
+        pltpu.make_async_copy(upper_in, upper, sems.at[0]),
+        pltpu.make_async_copy(lower_in, lower, sems.at[1]),
+    ]
+    for c in reads:
+        c.start()
+    for c in reads:
+        c.wait()
     even, _, _ = position()
     halo_rows(halo, upper, lower)
 
@@ -609,7 +618,7 @@
 
 
 def gap_means(gap, start, count):
-    total = jnp.sum(gap[pl.ds(start, count)], axis=0)
+    total = jnp.sum(gap[pl.ds(start, count), 0:1], axis=0)
     lane = lax.broadcasted_iota(jnp.int32, (1, LANES), 1)
     wet = jnp.sum(jnp.where(lane == SUB, total, 0.0), axis=1, keepdims=True)
     return [
@@ -618,12 +627,15 @@
 
 
 def second_cone(
-    fixed_in, regridded, upper, lower, one, three, gap, hs_in, us_in,
+    fixed_in, regridded, upper_in, lower_in, one_in, three_in, gap_in, hs_in, us_in,
     series, final0, hx, ux, coeff,
-    s0, s1, g, emitted, fixed, hs, us, halo, sems,
+    s0, s1, g, emitted, fixed, hs, us, halo, upper, lower, one, three, gap, sems,
 ):
     reads = []
-    pairs = ((us_in, us), (fixed_in, fixed), (hs_in, hs))
+    pairs = (
+        (upper_in, upper), (lower_in, lower), (one_in, one), (three_in, three), (gap_in, gap),
+        (us_in, us), (fixed_in, fixed), (hs_in, hs),
+    )
     for i, (src, dst) in enumerate(pairs):
         reads.append(pltpu.make_async_copy(src, dst, sems.at[i]))
         reads[-1].start()
@@ -631,12 +643,15 @@
     ocean = lax.axis_index("comp") == 1
     zero_pads(s0, 3)
     zero_pads(s1, 3)
+    for t in range(SUB):
+        g[t, 8 : 8 + CX, :CY] = regridded[t]
+    for c in reads[:5]:
+        c.wait()
     halo_rows(halo, upper, lower)
     for t in range(SUB):
         if t < SUB - 1:
             g[t, 0:8, :CY] = halo[t, 0:8, :]
             g[t, 8 + CX : 16 + CX, :CY] = halo[t, 8:16, :]
-        g[t, 8 : 8 + CX, :CY] = regridded[t]
 
     def put(f, tile, value):
         g[f, tile * 8 : tile * 8 + 8, CY:COLS] = value
@@ -644,7 +659,7 @@
     place_sides(put, list(range(SUB - 1)), one, three, even, first, last)
     g[SUB - 1, :, CY:COLS] = jnp.zeros((BAND, LANES), F32)
     means = [jnp.broadcast_to(v, (8, LANES)) for v in gap_means(gap, 0, gap.shape[0])]
-    for c in reads:
+    for c in reads[5:]:
         c.wait()
     for l in range(SUB):
         for i, start in ((l, 0), (SUB + l, LEVELS)):
@@ -726,7 +741,7 @@
                     if l + 1 < t:
                         h_next = strip.spread(src, l + 1, diff[l + 1])
                     else:
-                        h_next = strip.recall(hs, t - 3)
+                        h_next = strip.recall(hs, t - 4)
                     u = flux_between(mix[l], h_next, h)
                     v = added(h, u)
                     h = h_next
@@ -850,10 +865,10 @@
 
     whole, hs_rest, us_rest, token = call(
         first_rest,
-        [shape(LEVELS, CX, CY), band(3), band(3), shape(8, LANES)],
+        [shape(LEVELS, CX, CY), band(2), band(3), shape(8, LANES)],
         [
             field_buf(LEVELS), field_buf(LEVELS),
-            band_buf(3), band_buf(3), pltpu.SemaphoreType.DMA((2,)),
+            band_buf(2), band_buf(3), pltpu.SemaphoreType.DMA((2,)),
         ],
         [VM] * 8,
         out_specs=[VM, HBM, HBM, VM],
@@ -863,8 +878,8 @@
     peers = lax.axis_size(("gx", "gy"))
     gap, after = call(
         losses,
-        [shape(peers, 1, LANES), shape(8, LANES)],
-        [pltpu.VMEM((peers, 1, LANES), F32), pltpu.SemaphoreType.DMA(())],
+        [shape(peers, 2, LANES), shape(8, LANES)],
+        [pltpu.VMEM((peers, 2, LANES), F32), pltpu.SemaphoreType.DMA(())],
         [VM, VM, VM, VM],
         out_specs=[HBM, VM],
     )(received, factor, wet, token)
@@ -873,7 +888,15 @@
     lower, upper = shifted(top, "gx", -1), shifted(bottom, "gx", 1)
     packed = shape(BAND, LANES)
     one, three = call(
-        pack_second, [packed, packed], [pltpu.VMEM((SUB - 1, 16, CY), F32)], [VM] * 3
+        pack_second,
+        [packed, packed],
+        [
+            pltpu.VMEM((SUB - 1, 16, CY), F32),
+            pltpu.VMEM(upper.shape, F32),
+            pltpu.VMEM(lower.shape, F32),
+            pltpu.SemaphoreType.DMA((2,)),
+        ],
+        [VM, HBM, HBM],
     )(out, upper, lower)
     one, three = paired(one, "gy", 1), paired(three, "gy", 3)
 
@@ -883,9 +906,10 @@
         [
             field_buf(3), field_buf(3), band_buf(SUB), band_buf(SUB),
             band_buf(4), band_buf(3), band_buf(3), pltpu.VMEM((SUB - 1, 16, CY), F32),
-            pltpu.SemaphoreType.DMA((3,)),
+            *[pltpu.VMEM(v.shape, F32) for v in (upper, lower, one, three, gap)],
+            pltpu.SemaphoreType.DMA((8,)),
         ],
-        [HBM] + [VM] * 6 + [HBM, HBM],
+        [HBM, VM] + [HBM] * 7,
     )(fixed, out, upper, lower, one, three, gap, hs, us)
 
     everyone = shape(2 * peers, 1, LANES)
@@ -893,7 +917,7 @@
         second_rest,
         [shape(LEVELS, CX, CY), shape(8, LANES), everyone],
         [
-            field_buf(SUB), field_buf(SUB), band_buf(3), band_buf(3),
+            field_buf(SUB), field_buf(SUB), band_buf(2), band_buf(3),
             pltpu.VMEM(everyone.shape, F32), pltpu.SemaphoreType.DMA((3,)),
         ],
         [VM, VM, VM, HBM, HBM, VM, VM, VM, VM, pl.BlockSpec(memory_space=pl.ANY)],

time: 80.8 us -> 82.9 us (1.026)
  starting transfers between devices: 35 us -> 39.5 us
  Pallas kernels: 29.5 us -> 27.8 us
  waiting for transfers between devices: 14 us -> 12.7 us
    all_to_all x1, waiting for transfers between devices: 4.6 us -> 0.01 us  [per_device(): gap = lax.all_to_all(gap, ('gx', 'gy'), 0, 0)]
    ppermute x7, waiting for transfers between devices: 2.84 us -> 5 us  [paired(): lax.ppermute(value, axis, [(i, i ^ mask) for i in range(lax.axis_size(axi...]
    all_to_all x1, starting transfers between devices: 5.64 us -> 7.44 us  [per_device(): gap = lax.all_to_all(gap, ('gx', 'gy'), 0, 0)]
    all_to_all x1, starting transfers between devices: 5.59 us -> 7.31 us  [per_device(): gap = lax.all_to_all(gap, ('comp', 'gx', 'gy'), 0, 0)]
    ppermute x4, waiting for transfers between devices: 0.01 us -> 1.23 us  [shifted(): return lax.ppermute(value, axis, [(i, (i + by) % n) for i in range(n)])]
    ppermute x7, starting transfers between devices: 11.7 us -> 12.7 us  [paired(): lax.ppermute(value, axis, [(i, i ^ mask) for i in range(lax.axis_size(axi...]
    unnamed x24 -> x26, local copies, waits for them, and re-layouts: 0.99 us -> 1.68 us
  transfers between devices with their start and end apart: 13 -> 13, of which waited for: 4 -> 5; matrix products, arithmetic and copies ran while one was open for 0% -> 0% of each run, Pallas kernels for 20% -> 21%
where the time goes in v7:
time: 82.9 us; the launch traced here: 82.7 us
  starting transfers between devices  39.5 us (48%)
  Pallas kernels  27.8 us (34%)
  waiting for transfers between devices  12.7 us (15%)
  local copies, waits for them, and re-layouts  1.68 us (2%)
  between operations  0.88 us (1%)
    ppermute x7, starting transfers between devices, paired(): lax.ppermute(value, axis, [(i, i ^ mask) for i in range(lax.axis_size(axi...  12.7 us
    ppermute x4, starting transfers between devices, shifted(): return lax.ppermute(value, axis, [(i, (i + by) % n) for i in range(n)])  12.1 us
    all_to_all x1, starting transfers between devices, per_device(): gap = lax.all_to_all(gap, ('gx', 'gy'), 0, 0)  7.44 us
    all_to_all x1, starting transfers between devices, per_device(): gap = lax.all_to_all(gap, ('comp', 'gx', 'gy'), 0, 0)  7.31 us
    all_to_all x1, waiting for transfers between devices, per_device(): gap = lax.all_to_all(gap, ('comp', 'gx', 'gy'), 0, 0)  6.5 us
    pallas_call x1, Pallas kernels, per_device(): call(first_rest, [shape(LEVELS, CX, CY), band(2), band(3), shape(8, LANES...  5.91 us
    pallas_call x2, Pallas kernels, regridded(): call(regrid, [shape(SUB, CX, CY), edges, edges], [pltpu.VMEM((BLOCKS * 8,...  5.37 us
    ppermute x7, waiting for transfers between devices, paired(): lax.ppermute(value, axis, [(i, i ^ mask) for i in range(lax.axis_size(axi...  5 us
  transfers between devices with their start and end apart: 13, of which 5 were waited for; matrix products, arithmetic and copies ran while one was open for 0% of the time, Pallas kernels for 21%

profile of v7, /device:TPU:1, one launch (start us, length us, event | category | flops | bytes accessed | tf_op | source)
XLA Modules:
  0.0 82.7 jit_solution(7032952272842803051)
XLA Ops:
  0.7 2.1 %shard_map.113 = (f32[16,8,512]{2,1,0:T(8,128)}, f32[16,8,512]{2,1,0:T(8,128)}) custom-call(f32[16,32,512]{2,1,0:T(8,128)} %bitcast.14, bf16[6,32,512]{2,1,0:T(8,128)(2,1)} %bitcast.21, f32[32,512]{1,0:T(8,128)} %bitcast.24, f32[32,512]{1,0:T(8,128)} %land.3, s32[32,512]{1,0:T(8,128)} %mask.6), custom_call_target="tpu_custom_call" | custom-call | tf_op jit(solution)/shard_map/pallas_call | solution.py:791
  2.8 2.1 %collective-permute-start = (f32[16,8,512]{2,1,0:T(8,128)}, f32[16,8,512]{2,1,0:T(8,128)S(1)}, u32[]{:S(2)}, u32[]{:S(2)}) collective-permute-start(f32[16,8,512]{2,1,0:T(8,128)} %get-tuple-element.58), channel_id=1, source_target_pairs={{0,4},{4,8},{8,12},{12,16},{16,20},{20,24},{24,28},{28,32},{32,36}... | collective-permute-start | bytes 786440 | tf_op jit(solution)/shard_map/ppermute | solution.py:771
  4.9 4.8 %collective-permute-start.1 = (f32[16,8,512]{2,1,0:T(8,128)}, f32[16,8,512]{2,1,0:T(8,128)S(1)}, u32[]{:S(2)}, u32[]{:S(2)}) collective-permute-start(f32[16,8,512]{2,1,0:T(8,128)} %get-tuple-element.52.after), channel_id=1, source_target_pairs={{0,60},{4,0},{8,4},{12,8},{16,12},{20,16},{24,20},{28,24},{32,28},... | collective-permute-start | bytes 786440 | tf_op jit(solution)/shard_map/ppermute | solution.py:771
  10.8 2.7 %shard_map.114 = (f32[32,512]{1,0:T(8,128)S(1)}, f32[1,128]{1,0:T(1,128)S(1)}, f32[32,8,128]{2,1,0:T(8,128)S(1)}) custom-call(f32[16]{0:T(128)S(1)} %bitcast.33, f32[15]{0:T(128)S(1)} %bitcast.34, s32[4,2,32]{2,1,0:T(2,128)S(1)} %bitcast.27, s32[4,2,32]{2,1,0:T(2,128)S(1)} %bitcast.30, bf16[32,128,128]{2,1,0:T(8,128)(2,1)S(1)} %bitcast.18, ...), custom_call_target="tpu_custom_call" | custom-call | tf_op jit(solution)/shard_map/pallas_call | solution.py:813
  13.5 3.0 %collective-permute-start.4 = (f32[32,512]{1,0:T(8,128)S(1)}, f32[32,512]{1,0:T(8,128)S(1)}, u32[]{:S(2)}, u32[]{:S(2)}) collective-permute-start(f32[32,512]{1,0:T(8,128)S(1)} %get-tuple-element.63.factor), channel_id=1, source_target_pairs={{0,64},{64,0},{1,65},{65,1},{2,66},{66,2},{3,67},{67,3},{4,68},{68... | collective-permute-start | bytes 196616 | tf_op jit(solution)/shard_map/ppermute | solution.py:775
  16.9 1.3 %collective-permute-start.2 = (f32[48,256]{1,0:T(8,128)S(1)}, f32[48,256]{1,0:T(8,128)S(1)}, u32[]{:S(2)}, u32[]{:S(2)}) collective-permute-start(f32[48,256]{1,0:T(8,128)S(1)} %get-tuple-element.61), channel_id=1, source_target_pairs={{0,1},{1,0},{2,3},{3,2},{4,5},{5,4},{6,7},{7,6},{8,9},{9,8},{10,11... | collective-permute-start | bytes 147464 | tf_op jit(solution)/shard_map/ppermute | solution.py:775
  19.1 2.6 %collective-permute-done.3.three = f32[48,256]{1,0:T(8,128)S(1)} collective-permute-done((f32[48,256]{1,0:T(8,128)S(1)}, f32[48,256]{1,0:T(8,128)S(1)}, u32[]{:S(2)}, u32[]{:S(2)}) %collective-permute-start.3) | collective-permute-done | bytes 49184 | tf_op jit(solution)/shard_map/ppermute | solution.py:775
  21.7 4.0 %shard_map.116 = (bf16[6,32,512]{2,1,0:T(8,128)(2,1)S(1)}, f32[6,48,640]{2,1,0:T(8,128)S(1)}, f32[6,48,640]{2,1,0:T(8,128)S(1)}, f32[3,48,640]{2,1,0:T(8,128)S(1...) custom-call(f32[32,8,128]{2,1,0:T(8,128)S(1)} %get-tuple-element.53.coeff, f32[16,32,512]{2,1,0:T(8,128)S(1)} %bitcast.16, ...), custom_call_target="tpu_custom_call" | custom-call | tf_op jit(solution)/shard_map/pallas_call | solution.py:833
  25.7 2.4 %collective-permute-start.5 = (bf16[6,32,512]{2,1,0:T(8,128)(2,1)S(1)}, bf16[6,32,512]{2,1,0:T(8,128)(2,1)S(1)}, u32[]{:S(2)}, u32[]{:S(2)}) collective-permute-start(bf16[6,32,512]{2,1,0:T(8,128)(2,1)S(1)} %get-tuple-element.65), channel_id=1, source_target_pairs={{0,64},{64,0},{1,65},{65,1},{2,66},{66,2},{3,67},{67,3},{4,68},{68... | collective-permute-start | bytes 589832 | tf_op jit(solution)/shard_map/ppermute | solution.py:775
  28.2 5.9 %shard_map.117 = (f32[16,32,512]{2,1,0:T(8,128)}, f32[2,48,640]{2,1,0:T(8,128)S(1)}, f32[3,48,640]{2,1,0:T(8,128)S(1)}, f32[8,128]{1,0:T(8,128)S(1)}) custom-call(f32[32,8,128]{2,1,0:T(8,128)S(1)} %get-tuple-element.53.coeff, f32[16,32,512]{2,1,0:T(8,128)S(1)} %bitcast.17, f32[16,8,512]{2,1,0:T(8,128)S(1)} %collective-permute-done.upper, ...), custom_call_target="tpu_custom_call" | custom-call | tf_op jit(solution)/shard_map/pallas_call | solution.py:866
  35.6 7.4 %all-to-all-start = ((f32[64,2,128]{2,1,0:T(2,128)}), f32[64,2,128]{2,1,0:T(2,128)S(1)}, u32[]{:S(2)}, u32[]{:S(2)}) async-start(f32[64,2,128]{2,1,0:T(2,128)} %get-tuple-element.75), calls=%async_computation | async-start | bytes 131072 | tf_op jit(solution)/shard_map/all_to_all | solution.py:886
  43.0 2.4 %shard_map.119 = (f32[6,32,512]{2,1,0:T(8,128)S(1)}, f32[2,8,512]{2,1,0:T(8,128)S(1)}, f32[2,8,512]{2,1,0:T(8,128)S(1)}) custom-call(s32[4,2,32]{2,1,0:T(2,128)S(1)} %bitcast.28, s32[4,2,32]{2,1,0:T(2,128)S(1)} %bitcast.31, bf16[6,32,512]{2,1,0:T(8,128)(2,1)S(1)} %collective-permute-done.5.received, bf16[32,128,128]{2,1,0:T(8,128)(2,1)S(1)} %bitcast.19, ...), custom_call_target="tpu_custom_call" | custom-call | flops 67108864 | bytes 8388608 | tf_op jit(solution)/shard_map/pallas_call | solution.py:849
  45.4 1.5 %collective-permute-start.6 = (f32[2,8,512]{2,1,0:T(8,128)S(1)}, f32[2,8,512]{2,1,0:T(8,128)S(1)}, u32[]{:S(2)}, u32[]{:S(2)}) collective-permute-start(f32[2,8,512]{2,1,0:T(8,128)S(1)} %get-tuple-element.71), channel_id=1, source_target_pairs={{0,4},{4,8},{8,12},{12,16},{16,20},{20,24},{24,28},{28,32},{32,36}... | collective-permute-start | bytes 98312 | tf_op jit(solution)/shard_map/ppermute | solution.py:771
  46.9 3.7 %collective-permute-start.7 = (f32[2,8,512]{2,1,0:T(8,128)S(1)}, f32[2,8,512]{2,1,0:T(8,128)S(1)}, u32[]{:S(2)}, u32[]{:S(2)}) collective-permute-start(f32[2,8,512]{2,1,0:T(8,128)S(1)} %get-tuple-element.72), channel_id=1, source_target_pairs={{0,60},{4,0},{8,4},{12,8},{16,12},{20,16},{24,20},{28,24},{32,28},... | collective-permute-start | bytes 98312 | tf_op jit(solution)/shard_map/ppermute | solution.py:771
  50.6 1.2 %collective-permute-done.6.upper_in = f32[2,8,512]{2,1,0:T(8,128)S(1)} collective-permute-done((f32[2,8,512]{2,1,0:T(8,128)S(1)}, f32[2,8,512]{2,1,0:T(8,128)S(1)}, u32[]{:S(2)}, u32[]{:S(2)}) %collective-permute-start.6) | collective-permute-done | bytes 32800 | tf_op jit(solution)/shard_map/ppermute | solution.py:771
  52.0 1.6 %collective-permute-start.8 = (f32[48,128]{1,0:T(8,128)S(1)}, f32[48,128]{1,0:T(8,128)S(1)}, u32[]{:S(2)}, u32[]{:S(2)}) collective-permute-start(f32[48,128]{1,0:T(8,128)S(1)} %get-tuple-element.73), channel_id=1, source_target_pairs={{0,1},{1,0},{2,3},{3,2},{4,5},{5,4},{6,7},{7,6},{8,9},{9,8},{10,11... | collective-permute-start | bytes 73736 | tf_op jit(solution)/shard_map/ppermute | solution.py:775
  53.7 1.1 %collective-permute-start.9 = (f32[48,128]{1,0:T(8,128)S(1)}, f32[48,128]{1,0:T(8,128)S(1)}, u32[]{:S(2)}, u32[]{:S(2)}) collective-permute-start(f32[48,128]{1,0:T(8,128)S(1)} %get-tuple-element.74), channel_id=1, source_target_pairs={{0,3},{1,2},{2,1},{3,0},{4,7},{5,6},{6,5},{7,4},{8,11},{9,10},{10,... | collective-permute-start | bytes 73736 | tf_op jit(solution)/shard_map/ppermute | solution.py:775
  54.8 2.2 %collective-permute-done.9.three_in = f32[48,128]{1,0:T(8,128)S(1)} collective-permute-done((f32[48,128]{1,0:T(8,128)S(1)}, f32[48,128]{1,0:T(8,128)S(1)}, u32[]{:S(2)}, u32[]{:S(2)}) %collective-permute-start.9) | collective-permute-done | bytes 24608 | tf_op jit(solution)/shard_map/ppermute | solution.py:775
  56.9 2.8 %shard_map.121 = (bf16[6,32,512]{2,1,0:T(8,128)(2,1)}, f32[32,512]{1,0:T(8,128)S(1)}, f32[3,48,640]{2,1,0:T(8,128)S(1)}, f32[3,48,640]{2,1,0:T(8,128)S(1)}, f32[32,8,128]{2,1,0:T(8,128)S(1)}) custom-call(f32[4,48,640]{2,1,0:T(8,128)S(1)} %get-tuple-element.64.fixed_in, f32[6,32,512]{2,1,0:T(8,128)S(1)} %get-tuple-element.70.out.regridded, ...), custom_call_target="tpu_custom_call" | custom-call | tf_op jit(solution)/shard_map/pallas_call | solution.py:903
  59.7 2.6 %collective-permute-start.10 = (bf16[6,32,512]{2,1,0:T(8,128)(2,1)}, bf16[6,32,512]{2,1,0:T(8,128)(2,1)S(1)}, u32[]{:S(2)}, u32[]{:S(2)}) collective-permute-start(bf16[6,32,512]{2,1,0:T(8,128)(2,1)} %get-tuple-element.84.series), channel_id=1, source_target_pairs={{0,64},{64,0},{1,65},{65,1},{2,66},{66,2},{3,67},{67,3},{4,68},{68... | collective-permute-start | bytes 589832 | tf_op jit(solution)/shard_map/ppermute | solution.py:775
  62.3 2.7 %shard_map.122 = (f32[16,32,512]{2,1,0:T(8,128)}, f32[8,128]{1,0:T(8,128)S(1)}, f32[128,1,128]{2,1,0:T(1,128)}) custom-call(f32[32,8,128]{2,1,0:T(8,128)S(1)} %get-tuple-element.78.coeff, f32[3,48,640]{2,1,0:T(8,128)S(1)} %get-tuple-element.79.hx, f32[3,48,640]{2,1,0:T(8,128)S(1)} %get-tuple-element.80.ux, ...), custom_call_target="tpu_custom_call", output_to_operand_aliasing={{0}: (9, {})} | custom-call | tf_op jit(solution)/shard_map/pallas_call | solution.py:916
  64.9 7.3 %all-to-all-start.1 = ((f32[128,1,128]{2,1,0:T(1,128)}), f32[128,1,128]{2,1,0:T(1,128)S(1)}, u32[]{:S(2)}, u32[]{:S(2)}) async-start(f32[128,1,128]{2,1,0:T(1,128)} %get-tuple-element.89), calls=%async_computation.1 | async-start | bytes 131072 | tf_op jit(solution)/shard_map/all_to_all | solution.py:930
  72.2 3.0 %shard_map.123 = (f32[6,32,512]{2,1,0:T(8,128)S(1)}, f32[2,8,512]{2,1,0:T(8,128)}, f32[2,8,512]{2,1,0:T(8,128)}) custom-call(s32[4,2,32]{2,1,0:T(2,128)S(1)} %bitcast.29, s32[4,2,32]{2,1,0:T(2,128)S(1)} %bitcast.32, bf16[6,32,512]{2,1,0:T(8,128)(2,1)S(1)} %collective-permute-done.10.received, bf16[32,128,128]{2,1,0:T(8,128)(2,1)S(1)} %bitcast.20, ...), custom_call_target="tpu_custom_call" | custom-call | flops 67108864 | bytes 8388608 | tf_op jit(solution)/shard_map/pallas_call | solution.py:849
  75.2 6.5 %all-to-all-done.1.gap = f32[128,1,128]{2,1,0:T(1,128)S(1)} async-done(((f32[128,1,128]{2,1,0:T(1,128)}), f32[128,1,128]{2,1,0:T(1,128)S(1)}, u32[]{:S(2)}, u32[]{:S(2)}) %all-to-all-start.1) | async-done | bytes 65568 | tf_op jit(solution)/shard_map/all_to_all | solution.py:930
  (40 shorter events, 4.9 us)
Async XLA Ops:
  0.6 9.1 %copy-start.1 = (bf16[1,32,128,128]{3,2,1,0:T(8,128)(2,1)S(1)}, bf16[1,32,128,128]{3,2,1,0:T(8,128)(2,1)}, u32[]{:S(2)}) copy-start(bf16[1,32,128,128]{3,2,1,0:T(8,128)(2,1)} %param.17) | copy-start | bytes 3145732
  0.6 9.1 %copy-start.3 = (s32[32,512]{1,0:T(8,128)S(1)}, s32[32,512]{1,0:T(8,128)}, u32[]{:S(2)}) copy-start(s32[32,512]{1,0:T(8,128)} %mask.6) | copy-start | bytes 196612
  0.7 9.1 %copy-start.9 = (s32[1,32,4,2]{1,3,2,0:T(2,128)S(1)}, s32[1,32,4,2]{1,3,2,0:T(2,128)}, u32[]{:S(2)}) copy-start(s32[1,32,4,2]{1,3,2,0:T(2,128)} %param.18) | copy-start | bytes 3076
  0.7 9.1 %copy-start.10 = (s32[1,32,4,2]{1,3,2,0:T(2,128)S(1)}, s32[1,32,4,2]{1,3,2,0:T(2,128)}, u32[]{:S(2)}) copy-start(s32[1,32,4,2]{1,3,2,0:T(2,128)} %param.19) | copy-start | bytes 3076
  0.7 9.1 %copy-start.11 = (f32[1,16]{1,0:T(1,128)S(1)}, f32[1,16]{1,0:T(1,128)}, u32[]{:S(2)}) copy-start(f32[1,16]{1,0:T(1,128)} %param.12) | copy-start | bytes 196
  0.7 9.1 %copy-start.12 = (f32[1,15]{1,0:T(1,128)S(1)}, f32[1,15]{1,0:T(1,128)}, u32[]{:S(2)}) copy-start(f32[1,15]{1,0:T(1,128)} %param.13) | copy-start | bytes 184
  2.8 13.7 %copy-start = (f32[1,16,32,512]{3,2,1,0:T(8,128)S(1)}, f32[1,16,32,512]{3,2,1,0:T(8,128)}, u32[]{:S(2)}) copy-start(f32[1,16,32,512]{3,2,1,0:T(8,128)} %param.10) | copy-start | bytes 3145732
  2.8 13.6 %collective-permute-start = (f32[16,8,512]{2,1,0:T(8,128)}, f32[16,8,512]{2,1,0:T(8,128)S(1)}, u32[]{:S(2)}, u32[]{:S(2)}) collective-permute-start(f32[16,8,512]{2,1,0:T(8,128)} %get-tuple-element.58), channel_id=1, source_target_pairs={{0,4},{4,8},{8,12},{12,16},{16,20},{20,24},{24,28},{28,32},{32,36}... | collective-permute-start | bytes 786440 | tf_op jit(solution)/shard_map/ppermute | solution.py:771
  4.9 11.5 %collective-permute-start.1 = (f32[16,8,512]{2,1,0:T(8,128)}, f32[16,8,512]{2,1,0:T(8,128)S(1)}, u32[]{:S(2)}, u32[]{:S(2)}) collective-permute-start(f32[16,8,512]{2,1,0:T(8,128)} %get-tuple-element.52.after), channel_id=1, source_target_pairs={{0,60},{4,0},{8,4},{12,8},{16,12},{20,16},{24,20},{28,24},{32,28},... | collective-permute-start | bytes 786440 | tf_op jit(solution)/shard_map/ppermute | solution.py:771
  10.8 5.7 %copy-start.2 = (bf16[1,6,32,512]{3,2,1,0:T(8,128)(2,1)S(1)}, bf16[1,6,32,512]{3,2,1,0:T(8,128)(2,1)}, u32[]{:S(2)}) copy-start(bf16[1,6,32,512]{3,2,1,0:T(8,128)(2,1)} %param.11) | copy-start | bytes 589828
  10.8 5.7 %copy-start.4 = (f32[1,32,512]{2,1,0:T(8,128)S(1)}, f32[1,32,512]{2,1,0:T(8,128)}, u32[]{:S(2)}) copy-start(f32[1,32,512]{2,1,0:T(8,128)} %param.14) | copy-start | bytes 196612
  10.8 5.7 %copy-start.5 = (f32[32,512]{1,0:T(8,128)S(1)}, f32[32,512]{1,0:T(8,128)}, u32[]{:S(2)}) copy-start(f32[32,512]{1,0:T(8,128)} %land.3) | copy-start | bytes 196612
  13.5 5.4 %collective-permute-start.4 = (f32[32,512]{1,0:T(8,128)S(1)}, f32[32,512]{1,0:T(8,128)S(1)}, u32[]{:S(2)}, u32[]{:S(2)}) collective-permute-start(f32[32,512]{1,0:T(8,128)S(1)} %get-tuple-element.63.factor), channel_id=1, source_target_pairs={{0,64},{64,0},{1,65},{65,1},{2,66},{66,2},{3,67},{67,3},{4,68},{68... | collective-permute-start | bytes 196616 | tf_op jit(solution)/shard_map/ppermute | solution.py:775
  16.9 2.2 %collective-permute-start.2 = (f32[48,256]{1,0:T(8,128)S(1)}, f32[48,256]{1,0:T(8,128)S(1)}, u32[]{:S(2)}, u32[]{:S(2)}) collective-permute-start(f32[48,256]{1,0:T(8,128)S(1)} %get-tuple-element.61), channel_id=1, source_target_pairs={{0,1},{1,0},{2,3},{3,2},{4,5},{5,4},{6,7},{7,6},{8,9},{9,8},{10,11... | collective-permute-start | bytes 147464 | tf_op jit(solution)/shard_map/ppermute | solution.py:775
  18.2 3.5 %collective-permute-start.3 = (f32[48,256]{1,0:T(8,128)S(1)}, f32[48,256]{1,0:T(8,128)S(1)}, u32[]{:S(2)}, u32[]{:S(2)}) collective-permute-start(f32[48,256]{1,0:T(8,128)S(1)} %get-tuple-element.62), channel_id=1, source_target_pairs={{0,3},{1,2},{2,1},{3,0},{4,7},{5,6},{6,5},{7,4},{8,11},{9,10},{10,... | collective-permute-start | bytes 147464 | tf_op jit(solution)/shard_map/ppermute | solution.py:775
  25.7 9.1 %collective-permute-start.5 = (bf16[6,32,512]{2,1,0:T(8,128)(2,1)S(1)}, bf16[6,32,512]{2,1,0:T(8,128)(2,1)S(1)}, u32[]{:S(2)}, u32[]{:S(2)}) collective-permute-start(bf16[6,32,512]{2,1,0:T(8,128)(2,1)S(1)} %get-tuple-element.65), channel_id=1, source_target_pairs={{0,64},{64,0},{1,65},{65,1},{2,66},{66,2},{3,67},{67,3},{4,68},{68... | collective-permute-start | bytes 589832 | tf_op jit(solution)/shard_map/ppermute | solution.py:775
  35.6 21.4 %all-to-all-start = ((f32[64,2,128]{2,1,0:T(2,128)}), f32[64,2,128]{2,1,0:T(2,128)S(1)}, u32[]{:S(2)}, u32[]{:S(2)}) async-start(f32[64,2,128]{2,1,0:T(2,128)} %get-tuple-element.75), calls=%async_computation | async-start | bytes 131072 | tf_op jit(solution)/shard_map/all_to_all | solution.py:886
  45.4 6.4 %collective-permute-start.6 = (f32[2,8,512]{2,1,0:T(8,128)S(1)}, f32[2,8,512]{2,1,0:T(8,128)S(1)}, u32[]{:S(2)}, u32[]{:S(2)}) collective-permute-start(f32[2,8,512]{2,1,0:T(8,128)S(1)} %get-tuple-element.71), channel_id=1, source_target_pairs={{0,4},{4,8},{8,12},{12,16},{16,20},{20,24},{24,28},{28,32},{32,36}... | collective-permute-start | bytes 98312 | tf_op jit(solution)/shard_map/ppermute | solution.py:771
  46.9 4.9 %collective-permute-start.7 = (f32[2,8,512]{2,1,0:T(8,128)S(1)}, f32[2,8,512]{2,1,0:T(8,128)S(1)}, u32[]{:S(2)}, u32[]{:S(2)}) collective-permute-start(f32[2,8,512]{2,1,0:T(8,128)S(1)} %get-tuple-element.72), channel_id=1, source_target_pairs={{0,60},{4,0},{8,4},{12,8},{16,12},{20,16},{24,20},{28,24},{32,28},... | collective-permute-start | bytes 98312 | tf_op jit(solution)/shard_map/ppermute | solution.py:771
  52.0 2.7 %collective-permute-start.8 = (f32[48,128]{1,0:T(8,128)S(1)}, f32[48,128]{1,0:T(8,128)S(1)}, u32[]{:S(2)}, u32[]{:S(2)}) collective-permute-start(f32[48,128]{1,0:T(8,128)S(1)} %get-tuple-element.73), channel_id=1, source_target_pairs={{0,1},{1,0},{2,3},{3,2},{4,5},{5,4},{6,7},{7,6},{8,9},{9,8},{10,11... | collective-permute-start | bytes 73736 | tf_op jit(solution)/shard_map/ppermute | solution.py:775
  53.7 3.3 %collective-permute-start.9 = (f32[48,128]{1,0:T(8,128)S(1)}, f32[48,128]{1,0:T(8,128)S(1)}, u32[]{:S(2)}, u32[]{:S(2)}) collective-permute-start(f32[48,128]{1,0:T(8,128)S(1)} %get-tuple-element.74), channel_id=1, source_target_pairs={{0,3},{1,2},{2,1},{3,0},{4,7},{5,6},{6,5},{7,4},{8,11},{9,10},{10,... | collective-permute-start | bytes 73736 | tf_op jit(solution)/shard_map/ppermute | solution.py:775
  56.9 5.3 %copy-start.8 = (f32[2,48,640]{2,1,0:T(8,128)S(1)}, f32[2,48,640]{2,1,0:T(8,128)}, u32[]{:S(2)}) copy-start(f32[2,48,640]{2,1,0:T(8,128)} %copy-done.7) | copy-start | bytes 737284
  59.7 12.5 %collective-permute-start.10 = (bf16[6,32,512]{2,1,0:T(8,128)(2,1)}, bf16[6,32,512]{2,1,0:T(8,128)(2,1)S(1)}, u32[]{:S(2)}, u32[]{:S(2)}) collective-permute-start(bf16[6,32,512]{2,1,0:T(8,128)(2,1)} %get-tuple-element.84.series), channel_id=1, source_target_pairs={{0,64},{64,0},{1,65},{65,1},{2,66},{66,2},{3,67},{67,3},{4,68},{68... | collective-permute-start | bytes 589832 | tf_op jit(solution)/shard_map/ppermute | solution.py:775
  64.9 16.8 %all-to-all-start.1 = ((f32[128,1,128]{2,1,0:T(1,128)}), f32[128,1,128]{2,1,0:T(1,128)S(1)}, u32[]{:S(2)}, u32[]{:S(2)}) async-start(f32[128,1,128]{2,1,0:T(1,128)} %get-tuple-element.89), calls=%async_computation.1 | async-start | bytes 131072 | tf_op jit(solution)/shard_map/all_to_all | solution.py:930
  (2 other events, 1.6 us)

commit v8 on v7

--- a/solution.py
+++ b/solution.py
@@ -436,8 +436,7 @@
                     v = h
                 if l == t and t >= 3:
                     strip.save(us, t - 3, v)
-                    if t > 3:
-                        strip.save(hs, t - 4, h)
+                    strip.save(hs, t - 3, h)
                 v = less(v, u_prev)
                 if t < SUB - 1:
                     strip.store(dst, l, v)
@@ -521,7 +520,7 @@
     total = jnp.sum(total, axis=1, keepdims=True)
     total = jnp.sum(jnp.where(row == lane, total, 0.0), axis=0, keepdims=True) + wet[...]
     for k in range(rows.shape[0]):
-        rows[k] = jnp.broadcast_to(total, rows.shape[1:])
+        rows[k] = total
 
 
 def losses(
@@ -618,7 +617,7 @@
 
 
 def gap_means(gap, start, count):
-    total = jnp.sum(gap[pl.ds(start, count), 0:1], axis=0)
+    total = jnp.sum(gap[pl.ds(start, count)], axis=0)
     lane = lax.broadcasted_iota(jnp.int32, (1, LANES), 1)
     wet = jnp.sum(jnp.where(lane == SUB, total, 0.0), axis=1, keepdims=True)
     return [
@@ -741,7 +740,7 @@
                     if l + 1 < t:
                         h_next = strip.spread(src, l + 1, diff[l + 1])
                     else:
-                        h_next = strip.recall(hs, t - 4)
+                        h_next = strip.recall(hs, t - 3)
                     u = flux_between(mix[l], h_next, h)
                     v = added(h, u)
                     h = h_next
@@ -865,10 +864,10 @@
 
     whole, hs_rest, us_rest, token = call(
         first_rest,
-        [shape(LEVELS, CX, CY), band(2), band(3), shape(8, LANES)],
+        [shape(LEVELS, CX, CY), band(3), band(3), shape(8, LANES)],
         [
             field_buf(LEVELS), field_buf(LEVELS),
-            band_buf(2), band_buf(3), pltpu.SemaphoreType.DMA((2,)),
+            band_buf(3), band_buf(3), pltpu.SemaphoreType.DMA((2,)),
         ],
         [VM] * 8,
         out_specs=[VM, HBM, HBM, VM],
@@ -878,8 +877,8 @@
     peers = lax.axis_size(("gx", "gy"))
     gap, after = call(
         losses,
-        [shape(peers, 2, LANES), shape(8, LANES)],
-        [pltpu.VMEM((peers, 2, LANES), F32), pltpu.SemaphoreType.DMA(())],
+        [shape(peers, 1, LANES), shape(8, LANES)],
+        [pltpu.VMEM((peers, 1, LANES), F32), pltpu.SemaphoreType.DMA(())],
         [VM, VM, VM, VM],
         out_specs=[HBM, VM],
     )(received, factor, wet, token)
@@ -917,7 +916,7 @@
         second_rest,
         [shape(LEVELS, CX, CY), shape(8, LANES), everyone],
         [
-            field_buf(SUB), field_buf(SUB), band_buf(2), band_buf(3),
+            field_buf(SUB), field_buf(SUB), band_buf(3), band_buf(3),
             pltpu.VMEM(everyone.shape, F32), pltpu.SemaphoreType.DMA((3,)),
         ],
         [VM, VM, VM, HBM, HBM, VM, VM, VM, VM, pl.BlockSpec(memory_space=pl.ANY)],

time: 82.9 us -> 80.3 us (0.969)
  starting transfers between devices: 39.5 us -> 35.2 us
  waiting for transfers between devices: 12.7 us -> 13.9 us
  Pallas kernels: 27.8 us -> 28.9 us
    all_to_all x1, waiting for transfers between devices: 0.01 us -> 4.5 us  [per_device(): gap = lax.all_to_all(gap, ('gx', 'gy'), 0, 0)]
    ppermute x7, waiting for transfers between devices: 5 us -> 2.84 us  [paired(): lax.ppermute(value, axis, [(i, i ^ mask) for i in range(lax.axis_size(axi...]
    all_to_all x1, starting transfers between devices: 7.44 us -> 5.65 us  [per_device(): gap = lax.all_to_all(gap, ('gx', 'gy'), 0, 0)]
    all_to_all x1, starting transfers between devices: 7.31 us -> 5.7 us  [per_device(): gap = lax.all_to_all(gap, ('comp', 'gx', 'gy'), 0, 0)]
    pallas_call x1, Pallas kernels: 0.22 us -> 1.55 us  [per_device(): call(pack_second, [packed, packed], [pltpu.VMEM((SUB - 1, 16, CY), F32),...]
    ppermute x4, waiting for transfers between devices: 1.23 us -> 0.01 us  [shifted(): return lax.ppermute(value, axis, [(i, (i + by) % n) for i in range(n)])]
    ppermute x7, starting transfers between devices: 12.7 us -> 11.8 us  [paired(): lax.ppermute(value, axis, [(i, i ^ mask) for i in range(lax.axis_size(axi...]
    unnamed x26 -> x24, local copies, waits for them, and re-layouts: 1.68 us -> 0.99 us
  transfers between devices with their start and end apart: 13 -> 13, of which waited for: 5 -> 4; matrix products, arithmetic and copies ran while one was open for 0% -> 0% of each run, Pallas kernels for 21% -> 20%
where the time goes in v8:
time: 80.3 us; the launch traced here: 79.9 us
  starting transfers between devices  35.2 us (44%)
  Pallas kernels  28.9 us (36%)
  waiting for transfers between devices  13.9 us (17%)
  local copies, waits for them, and re-layouts  0.99 us (1%)
  between operations  0.91 us (1%)
    ppermute x4, starting transfers between devices, shifted(): return lax.ppermute(value, axis, [(i, (i + by) % n) for i in range(n)])  12.1 us
    ppermute x7, starting transfers between devices, paired(): lax.ppermute(value, axis, [(i, i ^ mask) for i in range(lax.axis_size(axi...  11.8 us
    all_to_all x1, waiting for transfers between devices, per_device(): gap = lax.all_to_all(gap, ('comp', 'gx', 'gy'), 0, 0)  6.57 us
    pallas_call x2, Pallas kernels, regridded(): call(regrid, [shape(SUB, CX, CY), edges, edges], [pltpu.VMEM((BLOCKS * 8,...  5.96 us
    pallas_call x1, Pallas kernels, per_device(): call(first_rest, [shape(LEVELS, CX, CY), band(3), band(3), shape(8, LANES...  5.82 us
    all_to_all x1, starting transfers between devices, per_device(): gap = lax.all_to_all(gap, ('comp', 'gx', 'gy'), 0, 0)  5.7 us
    all_to_all x1, starting transfers between devices, per_device(): gap = lax.all_to_all(gap, ('gx', 'gy'), 0, 0)  5.65 us
    all_to_all x1, waiting for transfers between devices, per_device(): gap = lax.all_to_all(gap, ('gx', 'gy'), 0, 0)  4.5 us
  transfers between devices with their start and end apart: 13, of which 4 were waited for; matrix products, arithmetic and copies ran while one was open for 0% of the time, Pallas kernels for 20%

profile of v8, /device:TPU:1, one launch (start us, length us, event | category | flops | bytes accessed | tf_op | source)
XLA Modules:
  0.0 79.9 jit_solution(10575918608119071961)
XLA Ops:
  0.7 2.1 %shard_map.113 = (f32[16,8,512]{2,1,0:T(8,128)}, f32[16,8,512]{2,1,0:T(8,128)}) custom-call(f32[16,32,512]{2,1,0:T(8,128)} %bitcast.14, bf16[6,32,512]{2,1,0:T(8,128)(2,1)} %bitcast.21, f32[32,512]{1,0:T(8,128)} %bitcast.24, f32[32,512]{1,0:T(8,128)} %land.3, s32[32,512]{1,0:T(8,128)} %mask.6), custom_call_target="tpu_custom_call" | custom-call | tf_op jit(solution)/shard_map/pallas_call | solution.py:790
  2.8 2.1 %collective-permute-start = (f32[16,8,512]{2,1,0:T(8,128)}, f32[16,8,512]{2,1,0:T(8,128)S(1)}, u32[]{:S(2)}, u32[]{:S(2)}) collective-permute-start(f32[16,8,512]{2,1,0:T(8,128)} %get-tuple-element.58), channel_id=1, source_target_pairs={{0,4},{4,8},{8,12},{12,16},{16,20},{20,24},{24,28},{28,32},{32,36}... | collective-permute-start | bytes 786440 | tf_op jit(solution)/shard_map/ppermute | solution.py:770
  4.9 4.8 %collective-permute-start.1 = (f32[16,8,512]{2,1,0:T(8,128)}, f32[16,8,512]{2,1,0:T(8,128)S(1)}, u32[]{:S(2)}, u32[]{:S(2)}) collective-permute-start(f32[16,8,512]{2,1,0:T(8,128)} %get-tuple-element.52.after), channel_id=1, source_target_pairs={{0,60},{4,0},{8,4},{12,8},{16,12},{20,16},{24,20},{28,24},{32,28},... | collective-permute-start | bytes 786440 | tf_op jit(solution)/shard_map/ppermute | solution.py:770
  9.8 0.9 %copy-done.6 = f32[16,8,512]{2,1,0:T(8,128)S(1)} copy-done((f32[16,8,512]{2,1,0:T(8,128)S(1)}, f32[16,8,512]{2,1,0:T(8,128)}, u32[]{:S(2)}) %copy-start.6) | copy-done | bytes 262168
  10.8 2.7 %shard_map.114 = (f32[32,512]{1,0:T(8,128)S(1)}, f32[1,128]{1,0:T(1,128)S(1)}, f32[32,8,128]{2,1,0:T(8,128)S(1)}) custom-call(f32[16]{0:T(128)S(1)} %bitcast.33, f32[15]{0:T(128)S(1)} %bitcast.34, s32[4,2,32]{2,1,0:T(2,128)S(1)} %bitcast.27, s32[4,2,32]{2,1,0:T(2,128)S(1)} %bitcast.30, bf16[32,128,128]{2,1,0:T(8,128)(2,1)S(1)} %bitcast.18, ...), custom_call_target="tpu_custom_call" | custom-call | tf_op jit(solution)/shard_map/pallas_call | solution.py:812
  13.5 3.0 %collective-permute-start.4 = (f32[32,512]{1,0:T(8,128)S(1)}, f32[32,512]{1,0:T(8,128)S(1)}, u32[]{:S(2)}, u32[]{:S(2)}) collective-permute-start(f32[32,512]{1,0:T(8,128)S(1)} %get-tuple-element.63.factor), channel_id=1, source_target_pairs={{0,64},{64,0},{1,65},{65,1},{2,66},{66,2},{3,67},{67,3},{4,68},{68... | collective-permute-start | bytes 196616 | tf_op jit(solution)/shard_map/ppermute | solution.py:774
  16.9 1.3 %collective-permute-start.2 = (f32[48,256]{1,0:T(8,128)S(1)}, f32[48,256]{1,0:T(8,128)S(1)}, u32[]{:S(2)}, u32[]{:S(2)}) collective-permute-start(f32[48,256]{1,0:T(8,128)S(1)} %get-tuple-element.61), channel_id=1, source_target_pairs={{0,1},{1,0},{2,3},{3,2},{4,5},{5,4},{6,7},{7,6},{8,9},{9,8},{10,11... | collective-permute-start | bytes 147464 | tf_op jit(solution)/shard_map/ppermute | solution.py:774
  19.1 2.6 %collective-permute-done.3.three = f32[48,256]{1,0:T(8,128)S(1)} collective-permute-done((f32[48,256]{1,0:T(8,128)S(1)}, f32[48,256]{1,0:T(8,128)S(1)}, u32[]{:S(2)}, u32[]{:S(2)}) %collective-permute-start.3) | collective-permute-done | bytes 49184 | tf_op jit(solution)/shard_map/ppermute | solution.py:774
  21.7 4.0 %shard_map.116 = (bf16[6,32,512]{2,1,0:T(8,128)(2,1)S(1)}, f32[6,48,640]{2,1,0:T(8,128)S(1)}, f32[6,48,640]{2,1,0:T(8,128)S(1)}, f32[3,48,640]{2,1,0:T(8,128)S(1...) custom-call(f32[32,8,128]{2,1,0:T(8,128)S(1)} %get-tuple-element.53.coeff, f32[16,32,512]{2,1,0:T(8,128)S(1)} %bitcast.16, ...), custom_call_target="tpu_custom_call" | custom-call | tf_op jit(solution)/shard_map/pallas_call | solution.py:832
  25.7 2.4 %collective-permute-start.5 = (bf16[6,32,512]{2,1,0:T(8,128)(2,1)S(1)}, bf16[6,32,512]{2,1,0:T(8,128)(2,1)S(1)}, u32[]{:S(2)}, u32[]{:S(2)}) collective-permute-start(bf16[6,32,512]{2,1,0:T(8,128)(2,1)S(1)} %get-tuple-element.65), channel_id=1, source_target_pairs={{0,64},{64,0},{1,65},{65,1},{2,66},{66,2},{3,67},{67,3},{4,68},{68... | collective-permute-start | bytes 589832 | tf_op jit(solution)/shard_map/ppermute | solution.py:774
  28.2 5.8 %shard_map.117 = (f32[16,32,512]{2,1,0:T(8,128)}, f32[3,48,640]{2,1,0:T(8,128)S(1)}, f32[3,48,640]{2,1,0:T(8,128)S(1)}, f32[8,128]{1,0:T(8,128)S(1)}) custom-call(f32[32,8,128]{2,1,0:T(8,128)S(1)} %get-tuple-element.53.coeff, f32[16,32,512]{2,1,0:T(8,128)S(1)} %bitcast.17, f32[16,8,512]{2,1,0:T(8,128)S(1)} %collective-permute-done.upper, ...), custom_call_target="tpu_custom_call" | custom-call | tf_op jit(solution)/shard_map/pallas_call | solution.py:865
  34.2 3.0 %shard_map.119 = (f32[6,32,512]{2,1,0:T(8,128)S(1)}, f32[2,8,512]{2,1,0:T(8,128)}, f32[2,8,512]{2,1,0:T(8,128)}) custom-call(s32[4,2,32]{2,1,0:T(2,128)S(1)} %bitcast.28, s32[4,2,32]{2,1,0:T(2,128)S(1)} %bitcast.31, bf16[6,32,512]{2,1,0:T(8,128)(2,1)S(1)} %collective-permute-done.5.received, bf16[32,128,128]{2,1,0:T(8,128)(2,1)S(1)} %bitcast.19, ...), custom_call_target="tpu_custom_call" | custom-call | flops 67108864 | bytes 8388608 | tf_op jit(solution)/shard_map/pallas_call | solution.py:848
  37.3 5.1 %collective-permute-start.7 = (f32[2,8,512]{2,1,0:T(8,128)}, f32[2,8,512]{2,1,0:T(8,128)}, u32[]{:S(2)}, u32[]{:S(2)}) collective-permute-start(f32[2,8,512]{2,1,0:T(8,128)} %get-tuple-element.72), channel_id=1, source_target_pairs={{0,60},{4,0},{8,4},{12,8},{16,12},{20,16},{24,20},{28,24},{32,28},... | collective-permute-start | bytes 98312 | tf_op jit(solution)/shard_map/ppermute | solution.py:770
  42.4 5.6 %all-to-all-start = ((f32[64,1,128]{2,1,0:T(1,128)}), f32[64,1,128]{2,1,0:T(1,128)}, u32[]{:S(2)}, u32[]{:S(2)}) async-start(f32[64,1,128]{2,1,0:T(1,128)} %copy-done.9), calls=%async_computation | async-start | bytes 65536 | tf_op jit(solution)/shard_map/all_to_all | solution.py:885
  48.1 1.5 %shard_map.120 = (f32[48,128]{1,0:T(8,128)}, f32[48,128]{1,0:T(8,128)}) custom-call(f32[6,32,512]{2,1,0:T(8,128)S(1)} %get-tuple-element.70.out.regridded, f32[2,8,512]{2,1,0:T(8,128)} %collective-permute-done.6.upper_in, f32[2,8,512]{2,1,0:T(8,128)} %collective-permute-done.7.lower_in), custom_call_target="tpu_custom_call" | custom-call | tf_op jit(solution)/shard_map/pallas_call | solution.py:889
  50.3 1.2 %collective-permute-start.9 = (f32[48,128]{1,0:T(8,128)}, f32[48,128]{1,0:T(8,128)}, u32[]{:S(2)}, u32[]{:S(2)}) collective-permute-start(f32[48,128]{1,0:T(8,128)} %get-tuple-element.74), channel_id=1, source_target_pairs={{0,3},{1,2},{2,1},{3,0},{4,7},{5,6},{6,5},{7,4},{8,11},{9,10},{10,... | collective-permute-start | bytes 73736 | tf_op jit(solution)/shard_map/ppermute | solution.py:774
  51.5 4.5 %all-to-all-done.gap_in = f32[64,1,128]{2,1,0:T(1,128)} async-done(((f32[64,1,128]{2,1,0:T(1,128)}), f32[64,1,128]{2,1,0:T(1,128)}, u32[]{:S(2)}, u32[]{:S(2)}) %all-to-all-start) | async-done | bytes 32800 | tf_op jit(solution)/shard_map/all_to_all | solution.py:885
  56.0 2.7 %shard_map.121 = (bf16[6,32,512]{2,1,0:T(8,128)(2,1)}, f32[32,512]{1,0:T(8,128)S(1)}, f32[3,48,640]{2,1,0:T(8,128)S(1)}, f32[3,48,640]{2,1,0:T(8,128)S(1)}, f32[32,8,128]{2,1,0:T(8,128)S(1)}) custom-call(f32[4,48,640]{2,1,0:T(8,128)S(1)} %get-tuple-element.64.fixed_in, f32[6,32,512]{2,1,0:T(8,128)S(1)} %get-tuple-element.70.out.regridded, ...), custom_call_target="tpu_custom_call" | custom-call | tf_op jit(solution)/shard_map/pallas_call | solution.py:902
  58.7 2.5 %collective-permute-start.10 = (bf16[6,32,512]{2,1,0:T(8,128)(2,1)}, bf16[6,32,512]{2,1,0:T(8,128)(2,1)S(1)}, u32[]{:S(2)}, u32[]{:S(2)}) collective-permute-start(bf16[6,32,512]{2,1,0:T(8,128)(2,1)} %get-tuple-element.84.series), channel_id=1, source_target_pairs={{0,64},{64,0},{1,65},{65,1},{2,66},{66,2},{3,67},{67,3},{4,68},{68... | collective-permute-start | bytes 589832 | tf_op jit(solution)/shard_map/ppermute | solution.py:774
  61.2 2.5 %shard_map.122 = (f32[16,32,512]{2,1,0:T(8,128)}, f32[8,128]{1,0:T(8,128)S(1)}, f32[128,1,128]{2,1,0:T(1,128)}) custom-call(f32[32,8,128]{2,1,0:T(8,128)S(1)} %get-tuple-element.78.coeff, f32[3,48,640]{2,1,0:T(8,128)S(1)} %get-tuple-element.79.hx, f32[3,48,640]{2,1,0:T(8,128)S(1)} %get-tuple-element.80.ux, ...), custom_call_target="tpu_custom_call", output_to_operand_aliasing={{0}: (9, {})} | custom-call | tf_op jit(solution)/shard_map/pallas_call | solution.py:915
  63.7 5.7 %all-to-all-start.1 = ((f32[128,1,128]{2,1,0:T(1,128)}), f32[128,1,128]{2,1,0:T(1,128)S(1)}, u32[]{:S(2)}, u32[]{:S(2)}) async-start(f32[128,1,128]{2,1,0:T(1,128)} %get-tuple-element.89), calls=%async_computation.1 | async-start | bytes 131072 | tf_op jit(solution)/shard_map/all_to_all | solution.py:929
  69.4 3.0 %shard_map.123 = (f32[6,32,512]{2,1,0:T(8,128)S(1)}, f32[2,8,512]{2,1,0:T(8,128)}, f32[2,8,512]{2,1,0:T(8,128)}) custom-call(s32[4,2,32]{2,1,0:T(2,128)S(1)} %bitcast.29, s32[4,2,32]{2,1,0:T(2,128)S(1)} %bitcast.32, bf16[6,32,512]{2,1,0:T(8,128)(2,1)S(1)} %collective-permute-done.10.received, bf16[32,128,128]{2,1,0:T(8,128)(2,1)S(1)} %bitcast.20, ...), custom_call_target="tpu_custom_call" | custom-call | flops 67108864 | bytes 8388608 | tf_op jit(solution)/shard_map/pallas_call | solution.py:848
  72.4 6.6 %all-to-all-done.1.gap = f32[128,1,128]{2,1,0:T(1,128)S(1)} async-done(((f32[128,1,128]{2,1,0:T(1,128)}), f32[128,1,128]{2,1,0:T(1,128)S(1)}, u32[]{:S(2)}, u32[]{:S(2)}) %all-to-all-start.1) | async-done | bytes 65568 | tf_op jit(solution)/shard_map/all_to_all | solution.py:929
  79.0 0.9 %shard_map.124 = f32[6,32,512]{2,1,0:T(8,128)} custom-call(f32[6,32,512]{2,1,0:T(8,128)S(1)} %get-tuple-element.88.regridded, s32[32,512]{1,0:T(8,128)S(1)} %copy-done.3, f32[128,1,128]{2,1,0:T(1,128)S(1)} %all-to-all-done.1.gap), custom_call_target="tpu_custom_call" | custom-call | tf_op jit(solution)/shard_map/pallas_call | solution.py:931
  (38 shorter events, 2.3 us)
Async XLA Ops:
  0.6 9.1 %copy-start.1 = (bf16[1,32,128,128]{3,2,1,0:T(8,128)(2,1)S(1)}, bf16[1,32,128,128]{3,2,1,0:T(8,128)(2,1)}, u32[]{:S(2)}) copy-start(bf16[1,32,128,128]{3,2,1,0:T(8,128)(2,1)} %param.17) | copy-start | bytes 3145732
  0.6 9.1 %copy-start.3 = (s32[32,512]{1,0:T(8,128)S(1)}, s32[32,512]{1,0:T(8,128)}, u32[]{:S(2)}) copy-start(s32[32,512]{1,0:T(8,128)} %mask.6) | copy-start | bytes 196612
  0.7 9.1 %copy-start.7 = (s32[1,32,4,2]{1,3,2,0:T(2,128)S(1)}, s32[1,32,4,2]{1,3,2,0:T(2,128)}, u32[]{:S(2)}) copy-start(s32[1,32,4,2]{1,3,2,0:T(2,128)} %param.18) | copy-start | bytes 3076
  0.7 9.1 %copy-start.8 = (s32[1,32,4,2]{1,3,2,0:T(2,128)S(1)}, s32[1,32,4,2]{1,3,2,0:T(2,128)}, u32[]{:S(2)}) copy-start(s32[1,32,4,2]{1,3,2,0:T(2,128)} %param.19) | copy-start | bytes 3076
  0.7 9.1 %copy-start.10 = (f32[1,16]{1,0:T(1,128)S(1)}, f32[1,16]{1,0:T(1,128)}, u32[]{:S(2)}) copy-start(f32[1,16]{1,0:T(1,128)} %param.12) | copy-start | bytes 196
  0.7 9.1 %copy-start.11 = (f32[1,15]{1,0:T(1,128)S(1)}, f32[1,15]{1,0:T(1,128)}, u32[]{:S(2)}) copy-start(f32[1,15]{1,0:T(1,128)} %param.13) | copy-start | bytes 184
  2.8 13.7 %copy-start = (f32[1,16,32,512]{3,2,1,0:T(8,128)S(1)}, f32[1,16,32,512]{3,2,1,0:T(8,128)}, u32[]{:S(2)}) copy-start(f32[1,16,32,512]{3,2,1,0:T(8,128)} %param.10) | copy-start | bytes 3145732
  2.8 13.6 %collective-permute-start = (f32[16,8,512]{2,1,0:T(8,128)}, f32[16,8,512]{2,1,0:T(8,128)S(1)}, u32[]{:S(2)}, u32[]{:S(2)}) collective-permute-start(f32[16,8,512]{2,1,0:T(8,128)} %get-tuple-element.58), channel_id=1, source_target_pairs={{0,4},{4,8},{8,12},{12,16},{16,20},{20,24},{24,28},{28,32},{32,36}... | collective-permute-start | bytes 786440 | tf_op jit(solution)/shard_map/ppermute | solution.py:770
  4.9 11.5 %collective-permute-start.1 = (f32[16,8,512]{2,1,0:T(8,128)}, f32[16,8,512]{2,1,0:T(8,128)S(1)}, u32[]{:S(2)}, u32[]{:S(2)}) collective-permute-start(f32[16,8,512]{2,1,0:T(8,128)} %get-tuple-element.52.after), channel_id=1, source_target_pairs={{0,60},{4,0},{8,4},{12,8},{16,12},{20,16},{24,20},{28,24},{32,28},... | collective-permute-start | bytes 786440 | tf_op jit(solution)/shard_map/ppermute | solution.py:770
  10.8 5.7 %copy-start.2 = (bf16[1,6,32,512]{3,2,1,0:T(8,128)(2,1)S(1)}, bf16[1,6,32,512]{3,2,1,0:T(8,128)(2,1)}, u32[]{:S(2)}) copy-start(bf16[1,6,32,512]{3,2,1,0:T(8,128)(2,1)} %param.11) | copy-start | bytes 589828
  10.8 5.7 %copy-start.4 = (f32[1,32,512]{2,1,0:T(8,128)S(1)}, f32[1,32,512]{2,1,0:T(8,128)}, u32[]{:S(2)}) copy-start(f32[1,32,512]{2,1,0:T(8,128)} %param.14) | copy-start | bytes 196612
  10.8 5.7 %copy-start.5 = (f32[32,512]{1,0:T(8,128)S(1)}, f32[32,512]{1,0:T(8,128)}, u32[]{:S(2)}) copy-start(f32[32,512]{1,0:T(8,128)} %land.3) | copy-start | bytes 196612
  13.5 5.4 %collective-permute-start.4 = (f32[32,512]{1,0:T(8,128)S(1)}, f32[32,512]{1,0:T(8,128)S(1)}, u32[]{:S(2)}, u32[]{:S(2)}) collective-permute-start(f32[32,512]{1,0:T(8,128)S(1)} %get-tuple-element.63.factor), channel_id=1, source_target_pairs={{0,64},{64,0},{1,65},{65,1},{2,66},{66,2},{3,67},{67,3},{4,68},{68... | collective-permute-start | bytes 196616 | tf_op jit(solution)/shard_map/ppermute | solution.py:774
  16.9 2.2 %collective-permute-start.2 = (f32[48,256]{1,0:T(8,128)S(1)}, f32[48,256]{1,0:T(8,128)S(1)}, u32[]{:S(2)}, u32[]{:S(2)}) collective-permute-start(f32[48,256]{1,0:T(8,128)S(1)} %get-tuple-element.61), channel_id=1, source_target_pairs={{0,1},{1,0},{2,3},{3,2},{4,5},{5,4},{6,7},{7,6},{8,9},{9,8},{10,11... | collective-permute-start | bytes 147464 | tf_op jit(solution)/shard_map/ppermute | solution.py:774
  18.2 3.5 %collective-permute-start.3 = (f32[48,256]{1,0:T(8,128)S(1)}, f32[48,256]{1,0:T(8,128)S(1)}, u32[]{:S(2)}, u32[]{:S(2)}) collective-permute-start(f32[48,256]{1,0:T(8,128)S(1)} %get-tuple-element.62), channel_id=1, source_target_pairs={{0,3},{1,2},{2,1},{3,0},{4,7},{5,6},{6,5},{7,4},{8,11},{9,10},{10,... | collective-permute-start | bytes 147464 | tf_op jit(solution)/shard_map/ppermute | solution.py:774
  25.7 8.3 %collective-permute-start.5 = (bf16[6,32,512]{2,1,0:T(8,128)(2,1)S(1)}, bf16[6,32,512]{2,1,0:T(8,128)(2,1)S(1)}, u32[]{:S(2)}, u32[]{:S(2)}) collective-permute-start(bf16[6,32,512]{2,1,0:T(8,128)(2,1)S(1)} %get-tuple-element.65), channel_id=1, source_target_pairs={{0,64},{64,0},{1,65},{65,1},{2,66},{66,2},{3,67},{67,3},{4,68},{68... | collective-permute-start | bytes 589832 | tf_op jit(solution)/shard_map/ppermute | solution.py:774
  34.2 3.0 %copy-start.9 = (f32[64,1,128]{2,1,0:T(1,128)}, f32[64,1,128]{2,1,0:T(1,128)S(1)}, u32[]{:S(2)}) copy-start(f32[64,1,128]{2,1,0:T(1,128)S(1)} %get-tuple-element.75) | copy-start | bytes 98308
  37.2 10.8 %collective-permute-start.6 = (f32[2,8,512]{2,1,0:T(8,128)}, f32[2,8,512]{2,1,0:T(8,128)}, u32[]{:S(2)}, u32[]{:S(2)}) collective-permute-start(f32[2,8,512]{2,1,0:T(8,128)} %get-tuple-element.71), channel_id=1, source_target_pairs={{0,4},{4,8},{8,12},{12,16},{16,20},{20,24},{24,28},{28,32},{32,36}... | collective-permute-start | bytes 98312 | tf_op jit(solution)/shard_map/ppermute | solution.py:770
  37.3 10.8 %collective-permute-start.7 = (f32[2,8,512]{2,1,0:T(8,128)}, f32[2,8,512]{2,1,0:T(8,128)}, u32[]{:S(2)}, u32[]{:S(2)}) collective-permute-start(f32[2,8,512]{2,1,0:T(8,128)} %get-tuple-element.72), channel_id=1, source_target_pairs={{0,60},{4,0},{8,4},{12,8},{16,12},{20,16},{24,20},{28,24},{32,28},... | collective-permute-start | bytes 98312 | tf_op jit(solution)/shard_map/ppermute | solution.py:770
  42.4 13.6 %all-to-all-start = ((f32[64,1,128]{2,1,0:T(1,128)}), f32[64,1,128]{2,1,0:T(1,128)}, u32[]{:S(2)}, u32[]{:S(2)}) async-start(f32[64,1,128]{2,1,0:T(1,128)} %copy-done.9), calls=%async_computation | async-start | bytes 65536 | tf_op jit(solution)/shard_map/all_to_all | solution.py:885
  49.6 6.4 %collective-permute-start.8 = (f32[48,128]{1,0:T(8,128)}, f32[48,128]{1,0:T(8,128)}, u32[]{:S(2)}, u32[]{:S(2)}) collective-permute-start(f32[48,128]{1,0:T(8,128)} %get-tuple-element.73), channel_id=1, source_target_pairs={{0,1},{1,0},{2,3},{3,2},{4,5},{5,4},{6,7},{7,6},{8,9},{9,8},{10,11... | collective-permute-start | bytes 73736 | tf_op jit(solution)/shard_map/ppermute | solution.py:774
  50.3 5.7 %collective-permute-start.9 = (f32[48,128]{1,0:T(8,128)}, f32[48,128]{1,0:T(8,128)}, u32[]{:S(2)}, u32[]{:S(2)}) collective-permute-start(f32[48,128]{1,0:T(8,128)} %get-tuple-element.74), channel_id=1, source_target_pairs={{0,3},{1,2},{2,1},{3,0},{4,7},{5,6},{6,5},{7,4},{8,11},{9,10},{10,... | collective-permute-start | bytes 73736 | tf_op jit(solution)/shard_map/ppermute | solution.py:774
  58.7 10.7 %collective-permute-start.10 = (bf16[6,32,512]{2,1,0:T(8,128)(2,1)}, bf16[6,32,512]{2,1,0:T(8,128)(2,1)S(1)}, u32[]{:S(2)}, u32[]{:S(2)}) collective-permute-start(bf16[6,32,512]{2,1,0:T(8,128)(2,1)} %get-tuple-element.84.series), channel_id=1, source_target_pairs={{0,64},{64,0},{1,65},{65,1},{2,66},{66,2},{3,67},{67,3},{4,68},{68... | collective-permute-start | bytes 589832 | tf_op jit(solution)/shard_map/ppermute | solution.py:774
  63.7 15.3 %all-to-all-start.1 = ((f32[128,1,128]{2,1,0:T(1,128)}), f32[128,1,128]{2,1,0:T(1,128)S(1)}, u32[]{:S(2)}, u32[]{:S(2)}) async-start(f32[128,1,128]{2,1,0:T(1,128)} %get-tuple-element.89), calls=%async_computation.1 | async-start | bytes 131072 | tf_op jit(solution)/shard_map/all_to_all | solution.py:929
  (1 other events, 1.0 us)

commit v9 on v8

--- a/solution.py
+++ b/solution.py
@@ -248,13 +248,15 @@
         copy(land.at[rows, :], buf.at[1])
         copy(mask.at[rows, :], ints.at[side])
         copy(guess.at[pl.ds(0, SUB - 1), pl.ds(side * (CX - 16), 16), :], short.at[side])
-    for c in copies:
+    for c in copies[1:5] + copies[6:]:
         c.wait()
     for side, buf in ((0, head), (1, tail)):
         buf[2] = ints[side].astype(F32)
         for t in range(SUB - 1):
             rows16 = short[side, t].astype(F32)
             buf[3 + t] = rows16[8:] if side else rows16[:8]
+    for c in (copies[0], copies[5]):
+        c.wait()
     for a, i, tile, spare in aux_slots():
         to_lower[tile, 6 + spare : 7 + spare, :] = head[a, i : i + 1, :]
         to_upper[tile, spare : spare + 1, :] = tail[a, 7 - i : 8 - i, :]

time: 80.3 us -> 80.3 us (level)
  no operation moved by 1% of the time
where the time goes in v9:
time: 80.3 us; the launch traced here: 79.9 us
  starting transfers between devices  35.2 us (44%)
  Pallas kernels  28.9 us (36%)
  waiting for transfers between devices  13.9 us (17%)
  local copies, waits for them, and re-layouts  0.99 us (1%)
  between operations  0.91 us (1%)
    ppermute x4, starting transfers between devices, shifted(): return lax.ppermute(value, axis, [(i, (i + by) % n) for i in range(n)])  12.1 us
    ppermute x7, starting transfers between devices, paired(): lax.ppermute(value, axis, [(i, i ^ mask) for i in range(lax.axis_size(axi...  11.8 us
    all_to_all x1, waiting for transfers between devices, per_device(): gap = lax.all_to_all(gap, ('comp', 'gx', 'gy'), 0, 0)  6.58 us
    pallas_call x2, Pallas kernels, regridded(): call(regrid, [shape(SUB, CX, CY), edges, edges], [pltpu.VMEM((BLOCKS * 8,...  5.96 us
    pallas_call x1, Pallas kernels, per_device(): call(first_rest, [shape(LEVELS, CX, CY), band(3), band(3), shape(8, LANES...  5.82 us
    all_to_all x1, starting transfers between devices, per_device(): gap = lax.all_to_all(gap, ('comp', 'gx', 'gy'), 0, 0)  5.69 us
    all_to_all x1, starting transfers between devices, per_device(): gap = lax.all_to_all(gap, ('gx', 'gy'), 0, 0)  5.64 us
    all_to_all x1, waiting for transfers between devices, per_device(): gap = lax.all_to_all(gap, ('gx', 'gy'), 0, 0)  4.5 us
  transfers between devices with their start and end apart: 13, of which 4 were waited for; matrix products, arithmetic and copies ran while one was open for 0% of the time, Pallas kernels for 20%

profile of v9, /device:TPU:1, one launch (start us, length us, event | category | flops | bytes accessed | tf_op | source)
XLA Modules:
  0.0 79.9 jit_solution(7666002865050841843)
XLA Ops:
  0.7 2.1 %shard_map.113 = (f32[16,8,512]{2,1,0:T(8,128)}, f32[16,8,512]{2,1,0:T(8,128)}) custom-call(f32[16,32,512]{2,1,0:T(8,128)} %bitcast.14, bf16[6,32,512]{2,1,0:T(8,128)(2,1)} %bitcast.21, f32[32,512]{1,0:T(8,128)} %bitcast.24, f32[32,512]{1,0:T(8,128)} %land.3, s32[32,512]{1,0:T(8,128)} %mask.6), custom_call_target="tpu_custom_call" | custom-call | tf_op jit(solution)/shard_map/pallas_call | solution.py:792
  2.8 2.1 %collective-permute-start = (f32[16,8,512]{2,1,0:T(8,128)}, f32[16,8,512]{2,1,0:T(8,128)S(1)}, u32[]{:S(2)}, u32[]{:S(2)}) collective-permute-start(f32[16,8,512]{2,1,0:T(8,128)} %get-tuple-element.58), channel_id=1, source_target_pairs={{0,4},{4,8},{8,12},{12,16},{16,20},{20,24},{24,28},{28,32},{32,36}... | collective-permute-start | bytes 786440 | tf_op jit(solution)/shard_map/ppermute | solution.py:772
  5.0 4.8 %collective-permute-start.1 = (f32[16,8,512]{2,1,0:T(8,128)}, f32[16,8,512]{2,1,0:T(8,128)S(1)}, u32[]{:S(2)}, u32[]{:S(2)}) collective-permute-start(f32[16,8,512]{2,1,0:T(8,128)} %get-tuple-element.52.after), channel_id=1, source_target_pairs={{0,60},{4,0},{8,4},{12,8},{16,12},{20,16},{24,20},{28,24},{32,28},... | collective-permute-start | bytes 786440 | tf_op jit(solution)/shard_map/ppermute | solution.py:772
  9.8 0.9 %copy-done.6 = f32[16,8,512]{2,1,0:T(8,128)S(1)} copy-done((f32[16,8,512]{2,1,0:T(8,128)S(1)}, f32[16,8,512]{2,1,0:T(8,128)}, u32[]{:S(2)}) %copy-start.6) | copy-done | bytes 262168
  10.8 2.7 %shard_map.114 = (f32[32,512]{1,0:T(8,128)S(1)}, f32[1,128]{1,0:T(1,128)S(1)}, f32[32,8,128]{2,1,0:T(8,128)S(1)}) custom-call(f32[16]{0:T(128)S(1)} %bitcast.33, f32[15]{0:T(128)S(1)} %bitcast.34, s32[4,2,32]{2,1,0:T(2,128)S(1)} %bitcast.27, s32[4,2,32]{2,1,0:T(2,128)S(1)} %bitcast.30, bf16[32,128,128]{2,1,0:T(8,128)(2,1)S(1)} %bitcast.18, ...), custom_call_target="tpu_custom_call" | custom-call | tf_op jit(solution)/shard_map/pallas_call | solution.py:814
  13.5 3.0 %collective-permute-start.4 = (f32[32,512]{1,0:T(8,128)S(1)}, f32[32,512]{1,0:T(8,128)S(1)}, u32[]{:S(2)}, u32[]{:S(2)}) collective-permute-start(f32[32,512]{1,0:T(8,128)S(1)} %get-tuple-element.63.factor), channel_id=1, source_target_pairs={{0,64},{64,0},{1,65},{65,1},{2,66},{66,2},{3,67},{67,3},{4,68},{68... | collective-permute-start | bytes 196616 | tf_op jit(solution)/shard_map/ppermute | solution.py:776
  16.9 1.3 %collective-permute-start.2 = (f32[48,256]{1,0:T(8,128)S(1)}, f32[48,256]{1,0:T(8,128)S(1)}, u32[]{:S(2)}, u32[]{:S(2)}) collective-permute-start(f32[48,256]{1,0:T(8,128)S(1)} %get-tuple-element.61), channel_id=1, source_target_pairs={{0,1},{1,0},{2,3},{3,2},{4,5},{5,4},{6,7},{7,6},{8,9},{9,8},{10,11... | collective-permute-start | bytes 147464 | tf_op jit(solution)/shard_map/ppermute | solution.py:776
  19.1 2.6 %collective-permute-done.3.three = f32[48,256]{1,0:T(8,128)S(1)} collective-permute-done((f32[48,256]{1,0:T(8,128)S(1)}, f32[48,256]{1,0:T(8,128)S(1)}, u32[]{:S(2)}, u32[]{:S(2)}) %collective-permute-start.3) | collective-permute-done | bytes 49184 | tf_op jit(solution)/shard_map/ppermute | solution.py:776
  21.7 4.0 %shard_map.116 = (bf16[6,32,512]{2,1,0:T(8,128)(2,1)S(1)}, f32[6,48,640]{2,1,0:T(8,128)S(1)}, f32[6,48,640]{2,1,0:T(8,128)S(1)}, f32[3,48,640]{2,1,0:T(8,128)S(1...) custom-call(f32[32,8,128]{2,1,0:T(8,128)S(1)} %get-tuple-element.53.coeff, f32[16,32,512]{2,1,0:T(8,128)S(1)} %bitcast.16, ...), custom_call_target="tpu_custom_call" | custom-call | tf_op jit(solution)/shard_map/pallas_call | solution.py:834
  25.7 2.4 %collective-permute-start.5 = (bf16[6,32,512]{2,1,0:T(8,128)(2,1)S(1)}, bf16[6,32,512]{2,1,0:T(8,128)(2,1)S(1)}, u32[]{:S(2)}, u32[]{:S(2)}) collective-permute-start(bf16[6,32,512]{2,1,0:T(8,128)(2,1)S(1)} %get-tuple-element.65), channel_id=1, source_target_pairs={{0,64},{64,0},{1,65},{65,1},{2,66},{66,2},{3,67},{67,3},{4,68},{68... | collective-permute-start | bytes 589832 | tf_op jit(solution)/shard_map/ppermute | solution.py:776
  28.2 5.8 %shard_map.117 = (f32[16,32,512]{2,1,0:T(8,128)}, f32[3,48,640]{2,1,0:T(8,128)S(1)}, f32[3,48,640]{2,1,0:T(8,128)S(1)}, f32[8,128]{1,0:T(8,128)S(1)}) custom-call(f32[32,8,128]{2,1,0:T(8,128)S(1)} %get-tuple-element.53.coeff, f32[16,32,512]{2,1,0:T(8,128)S(1)} %bitcast.17, f32[16,8,512]{2,1,0:T(8,128)S(1)} %collective-permute-done.upper, ...), custom_call_target="tpu_custom_call" | custom-call | tf_op jit(solution)/shard_map/pallas_call | solution.py:867
  34.2 3.0 %shard_map.119 = (f32[6,32,512]{2,1,0:T(8,128)S(1)}, f32[2,8,512]{2,1,0:T(8,128)}, f32[2,8,512]{2,1,0:T(8,128)}) custom-call(s32[4,2,32]{2,1,0:T(2,128)S(1)} %bitcast.28, s32[4,2,32]{2,1,0:T(2,128)S(1)} %bitcast.31, bf16[6,32,512]{2,1,0:T(8,128)(2,1)S(1)} %collective-permute-done.5.received, bf16[32,128,128]{2,1,0:T(8,128)(2,1)S(1)} %bitcast.19, ...), custom_call_target="tpu_custom_call" | custom-call | flops 67108864 | bytes 8388608 | tf_op jit(solution)/shard_map/pallas_call | solution.py:850
  37.3 5.1 %collective-permute-start.7 = (f32[2,8,512]{2,1,0:T(8,128)}, f32[2,8,512]{2,1,0:T(8,128)}, u32[]{:S(2)}, u32[]{:S(2)}) collective-permute-start(f32[2,8,512]{2,1,0:T(8,128)} %get-tuple-element.72), channel_id=1, source_target_pairs={{0,60},{4,0},{8,4},{12,8},{16,12},{20,16},{24,20},{28,24},{32,28},... | collective-permute-start | bytes 98312 | tf_op jit(solution)/shard_map/ppermute | solution.py:772
  42.4 5.6 %all-to-all-start = ((f32[64,1,128]{2,1,0:T(1,128)}), f32[64,1,128]{2,1,0:T(1,128)}, u32[]{:S(2)}, u32[]{:S(2)}) async-start(f32[64,1,128]{2,1,0:T(1,128)} %copy-done.9), calls=%async_computation | async-start | bytes 65536 | tf_op jit(solution)/shard_map/all_to_all | solution.py:887
  48.1 1.5 %shard_map.120 = (f32[48,128]{1,0:T(8,128)}, f32[48,128]{1,0:T(8,128)}) custom-call(f32[6,32,512]{2,1,0:T(8,128)S(1)} %get-tuple-element.70.out.regridded, f32[2,8,512]{2,1,0:T(8,128)} %collective-permute-done.6.upper_in, f32[2,8,512]{2,1,0:T(8,128)} %collective-permute-done.7.lower_in), custom_call_target="tpu_custom_call" | custom-call | tf_op jit(solution)/shard_map/pallas_call | solution.py:891
  50.3 1.2 %collective-permute-start.9 = (f32[48,128]{1,0:T(8,128)}, f32[48,128]{1,0:T(8,128)}, u32[]{:S(2)}, u32[]{:S(2)}) collective-permute-start(f32[48,128]{1,0:T(8,128)} %get-tuple-element.74), channel_id=1, source_target_pairs={{0,3},{1,2},{2,1},{3,0},{4,7},{5,6},{6,5},{7,4},{8,11},{9,10},{10,... | collective-permute-start | bytes 73736 | tf_op jit(solution)/shard_map/ppermute | solution.py:776
  51.5 4.5 %all-to-all-done.gap_in = f32[64,1,128]{2,1,0:T(1,128)} async-done(((f32[64,1,128]{2,1,0:T(1,128)}), f32[64,1,128]{2,1,0:T(1,128)}, u32[]{:S(2)}, u32[]{:S(2)}) %all-to-all-start) | async-done | bytes 32800 | tf_op jit(solution)/shard_map/all_to_all | solution.py:887
  56.0 2.7 %shard_map.121 = (bf16[6,32,512]{2,1,0:T(8,128)(2,1)}, f32[32,512]{1,0:T(8,128)S(1)}, f32[3,48,640]{2,1,0:T(8,128)S(1)}, f32[3,48,640]{2,1,0:T(8,128)S(1)}, f32[32,8,128]{2,1,0:T(8,128)S(1)}) custom-call(f32[4,48,640]{2,1,0:T(8,128)S(1)} %get-tuple-element.64.fixed_in, f32[6,32,512]{2,1,0:T(8,128)S(1)} %get-tuple-element.70.out.regridded, ...), custom_call_target="tpu_custom_call" | custom-call | tf_op jit(solution)/shard_map/pallas_call | solution.py:904
  58.7 2.5 %collective-permute-start.10 = (bf16[6,32,512]{2,1,0:T(8,128)(2,1)}, bf16[6,32,512]{2,1,0:T(8,128)(2,1)S(1)}, u32[]{:S(2)}, u32[]{:S(2)}) collective-permute-start(bf16[6,32,512]{2,1,0:T(8,128)(2,1)} %get-tuple-element.84.series), channel_id=1, source_target_pairs={{0,64},{64,0},{1,65},{65,1},{2,66},{66,2},{3,67},{67,3},{4,68},{68... | collective-permute-start | bytes 589832 | tf_op jit(solution)/shard_map/ppermute | solution.py:776
  61.2 2.5 %shard_map.122 = (f32[16,32,512]{2,1,0:T(8,128)}, f32[8,128]{1,0:T(8,128)S(1)}, f32[128,1,128]{2,1,0:T(1,128)}) custom-call(f32[32,8,128]{2,1,0:T(8,128)S(1)} %get-tuple-element.78.coeff, f32[3,48,640]{2,1,0:T(8,128)S(1)} %get-tuple-element.79.hx, f32[3,48,640]{2,1,0:T(8,128)S(1)} %get-tuple-element.80.ux, ...), custom_call_target="tpu_custom_call", output_to_operand_aliasing={{0}: (9, {})} | custom-call | tf_op jit(solution)/shard_map/pallas_call | solution.py:917
  63.7 5.7 %all-to-all-start.1 = ((f32[128,1,128]{2,1,0:T(1,128)}), f32[128,1,128]{2,1,0:T(1,128)S(1)}, u32[]{:S(2)}, u32[]{:S(2)}) async-start(f32[128,1,128]{2,1,0:T(1,128)} %get-tuple-element.89), calls=%async_computation.1 | async-start | bytes 131072 | tf_op jit(solution)/shard_map/all_to_all | solution.py:931
  69.4 3.0 %shard_map.123 = (f32[6,32,512]{2,1,0:T(8,128)S(1)}, f32[2,8,512]{2,1,0:T(8,128)}, f32[2,8,512]{2,1,0:T(8,128)}) custom-call(s32[4,2,32]{2,1,0:T(2,128)S(1)} %bitcast.29, s32[4,2,32]{2,1,0:T(2,128)S(1)} %bitcast.32, bf16[6,32,512]{2,1,0:T(8,128)(2,1)S(1)} %collective-permute-done.10.received, bf16[32,128,128]{2,1,0:T(8,128)(2,1)S(1)} %bitcast.20, ...), custom_call_target="tpu_custom_call" | custom-call | flops 67108864 | bytes 8388608 | tf_op jit(solution)/shard_map/pallas_call | solution.py:850
  72.4 6.6 %all-to-all-done.1.gap = f32[128,1,128]{2,1,0:T(1,128)S(1)} async-done(((f32[128,1,128]{2,1,0:T(1,128)}), f32[128,1,128]{2,1,0:T(1,128)S(1)}, u32[]{:S(2)}, u32[]{:S(2)}) %all-to-all-start.1) | async-done | bytes 65568 | tf_op jit(solution)/shard_map/all_to_all | solution.py:931
  79.0 0.9 %shard_map.124 = f32[6,32,512]{2,1,0:T(8,128)} custom-call(f32[6,32,512]{2,1,0:T(8,128)S(1)} %get-tuple-element.88.regridded, s32[32,512]{1,0:T(8,128)S(1)} %copy-done.3, f32[128,1,128]{2,1,0:T(1,128)S(1)} %all-to-all-done.1.gap), custom_call_target="tpu_custom_call" | custom-call | tf_op jit(solution)/shard_map/pallas_call | solution.py:933
  (38 shorter events, 2.3 us)
Async XLA Ops:
  0.6 9.1 %copy-start.1 = (bf16[1,32,128,128]{3,2,1,0:T(8,128)(2,1)S(1)}, bf16[1,32,128,128]{3,2,1,0:T(8,128)(2,1)}, u32[]{:S(2)}) copy-start(bf16[1,32,128,128]{3,2,1,0:T(8,128)(2,1)} %param.17) | copy-start | bytes 3145732
  0.6 9.1 %copy-start.3 = (s32[32,512]{1,0:T(8,128)S(1)}, s32[32,512]{1,0:T(8,128)}, u32[]{:S(2)}) copy-start(s32[32,512]{1,0:T(8,128)} %mask.6) | copy-start | bytes 196612
  0.7 9.1 %copy-start.7 = (s32[1,32,4,2]{1,3,2,0:T(2,128)S(1)}, s32[1,32,4,2]{1,3,2,0:T(2,128)}, u32[]{:S(2)}) copy-start(s32[1,32,4,2]{1,3,2,0:T(2,128)} %param.18) | copy-start | bytes 3076
  0.7 9.1 %copy-start.8 = (s32[1,32,4,2]{1,3,2,0:T(2,128)S(1)}, s32[1,32,4,2]{1,3,2,0:T(2,128)}, u32[]{:S(2)}) copy-start(s32[1,32,4,2]{1,3,2,0:T(2,128)} %param.19) | copy-start | bytes 3076
  0.7 9.1 %copy-start.10 = (f32[1,16]{1,0:T(1,128)S(1)}, f32[1,16]{1,0:T(1,128)}, u32[]{:S(2)}) copy-start(f32[1,16]{1,0:T(1,128)} %param.12) | copy-start | bytes 196
  0.7 9.1 %copy-start.11 = (f32[1,15]{1,0:T(1,128)S(1)}, f32[1,15]{1,0:T(1,128)}, u32[]{:S(2)}) copy-start(f32[1,15]{1,0:T(1,128)} %param.13) | copy-start | bytes 184
  2.8 13.7 %copy-start = (f32[1,16,32,512]{3,2,1,0:T(8,128)S(1)}, f32[1,16,32,512]{3,2,1,0:T(8,128)}, u32[]{:S(2)}) copy-start(f32[1,16,32,512]{3,2,1,0:T(8,128)} %param.10) | copy-start | bytes 3145732
  2.8 13.6 %collective-permute-start = (f32[16,8,512]{2,1,0:T(8,128)}, f32[16,8,512]{2,1,0:T(8,128)S(1)}, u32[]{:S(2)}, u32[]{:S(2)}) collective-permute-start(f32[16,8,512]{2,1,0:T(8,128)} %get-tuple-element.58), channel_id=1, source_target_pairs={{0,4},{4,8},{8,12},{12,16},{16,20},{20,24},{24,28},{28,32},{32,36}... | collective-permute-start | bytes 786440 | tf_op jit(solution)/shard_map/ppermute | solution.py:772
  5.0 11.5 %collective-permute-start.1 = (f32[16,8,512]{2,1,0:T(8,128)}, f32[16,8,512]{2,1,0:T(8,128)S(1)}, u32[]{:S(2)}, u32[]{:S(2)}) collective-permute-start(f32[16,8,512]{2,1,0:T(8,128)} %get-tuple-element.52.after), channel_id=1, source_target_pairs={{0,60},{4,0},{8,4},{12,8},{16,12},{20,16},{24,20},{28,24},{32,28},... | collective-permute-start | bytes 786440 | tf_op jit(solution)/shard_map/ppermute | solution.py:772
  10.8 5.7 %copy-start.2 = (bf16[1,6,32,512]{3,2,1,0:T(8,128)(2,1)S(1)}, bf16[1,6,32,512]{3,2,1,0:T(8,128)(2,1)}, u32[]{:S(2)}) copy-start(bf16[1,6,32,512]{3,2,1,0:T(8,128)(2,1)} %param.11) | copy-start | bytes 589828
  10.8 5.7 %copy-start.4 = (f32[1,32,512]{2,1,0:T(8,128)S(1)}, f32[1,32,512]{2,1,0:T(8,128)}, u32[]{:S(2)}) copy-start(f32[1,32,512]{2,1,0:T(8,128)} %param.14) | copy-start | bytes 196612
  10.8 5.7 %copy-start.5 = (f32[32,512]{1,0:T(8,128)S(1)}, f32[32,512]{1,0:T(8,128)}, u32[]{:S(2)}) copy-start(f32[32,512]{1,0:T(8,128)} %land.3) | copy-start | bytes 196612
  13.5 5.4 %collective-permute-start.4 = (f32[32,512]{1,0:T(8,128)S(1)}, f32[32,512]{1,0:T(8,128)S(1)}, u32[]{:S(2)}, u32[]{:S(2)}) collective-permute-start(f32[32,512]{1,0:T(8,128)S(1)} %get-tuple-element.63.factor), channel_id=1, source_target_pairs={{0,64},{64,0},{1,65},{65,1},{2,66},{66,2},{3,67},{67,3},{4,68},{68... | collective-permute-start | bytes 196616 | tf_op jit(solution)/shard_map/ppermute | solution.py:776
  16.9 2.2 %collective-permute-start.2 = (f32[48,256]{1,0:T(8,128)S(1)}, f32[48,256]{1,0:T(8,128)S(1)}, u32[]{:S(2)}, u32[]{:S(2)}) collective-permute-start(f32[48,256]{1,0:T(8,128)S(1)} %get-tuple-element.61), channel_id=1, source_target_pairs={{0,1},{1,0},{2,3},{3,2},{4,5},{5,4},{6,7},{7,6},{8,9},{9,8},{10,11... | collective-permute-start | bytes 147464 | tf_op jit(solution)/shard_map/ppermute | solution.py:776
  18.2 3.5 %collective-permute-start.3 = (f32[48,256]{1,0:T(8,128)S(1)}, f32[48,256]{1,0:T(8,128)S(1)}, u32[]{:S(2)}, u32[]{:S(2)}) collective-permute-start(f32[48,256]{1,0:T(8,128)S(1)} %get-tuple-element.62), channel_id=1, source_target_pairs={{0,3},{1,2},{2,1},{3,0},{4,7},{5,6},{6,5},{7,4},{8,11},{9,10},{10,... | collective-permute-start | bytes 147464 | tf_op jit(solution)/shard_map/ppermute | solution.py:776
  25.7 8.3 %collective-permute-start.5 = (bf16[6,32,512]{2,1,0:T(8,128)(2,1)S(1)}, bf16[6,32,512]{2,1,0:T(8,128)(2,1)S(1)}, u32[]{:S(2)}, u32[]{:S(2)}) collective-permute-start(bf16[6,32,512]{2,1,0:T(8,128)(2,1)S(1)} %get-tuple-element.65), channel_id=1, source_target_pairs={{0,64},{64,0},{1,65},{65,1},{2,66},{66,2},{3,67},{67,3},{4,68},{68... | collective-permute-start | bytes 589832 | tf_op jit(solution)/shard_map/ppermute | solution.py:776
  34.2 3.0 %copy-start.9 = (f32[64,1,128]{2,1,0:T(1,128)}, f32[64,1,128]{2,1,0:T(1,128)S(1)}, u32[]{:S(2)}) copy-start(f32[64,1,128]{2,1,0:T(1,128)S(1)} %get-tuple-element.75) | copy-start | bytes 98308
  37.2 10.8 %collective-permute-start.6 = (f32[2,8,512]{2,1,0:T(8,128)}, f32[2,8,512]{2,1,0:T(8,128)}, u32[]{:S(2)}, u32[]{:S(2)}) collective-permute-start(f32[2,8,512]{2,1,0:T(8,128)} %get-tuple-element.71), channel_id=1, source_target_pairs={{0,4},{4,8},{8,12},{12,16},{16,20},{20,24},{24,28},{28,32},{32,36}... | collective-permute-start | bytes 98312 | tf_op jit(solution)/shard_map/ppermute | solution.py:772
  37.3 10.8 %collective-permute-start.7 = (f32[2,8,512]{2,1,0:T(8,128)}, f32[2,8,512]{2,1,0:T(8,128)}, u32[]{:S(2)}, u32[]{:S(2)}) collective-permute-start(f32[2,8,512]{2,1,0:T(8,128)} %get-tuple-element.72), channel_id=1, source_target_pairs={{0,60},{4,0},{8,4},{12,8},{16,12},{20,16},{24,20},{28,24},{32,28},... | collective-permute-start | bytes 98312 | tf_op jit(solution)/shard_map/ppermute | solution.py:772
  42.4 13.6 %all-to-all-start = ((f32[64,1,128]{2,1,0:T(1,128)}), f32[64,1,128]{2,1,0:T(1,128)}, u32[]{:S(2)}, u32[]{:S(2)}) async-start(f32[64,1,128]{2,1,0:T(1,128)} %copy-done.9), calls=%async_computation | async-start | bytes 65536 | tf_op jit(solution)/shard_map/all_to_all | solution.py:887
  49.6 6.4 %collective-permute-start.8 = (f32[48,128]{1,0:T(8,128)}, f32[48,128]{1,0:T(8,128)}, u32[]{:S(2)}, u32[]{:S(2)}) collective-permute-start(f32[48,128]{1,0:T(8,128)} %get-tuple-element.73), channel_id=1, source_target_pairs={{0,1},{1,0},{2,3},{3,2},{4,5},{5,4},{6,7},{7,6},{8,9},{9,8},{10,11... | collective-permute-start | bytes 73736 | tf_op jit(solution)/shard_map/ppermute | solution.py:776
  50.3 5.7 %collective-permute-start.9 = (f32[48,128]{1,0:T(8,128)}, f32[48,128]{1,0:T(8,128)}, u32[]{:S(2)}, u32[]{:S(2)}) collective-permute-start(f32[48,128]{1,0:T(8,128)} %get-tuple-element.74), channel_id=1, source_target_pairs={{0,3},{1,2},{2,1},{3,0},{4,7},{5,6},{6,5},{7,4},{8,11},{9,10},{10,... | collective-permute-start | bytes 73736 | tf_op jit(solution)/shard_map/ppermute | solution.py:776
  58.7 10.7 %collective-permute-start.10 = (bf16[6,32,512]{2,1,0:T(8,128)(2,1)}, bf16[6,32,512]{2,1,0:T(8,128)(2,1)S(1)}, u32[]{:S(2)}, u32[]{:S(2)}) collective-permute-start(bf16[6,32,512]{2,1,0:T(8,128)(2,1)} %get-tuple-element.84.series), channel_id=1, source_target_pairs={{0,64},{64,0},{1,65},{65,1},{2,66},{66,2},{3,67},{67,3},{4,68},{68... | collective-permute-start | bytes 589832 | tf_op jit(solution)/shard_map/ppermute | solution.py:776
  63.7 15.3 %all-to-all-start.1 = ((f32[128,1,128]{2,1,0:T(1,128)}), f32[128,1,128]{2,1,0:T(1,128)S(1)}, u32[]{:S(2)}, u32[]{:S(2)}) async-start(f32[128,1,128]{2,1,0:T(1,128)} %get-tuple-element.89), calls=%async_computation.1 | async-start | bytes 131072 | tf_op jit(solution)/shard_map/all_to_all | solution.py:931
  (1 other events, 1.0 us)
